TPU v7x, 128 devices: a whole 4x4x4 slice. The times are simulated.
128 devices in a mesh: dp: 4 (over z), tensor: 32 (over x, y, core).
Axes of the slice: x: 4, y: 4, z: 4, core: 2. Of those that a mesh axis runs over, the one named last changes fastest.
Arguments:
- x_rows: bfloat16 [16384, 4096], P(('dp', 'tensor')), may hold values from -6 to 6
- grad_out: bfloat16 [16384, 16384], P('dp', 'tensor'), may hold values from -0.0625 to 0.0625
- error_buffer: float32 [4, 4096, 16384], P('dp', None, 'tensor'), may hold values from -12 to 12, as said below
- q_init: float32 [16384, 32], P('tensor'), may hold values from -6 to 6
Outputs:
- new_error: float32 [4, 4096, 16384], P('dp', None, 'tensor')
- p_basis: float32 [4096, 32], replicated
- q_factor: float32 [16384, 32], P('tensor')
Inputs may be any that keep to these rules, and one draw needn't show every extreme that they name: `error_buffer`: finite float32 values.
All inputs are finite; a program needn't handle non-finite values.
Results may differ from a plain program's by a relative error of at most 0.0003.
Values may be sent and summed in bfloat16 or wider, within the bound.
No kernel may reach another device: no remote copies, remote signals or barrier semaphores. Data moves between devices by JAX's collectives and lax.ppermute only.
A program may use at most 128 MiB of HBM per device.

v0:
```python
import jax
import jax.numpy as jnp
from jax import lax
from jax.sharding import PartitionSpec as P


def body(x_rows, grad_out, error_buffer, q_init):
    replicas = lax.axis_size("dp")
    highest = lax.Precision.HIGHEST
    merged = error_buffer[0] + lax.dot_general(
        lax.all_gather(x_rows, "tensor", axis=0, tiled=True),
        grad_out,
        (((0,), (0,)), ((), ())),
        preferred_element_type=jnp.float32,
    )
    p_whole = lax.psum(jnp.dot(merged, q_init, precision=highest), ("dp", "tensor")) / replicas
    gram_matrix = jnp.dot(p_whole.T, p_whole, precision=highest)
    lower_factor = jnp.linalg.cholesky(gram_matrix)
    p_basis = lax.linalg.triangular_solve(
        lower_factor, p_whole, left_side=False, lower=True, transpose_a=True
    )
    q_factor = lax.psum(jnp.dot(merged.T, p_basis, precision=highest), "dp") / replicas
    new_error = merged - jnp.dot(p_basis, q_factor.T, precision=highest)
    return (new_error[None], p_basis, q_factor)


def solution(mesh):
    in_specs = (
        P(("dp", "tensor"), None),
        P("dp", "tensor"),
        P("dp", None, "tensor"),
        P("tensor", None),
    )
    out_specs = (P("dp", None, "tensor"), P(), P("tensor", None))
    return jax.shard_map(body, mesh=mesh, in_specs=in_specs, out_specs=out_specs, check_vma=False)
```

profile of v0, /device:TPU:0, one launch (start us, length us, event | category | flops | bytes accessed | tf_op | source)
XLA Modules:
  0.0 387.0 jit_solution(1963678670981568014)
XLA Ops:
  7.2 0.0 copy-start
  7.2 0.0 all-gather.2.cloned.1.call-start
  7.2 0.7 all-gather.2.cloned.1.call-update
  7.9 0.0 all-reduce.3.cloned.1.call-start
  8.0 118.5 %all-gather.2.cloned.1.call-done = bf16[4096,4096]{1,0:T(8,128)(2,1)} async-done(((bf16[128,4096]{1,0:T(8,128)(2,1)}), bf16[4096,4096]{1,0:T(8,128)(2,1)}) %all-gather.2.cloned.1.call-update) | async-done | bytes 33554448 | tf_op jit(solution)/shard_map/all_gather | solution.py:11
  126.5 28.0 %bitcast_add_fusion = f32[4096,512]{1,0:T(8,128)} fusion(f32[1,4096,512]{2,1,0:T(8,128)} %param.6, bf16[4096,4096]{1,0:T(8,128)(2,1)} %all-gather.2.cloned.1.call-done, bf16[4096,512]{1,0:T(8,128)(2,1)} %param.5), kind=kOutput, calls=%fused_computation | convolution fusion | flops 17181966336 | bytes 54525952 | tf_op jit(solution)/shard_map/dot_general | solution.py:10
  154.5 10.8 %fusion.11 = f32[4096,32]{0,1:T(8,128)} fusion(f32[4096,512]{1,0:T(8,128)} %bitcast_add_fusion, f32[512,32]{0,1:T(8,128)S(1)} %copy-done), kind=kOutput, calls=%fused_computation.20 | convolution fusion | flops 805306368 | bytes 8978432 | tf_op jit(solution)/shard_map/dot_general | solution.py:16
  165.3 0.0 all-reduce.3.cloned.1.call-update
  165.3 0.2 all-reduce.5.cloned.1.call-start
  165.5 143.9 %all-reduce.3.cloned.1.call-done = f32[4096,32]{0,1:T(8,128)} async-done(((f32[4096,32]{0,1:T(8,128)}), f32[4096,32]{0,1:T(8,128)}) %all-reduce.3.cloned.1.call-update) | async-done | bytes 524304 | tf_op jit(solution)/shard_map/psum | solution.py:16
  309.4 1.8 fusion.2
  311.2 0.1 copy.7
  311.3 2.9 cholesky.16
  314.2 0.6 compare_reduce_fusion
  314.9 0.7 fusion.6
  315.5 2.4 custom-call.6
  318.0 1.7 fusion
  319.7 0.0 copy-start.1
  319.7 8.2 %fusion.12 = f32[512,32]{0,1:T(8,128)} fusion(f32[4096,512]{1,0:T(8,128)} %bitcast_add_fusion, f32[4096,32]{0,1:T(8,128)S(1)} %fusion), kind=kOutput, calls=%fused_computation.21 | convolution fusion | flops 805306368 | bytes 8978432 | tf_op jit(solution)/shard_map/dot_general | solution.py:22
  327.9 0.0 all-reduce.5.cloned.1.call-update
  327.9 40.5 %all-reduce.5.cloned.1.call-done = f32[512,32]{0,1:T(8,128)} async-done(((f32[512,32]{0,1:T(8,128)}), f32[512,32]{0,1:T(8,128)}) %all-reduce.5.cloned.1.call-update) | async-done | bytes 65552 | tf_op jit(solution)/shard_map/psum | solution.py:22
  368.4 0.8 broadcast_multiply_fusion
  369.2 11.3 %subtract_bitcast_fusion = f32[1,4096,512]{2,1,0:T(8,128)} fusion(f32[4096,512]{1,0:T(8,128)} %bitcast_add_fusion, f32[4096,32]{0,1:T(8,128)S(1)} %fusion, f32[512,32]{0,1:T(8,128)S(1)} %broadcast_multiply_fusion), kind=kOutput, calls=%fused_computation.1 | convolution fusion | flops 807403520 | bytes 17367040 | tf_op jit(solution)/shard_map/dot_general | solution.py:23
  380.5 0.0 copy-done.2
  (5 shorter events, 0.0 us)
Async XLA Ops:
  7.2 147.3 %copy-start = (f32[512,32]{0,1:T(8,128)S(1)}, f32[512,32]{0,1:T(8,128)}, u32[]{:S(2)}) copy-start(f32[512,32]{0,1:T(8,128)} %param.7) | copy-start | bytes 196612
  7.2 119.3 %all-gather.2.cloned.1.call-start = ((), (), s32[]{:S(2)}) async-start(), calls=%async_computation | async-start | bytes 34603008 | tf_op jit(solution)/shard_map/all_gather | solution.py:11
  7.9 301.5 %all-reduce.3.cloned.1.call-start = ((), (), s32[]{:S(2)}) async-start(), calls=%async_computation.1 | async-start | bytes 1048576 | tf_op jit(solution)/shard_map/psum | solution.py:16
  165.3 203.1 %all-reduce.5.cloned.1.call-start = ((), (), s32[]{:S(2)}) async-start(), calls=%async_computation.2 | async-start | bytes 131072 | tf_op jit(solution)/shard_map/psum | solution.py:22
  319.7 60.8 %copy-start.1 = (f32[4096,32]{0,1:T(8,128)}, f32[4096,32]{0,1:T(8,128)S(1)}, u32[]{:S(2)}) copy-start(f32[4096,32]{0,1:T(8,128)S(1)} %fusion) | copy-start | bytes 1572868
  369.2 11.3 %copy-start.2 = (f32[512,32]{0,1:T(8,128)}, f32[512,32]{0,1:T(8,128)S(1)}, u32[]{:S(2)}) copy-start(f32[512,32]{0,1:T(8,128)S(1)} %broadcast_multiply_fusion) | copy-start | bytes 196612
Sparse Core Ops, SparseCore 0:
  10.3 116.1 all-gather.1
  165.4 143.9 all-reduce.2
  328.0 40.3 all-reduce.4
where the time goes:
time: 387 us
  waiting for transfers between devices  304 us (79%)
  matrix products  61.7 us (16%)
  between operations  13.8 us (4%)
  other arithmetic  7.53 us (2%)
    psum x1, waiting for transfers between devices, body(): lax.psum(jnp.dot(merged, q_init, precision=highest), ('dp', 'tensor'))  144 us
    all_gather x1, waiting for transfers between devices, body(): lax.all_gather(x_rows, 'tensor', axis=0, tiled=True)  118 us
    psum x1, waiting for transfers between devices, body(): lax.psum(jnp.dot(merged.T, p_basis, precision=highest), 'dp') / replicas  40.5 us
    dot_general x1, matrix products, body(): lax.dot_general(lax.all_gather(x_rows, 'tensor', axis=0, tiled=True), gra...  28 us
    dot_general x1, matrix products, body(): new_error = merged - jnp.dot(p_basis, q_factor.T, precision=highest)  11.3 us
    dot_general x1, matrix products, body(): jnp.dot(merged, q_init, precision=highest)  10.8 us
    dot_general x1, matrix products, body(): jnp.dot(merged.T, p_basis, precision=highest)  8.19 us
  transfers between devices with their start and end apart: 3, of which 3 were waited for; matrix products, arithmetic and copies ran while one was open for 0% of the time, Pallas kernels for 0%

commit v1 on v0

v1 whole, which is shorter than its diff:
```python
import functools

import jax
import jax.numpy as jnp
import numpy as np
from jax import lax
from jax.experimental import pallas as pl
from jax.experimental.pallas import tpu as pltpu
from jax.sharding import PartitionSpec as P

F32, BF16 = jnp.float32, jnp.bfloat16
N, R, D, F, T = 4, 32, 4096, 512, 128
OFFSETS = (0, -1, 1, 2)
VMEM_LIMIT = 56 * 1024 * 1024
WHOLE = pl.BlockSpec(memory_space=pltpu.VMEM)
SMEM = pl.BlockSpec(memory_space=pltpu.SMEM)
NT = (((1,), (1,)), ((), ()))
TN = (((0,), (0,)), ((), ()))


def flat(x, y, c):
    return ((x % N) * N + y % N) * 2 + c


def along(x, y, c, first, d):
    return flat(x + d, y, c) if (c == 0) == first else flat(x, y + d, c)


PLANE = [(x, y, c) for x in range(N) for y in range(N) for c in range(2)]


def hop(array, first, d):
    pairs = [(flat(*p), along(*p, first, d)) for p in PLANE]
    return lax.ppermute(array, "tensor", pairs)


def swap(array):
    return lax.ppermute(array, "tensor", [(i, i ^ 1) for i in range(2 * N * N)])


def hop_z(array, d):
    return lax.ppermute(array, "dp", [(i, (i + d) % N) for i in range(N)])


def block_table():
    table = np.zeros((2 * N * N, 2, N, N), np.int32)
    for x, y, c in PLANE:
        for k in range(2):
            colour = c ^ k
            for i, second in enumerate(OFFSETS):
                for j, first in enumerate(OFFSETS):
                    dx, dy = (first, second) if colour == 0 else (second, first)
                    table[flat(x, y, c), k, i, j] = flat(x + dx, y + dy, colour) * T
    return table.reshape(2 * N * N, 2 * N * N)


def split(value, parts):
    pieces = []
    for _ in range(parts):
        piece = value.astype(BF16)
        pieces.append(piece)
        value = value - piece.astype(F32)
    return pieces


def dot(a, b, dims=(((1,), (0,)), ((), ()))):
    return lax.dot_general(a, b, dims, preferred_element_type=F32)


def dot_left(value, exact, dims):
    rows = value.shape[0]
    out = dot(jnp.concatenate(split(value, 3), 0), exact, dims)
    return out[:rows] + (out[rows : 2 * rows] + out[2 * rows :])


def dot_both(value, other, dims):
    rows = value.shape[0]
    a = jnp.concatenate(split(value, 3), 0)
    b1, b2, b3 = split(other, 3)
    p1, p2, p3 = dot(a, b1, dims), dot(a[: 2 * rows], b2, dims), dot(a[:rows], b3, dims)
    low = p1[2 * rows :] + p2[rows:] + p3
    return p1[:rows] + ((p1[rows : 2 * rows] + p2[:rows]) + low)


def params(**kw):
    return pltpu.CompilerParams(vmem_limit_bytes=VMEM_LIMIT, **kw)


def cost(flops, nbytes):
    return pl.CostEstimate(flops=int(flops), bytes_accessed=int(nbytes), transcendentals=0)


def shape(dims, dtype=F32):
    return jax.ShapeDtypeStruct(dims, dtype)


def tokens_kernel(off_ref, q_ref, g_ref, own_ref, other_ref):
    q = jnp.concatenate(split(q_ref[...], 3), 0)
    for k, out in enumerate((own_ref, other_ref)):
        for i in range(N):
            rows = []
            for j in range(N):
                at = pl.multiple_of(off_ref[(k * N + i) * N + j], T)
                rows.append(g_ref[pl.ds(at, T), :])
            r = dot(q, jnp.concatenate(rows, 0), NT)
            out[i] = r[:R] + (r[R : 2 * R] + r[2 * R :])


def tokens(off, q, g):
    return pl.pallas_call(
        tokens_kernel,
        out_shape=[shape((N, R, N * T))] * 2,
        in_specs=[SMEM, WHOLE, WHOLE],
        out_specs=[WHOLE] * 2,
        compiler_params=params(),
        cost_estimate=cost(2 * 256 * F * D, 5 << 20),
    )(off, q, g)


def errors_kernel(q_ref, e_ref, out_ref):
    q = jnp.concatenate(split(q_ref[...], 3), 0)
    e1, e2 = split(e_ref[...], 2)
    r, s = dot(q, e1, NT), dot(q[: 2 * R], e2, NT)
    out_ref[0] = r[:R] + ((r[R : 2 * R] + s[:R]) + (r[2 * R :] + s[R:]))


def errors(q, e):
    return pl.pallas_call(
        errors_kernel,
        grid=(2 * N,),
        out_shape=shape((2 * N, R, D // 8)),
        in_specs=[pl.BlockSpec((R, F), lambda i: (0, 0)), pl.BlockSpec((D // 8, F), lambda i: (i, 0))],
        out_specs=pl.BlockSpec((1, R, D // 8), lambda i: (i, 0, 0)),
        compiler_params=params(),
        cost_estimate=cost(4 * 256 * F * D, 9 << 20),
    )(q, e)


def turn_kernel(a_ref, b_ref, out_ref):
    out_ref[:, :T] = a_ref[...].T
    out_ref[:, T:] = b_ref[...].T


def turn(a, b):
    return pl.pallas_call(
        turn_kernel,
        grid=(4,),
        out_shape=shape((D, 2 * T), BF16),
        in_specs=[pl.BlockSpec((T, D // 4), lambda i: (0, i))] * 2,
        out_specs=pl.BlockSpec((D // 4, 2 * T), lambda i: (i, 0)),
        compiler_params=params(),
        cost_estimate=cost(1e9, 4 << 20),
    )(a, b)


def turn3_kernel(a_ref, b_ref, c_ref, out_ref):
    out_ref[:, :T] = a_ref[...].T
    out_ref[:, T:] = jnp.concatenate([b_ref[...], c_ref[...]], 0).T


def turn3(a, b, c):
    half = pl.BlockSpec((T // 2, D // 4), lambda i: (0, i))
    return pl.pallas_call(
        turn3_kernel,
        grid=(4,),
        out_shape=shape((D, 2 * T), BF16),
        in_specs=[pl.BlockSpec((T, D // 4), lambda i: (0, i)), half, half],
        out_specs=pl.BlockSpec((D // 4, 2 * T), lambda i: (i, 0)),
        compiler_params=params(),
        cost_estimate=cost(1e9, 4 << 20),
    )(a, b, c)


def sketch_kernel(pos_ref, h0, h1, h2, h3, e_ref, g0_ref, g1_ref, own_ref, other_ref):
    c, z = pos_ref[0], pos_ref[1]
    h = (h0[...] + h3[...]) + (h1[...] + h2[...])
    n = D // 8
    for k, out in enumerate((own_ref, other_ref)):
        for i in range(N):
            chunk = (c ^ k) * N + (z + i) % N
            rows = pl.ds(pl.multiple_of(chunk * n, n), n)
            x = jnp.concatenate([g0_ref[rows, :], g1_ref[rows, :]], 1)
            out[i] = dot_left(h, x, NT) + e_ref[chunk]


def sketch_part(pos, h, e, g0, g1):
    return pl.pallas_call(
        sketch_kernel,
        out_shape=[shape((N, R, D // 8))] * 2,
        in_specs=[SMEM] + [WHOLE] * 7,
        out_specs=[WHOLE] * 2,
        compiler_params=params(),
        cost_estimate=cost(2 * 256 * F * D, 6 << 20),
    )(pos, *h, e, g0, g1)


def add_kernel(a_ref, b_ref, *outs):
    for i, out in enumerate(outs):
        out[...] = a_ref[i] + b_ref[i]


def add_parts(a, b):
    return pl.pallas_call(
        add_kernel,
        out_shape=[shape(a.shape[1:])] * N,
        in_specs=[WHOLE] * 2,
        out_specs=[WHOLE] * N,
        compiler_params=params(),
        cost_estimate=cost(1e6, 3 * a.size * 4),
    )(a, b)


def basis_kernel(pos_ref, mine_ref, other_ref, out_ref, s_ref):
    c, z = pos_ref[0], pos_ref[1]
    n = D // 8
    for half, ref in ((1 - c, mine_ref), (c, other_ref)):
        for i, d in enumerate(OFFSETS):
            chunk = half * N + (z + d + N) % N
            s_ref[:, pl.ds(pl.multiple_of(chunk * n, n), n)] = ref[i] * 0.25
    s = s_ref[...]
    gram = dot_both(s, s, NT)
    row = lax.broadcasted_iota(jnp.int32, (R, 2 * R), 0)
    col = lax.broadcasted_iota(jnp.int32, (R, 2 * R), 1)
    work = jnp.concatenate([gram, jnp.zeros((R, R), F32)], 1) + jnp.where(col == row + R, 1.0, 0.0)
    done = jnp.zeros((R, 2 * R), F32)
    for j in range(R):
        inv = 1.0 / jnp.sqrt(work[j : j + 1, j : j + 1])
        line = work[j : j + 1, :] * inv
        done = jnp.where(row == j, line, done)
        work = work - jnp.where(row > j, work[:, j : j + 1] * inv, 0.0) * line
    out_ref[...] = dot_both(done[:, R:], s, (((1,), (0,)), ((), ())))


def basis(pos, mine, other):
    return pl.pallas_call(
        basis_kernel,
        out_shape=shape((R, D)),
        in_specs=[SMEM, WHOLE, WHOLE],
        out_specs=WHOLE,
        scratch_shapes=[pltpu.VMEM((R, D), F32)],
        compiler_params=params(),
        cost_estimate=cost(8e9, 1 << 20),
    )(pos, mine, other)


def merge_kernel(n, last, off_ref, *refs):
    acc_ref, refs = refs[0], refs[1:]
    xs, gs, refs = refs[:n], refs[n : 3 * n], refs[3 * n :]
    total = acc_ref[...]
    for i in range(n):
        total += dot(xs[i][...], jnp.concatenate([gs[2 * i][...], gs[2 * i + 1][...]], 0))
    if not last:
        refs[0][...] = total
        return
    p_ref, out_ref, q_ref = refs
    out_ref[...] = total

    @pl.when(pl.program_id(0) == 0)
    def _():
        q_ref[...] = jnp.zeros_like(q_ref)

    p = jnp.concatenate(split(p_ref[...], 3), 0)
    t1, t2 = split(total, 2)
    a, b = dot(p, t1), dot(p[: 2 * R], t2)
    q_ref[...] += a[:R] + ((a[R : 2 * R] + b[:R]) + (a[2 * R :] + b[R:]))


def merge(off, acc, groups, g, p=None, rows=512):
    n, last = len(groups), p is not None
    tile = lambda i, off: (i, 0)
    starts = tuple(s for s, _ in groups)
    at = lambda k: pl.BlockSpec((T, F), lambda i, off: (off[k] // T, 0))
    in_specs = [pl.BlockSpec((rows, F), tile)]
    in_specs += [pl.BlockSpec((rows, 2 * T), tile)] * n
    for s in starts:
        in_specs += [at(s), at(s + 1)]
    out_shape, out_specs = [shape((D, F))], [pl.BlockSpec((rows, F), tile)]
    args = [acc] + [x for _, x in groups] + [g] * (2 * n)
    if last:
        in_specs.append(pl.BlockSpec((R, rows), lambda i, off: (0, i)))
        out_shape.append(shape((R, F)))
        out_specs.append(pl.BlockSpec((R, F), lambda i, off: (0, 0)))
        args.append(p)
    return pl.pallas_call(
        functools.partial(merge_kernel, n, last),
        grid_spec=pltpu.PrefetchScalarGridSpec(
            num_scalar_prefetch=1, grid=(D // rows,), in_specs=in_specs, out_specs=out_specs
        ),
        out_shape=out_shape,
        compiler_params=params(),
        cost_estimate=cost(2 * 256 * n * D * F, (16 << 20) + n * (2 << 20)),
    )(off, *args)


def final_kernel(m_ref, p_ref, q0, q1, q2, q3, out_ref, q_ref):
    q = ((q0[...] + q3[...]) + (q1[...] + q2[...])) * 0.25
    q_ref[...] = q
    p1, p2 = split(p_ref[...], 2)
    s1, s2 = split(q, 2)
    out_ref[...] = m_ref[...] - dot(jnp.concatenate([p1, p1, p2], 0), jnp.concatenate([s1, s2, s1], 0), TN)


def final(merged, p, q, rows=512):
    whole = pl.BlockSpec((R, F), lambda i: (0, 0))
    return pl.pallas_call(
        final_kernel,
        grid=(D // rows,),
        in_specs=[pl.BlockSpec((rows, F), lambda i: (i, 0)), pl.BlockSpec((R, rows), lambda i: (0, i))] + [whole] * N,
        out_shape=[shape((D, F)), shape((R, F))],
        out_specs=[pl.BlockSpec((rows, F), lambda i: (i, 0)), whole],
        compiler_params=params(),
        cost_estimate=cost(2 * 128 * D * F, 16 << 20),
    )(merged, p, *q)


def ring_sum(value, send):
    left, right, far = send(value, 1), send(value, -1), send(value, 2)
    return (value + far) + (left + right)


def body(x, g, e, q_init):
    me = lax.axis_index("tensor")
    pos = jnp.stack([me % 2, lax.axis_index("dp")]).astype(jnp.int32)
    off = lax.dynamic_index_in_dim(jnp.asarray(block_table()), me, 0, keepdims=False)
    e, q = e[0], q_init.T

    a, b = hop(x, True, 1), hop(x, True, -1)

    own, other = tokens(off, q, g)
    got = swap(other)
    h_mine, h_far, h_right, h_opp = add_parts(own, got)
    h = [h_mine, hop(h_right, False, 1), hop(h_far, False, -1), hop(h_opp, False, 2)]
    e_part = errors(q, e)

    c, d = hop(a[: T // 2], True, 1), hop(b[T // 2 :], True, -1)
    g0 = turn(x, a)
    l0, r0 = hop(g0, False, 1), hop(g0, False, -1)
    g1 = turn3(b, c, d)
    l1, r1 = hop(g1, False, 1), hop(g1, False, -1)
    o0, o1 = hop(l0, False, 1), hop(r1, False, -1)

    s_own, s_other = sketch_part(pos, h, e_part, g0, g1)
    parts = add_parts(s_own, swap(s_other))
    s = (parts[0] + hop_z(parts[2], 2)) + (hop_z(parts[1], 1) + hop_z(parts[3], -1))
    s = ring_sum(s, functools.partial(hop, first=True) if False else (lambda v, k: hop(v, True, k)))
    s = swap(s)
    s = ring_sum(s, lambda v, k: hop(v, True, k))
    stack = jnp.stack([s, hop_z(s, 1), hop_z(s, -1), hop_z(s, 2)])
    p = basis(pos, stack, swap(stack))

    acc = e
    (acc,) = merge(off, acc, [(0, g0), (2, g1), (16, swap(g0)), (18, swap(g1))], g)
    (acc,) = merge(
        off,
        acc,
        [(4, l0), (6, l1), (8, r0), (10, r1), (20, swap(l0)), (22, swap(l1)), (24, swap(r0)), (26, swap(r1))],
        g,
    )
    acc, qp = merge(off, acc, [(12, o0), (14, o1), (28, swap(o0)), (30, swap(o1))], g, p)
    qs = [qp, hop_z(qp, 1), hop_z(qp, -1), hop_z(qp, 2)]
    err, qf = final(acc, p, qs)
    return err[None], p.T, qf.T


def solution(mesh):
    in_specs = (
        P(("dp", "tensor"), None),
        P("dp", "tensor"),
        P("dp", None, "tensor"),
        P("tensor", None),
    )
    out_specs = (P("dp", None, "tensor"), P(), P("tensor", None))
    return jax.shard_map(body, mesh=mesh, in_specs=in_specs, out_specs=out_specs, check_vma=False)
```

time: 387 us -> 242 us (0.63)
  waiting for transfers between devices: 304 us -> 90.8 us
  Pallas kernels: 0 us -> 91.3 us
  matrix products: 61.7 us -> 0 us
  starting transfers between devices: 0.3 us -> 50.6 us
  between operations: 13.8 us -> 0.87 us
  other arithmetic: 7.53 us -> 1.57 us
  local copies, waits for them, and re-layouts: 0.09 us -> 5.31 us
    psum x2 -> x0, waiting for transfers between devices: 184 us -> none  [the longest x1 144 us: body(): lax.psum(jnp.dot(merged, q_init, precision=highest), ('dp', 'tensor'))]
    all_gather x1 -> x0, waiting for transfers between devices: 118 us -> none  [body(): lax.all_gather(x_rows, 'tensor', axis=0, tiled=True)]
    pallas_call x0 -> x12, Pallas kernels: none -> 91.3 us  [the longest x3 45.2 us: merge(): pl.pallas_call(functools.partial(merge_kernel, n, last), grid_spec=pltpu....]
    ppermute x0 -> x40, waiting for transfers between devices: none -> 90.8 us  [the longest x19 67.5 us: hop(): return lax.ppermute(array, 'tensor', pairs)]
    dot_general x5 -> x0, matrix products: 60 us -> none  [the longest x1 28 us: body(): lax.dot_general(lax.all_gather(x_rows, 'tensor', axis=0, tiled=True), gra...]
    ppermute x0 -> x40, starting transfers between devices: none -> 50.6 us  [the longest x19 32.9 us: hop(): return lax.ppermute(array, 'tensor', pairs)]
    another operation x5 -> x2, other arithmetic: 6.68 us -> 0.66 us  [the longest x1 0.65 us: body(): pos = jnp.stack([me % 2, lax.axis_index('dp')]).astype(jnp.int32)]
    unnamed x6 -> x38, local copies, waits for them, and re-layouts: 0.02 us -> 4.03 us
  transfers between devices with their start and end apart: 3 -> 40, of which waited for: 3 -> 17; matrix products, arithmetic and copies ran while one was open for 0% -> 1% of each run, Pallas kernels for 0% -> 28%
where the time goes in v1:
time: 242 us; the launch traced here: 241 us
  Pallas kernels  91.3 us (38%)
  waiting for transfers between devices  90.8 us (38%)
  starting transfers between devices  50.6 us (21%)
  local copies, waits for them, and re-layouts  5.31 us (2%)
    ppermute x19, waiting for transfers between devices, hop(): return lax.ppermute(array, 'tensor', pairs)  67.5 us
    pallas_call x3, Pallas kernels, merge(): pl.pallas_call(functools.partial(merge_kernel, n, last), grid_spec=pltpu....  45.2 us
    ppermute x19, starting transfers between devices, hop(): return lax.ppermute(array, 'tensor', pairs)  32.9 us
    ppermute x9, waiting for transfers between devices, hop_z(): return lax.ppermute(array, 'dp', [(i, (i + d) % N) for i in range(N)])  18.8 us
    ppermute x9, starting transfers between devices, hop_z(): return lax.ppermute(array, 'dp', [(i, (i + d) % N) for i in range(N)])  16.4 us
    pallas_call x1, Pallas kernels, final(): pl.pallas_call(final_kernel, grid=(D // rows,), in_specs=[pl.BlockSpec((r...  9.9 us
    pallas_call x1, Pallas kernels, errors(): pl.pallas_call(errors_kernel, grid=(2 * N,), out_shape=shape((2 * N, R, D...  8.24 us
    pallas_call x1, Pallas kernels, basis(): pl.pallas_call(basis_kernel, out_shape=shape((R, D)), in_specs=[SMEM, WHO...  7.24 us
  transfers between devices with their start and end apart: 40, of which 17 were waited for; matrix products, arithmetic and copies ran while one was open for 1% of the time, Pallas kernels for 28%

profile of v1, /device:TPU:0, one launch (start us, length us, event | category | flops | bytes accessed | tf_op | source)
XLA Modules:
  0.0 240.5 jit_solution(12341061958383896865)
XLA Ops:
  3.9 13.0 %collective-permute-done.b_ref = bf16[128,4096]{1,0:T(8,128)(2,1)S(1)} collective-permute-done((bf16[128,4096]{1,0:T(8,128)(2,1)}, bf16[128,4096]{1,0:T(8,128)(2,1)S(1)}, u32[]{:S(2)}, u32[]{:S(2)}) %collective-permute-start) | collective-permute-done | bytes 1048608 | tf_op jit(solution)/shard_map/ppermute | solution.py:34
  17.4 2.9 %collective-permute-start.3 = (bf16[64,4096]{1,0:T(8,128)(2,1)S(1)}, bf16[64,4096]{1,0:T(8,128)(2,1)}, u32[]{:S(2)}, u32[]{:S(2)}) collective-permute-start(bf16[64,4096]{1,0:T(8,128)(2,1)S(1)} %slice.9), channel_id=1, source_target_pairs={{0,24},{1,7},{2,26},{3,1},{4,28},{5,3},{6,30},{7,5},{8,0},{9,15},{... | collective-permute-start | bytes 1572872 | tf_op jit(solution)/shard_map/ppermute | solution.py:34
  21.6 4.4 %shard_map.80 = (f32[4,32,512]{2,1,0:T(8,128)}, f32[4,32,512]{2,1,0:T(8,128)}) custom-call(s32[32]{0:T(128)} %dynamic-slice_bitcast_fusion.off_ref, f32[32,512]{1,0:T(8,128)} %bitcast.16, bf16[4096,512]{1,0:T(8,128)(2,1)} %refs_12_.5), custom_call_target="tpu_custom_call" | custom-call | flops 1073741824 | bytes 5242880 | tf_op jit(solution)/shard_map/pallas_call | solution.py:110
  26.6 8.2 %shard_map.82.e_ref = f32[8,32,512]{2,1,0:T(8,128)} custom-call(f32[32,512]{1,0:T(8,128)} %bitcast.17, f32[4096,512]{1,0:T(8,128)} %bitcast.13), custom_call_target="tpu_custom_call" | custom-call | flops 2147483648 | bytes 9437184 | tf_op jit(solution)/shard_map/pallas_call | solution.py:128
  42.6 4.1 %shard_map.76.refs_1_.g0_ref = bf16[4096,256]{1,0:T(8,128)(2,1)} custom-call(bf16[128,4096]{1,0:T(8,128)(2,1)} %a_ref.1, bf16[128,4096]{1,0:T(8,128)(2,1)} %copy-done.3), custom_call_target="tpu_custom_call" | custom-call | flops 1000000000 | bytes 4194304 | tf_op jit(solution)/shard_map/pallas_call | solution.py:145
  47.5 4.1 %shard_map.77.refs_2_.g1_ref = bf16[4096,256]{1,0:T(8,128)(2,1)} custom-call(bf16[128,4096]{1,0:T(8,128)(2,1)} %copy-done.2, bf16[64,4096]{1,0:T(8,128)(2,1)} %collective-permute-done.2.b_ref, bf16[64,4096]{1,0:T(8,128)(2,1)} %collective-permute-done.3.c_ref), custom_call_target="tpu_custom_call" | custom-call | flops 1000000000 | bytes 4194304 | tf_op jit(solution)/shard_map/pallas_call | solution.py:163
  52.3 4.7 %shard_map.83 = (f32[4,32,512]{2,1,0:T(8,128)}, f32[4,32,512]{2,1,0:T(8,128)}) custom-call(s32[2]{0:T(128)} %pad_add_fusion.pos_ref, f32[32,512]{1,0:T(8,128)} %get-tuple-element.21.h0, f32[32,512]{1,0:T(8,128)} %copy-done.12, f32[32,512]{1,0:T(8,128)} %copy-done.13, f32[32,512]{1,0:T(8,128)} %copy-done.14, f32[8,32,512]{2,1,0:T(8,128)} %shard_map.82.e_ref, ...), custom_call_target="tpu_custom_call" | custom-call | flops 1073741824 | bytes 6291456 | tf_op jit(solution)/shard_map/pallas_call | solution.py:187
  61.2 3.9 %collective-permute-start.23 = (f32[32,512]{1,0:T(8,128)}, f32[32,512]{1,0:T(8,128)S(1)}, u32[]{:S(2)}, u32[]{:S(2)}) collective-permute-start(f32[32,512]{1,0:T(8,128)} %get-tuple-element.28), channel_id=1, source_target_pairs={{0,64},{32,96},{64,0},{96,32},{1,65},{33,97},{65,1},{97,33},{2,66}... | collective-permute-start | bytes 196616 | tf_op jit(solution)/shard_map/ppermute | solution.py:42
  84.3 3.7 %collective-permute-done.30 = f32[32,512]{1,0:T(8,128)S(1)} collective-permute-done((f32[32,512]{1,0:T(8,128)S(1)}, f32[32,512]{1,0:T(8,128)S(1)}, u32[]{:S(2)}, u32[]{:S(2)}) %collective-permute-start.30) | collective-permute-done | bytes 65568 | tf_op jit(solution)/shard_map/ppermute | solution.py:34
  89.0 4.5 %collective-permute-done.31 = f32[32,512]{1,0:T(8,128)S(1)} collective-permute-done((f32[32,512]{1,0:T(8,128)S(1)}, f32[32,512]{1,0:T(8,128)S(1)}, u32[]{:S(2)}, u32[]{:S(2)}) %collective-permute-start.31) | collective-permute-done | bytes 65568 | tf_op jit(solution)/shard_map/ppermute | solution.py:34
  95.3 3.2 %collective-permute-done.32 = f32[32,512]{1,0:T(8,128)S(1)} collective-permute-done((f32[32,512]{1,0:T(8,128)S(1)}, f32[32,512]{1,0:T(8,128)S(1)}, u32[]{:S(2)}, u32[]{:S(2)}) %collective-permute-start.32) | collective-permute-done | bytes 65568 | tf_op jit(solution)/shard_map/ppermute | solution.py:34
  98.7 5.4 %collective-permute-done.33 = f32[32,512]{1,0:T(8,128)S(1)} collective-permute-done((f32[32,512]{1,0:T(8,128)S(1)}, f32[32,512]{1,0:T(8,128)S(1)}, u32[]{:S(2)}, u32[]{:S(2)}) %collective-permute-start.33) | collective-permute-done | bytes 65568 | tf_op jit(solution)/shard_map/ppermute | solution.py:42
  110.5 3.9 %collective-permute-done.35 = f32[32,512]{1,0:T(8,128)S(1)} collective-permute-done((f32[32,512]{1,0:T(8,128)S(1)}, f32[32,512]{1,0:T(8,128)S(1)}, u32[]{:S(2)}, u32[]{:S(2)}) %collective-permute-start.35) | collective-permute-done | bytes 65568 | tf_op jit(solution)/shard_map/ppermute | solution.py:42
  119.0 8.5 %collective-permute-done.9.refs_4_ = bf16[4096,256]{1,0:T(8,128)(2,1)} collective-permute-done((bf16[4096,256]{1,0:T(8,128)(2,1)S(1)}, bf16[4096,256]{1,0:T(8,128)(2,1)}, u32[]{:S(2)}, u32[]{:S(2)}) %collective-permute-start.9) | collective-permute-done | bytes 2097184 | tf_op jit(solution)/shard_map/ppermute | solution.py:34
  127.5 3.8 %collective-permute-start.15 = (bf16[4096,256]{1,0:T(8,128)(2,1)}, bf16[4096,256]{1,0:T(8,128)(2,1)}, u32[]{:S(2)}, u32[]{:S(2)}) collective-permute-start(bf16[4096,256]{1,0:T(8,128)(2,1)} %collective-permute-done.9.refs_4_), channel_id=1, source_target_pairs={{0,6},{1,25},{2,0},{3,27},{4,2},{5,29},{6,4},{7,31},{8,14},{9,1},{... | collective-permute-start | bytes 6291464 | tf_op jit(solution)/shard_map/ppermute | solution.py:34
  131.3 12.3 %collective-permute-done.7.refs_2_ = bf16[4096,256]{1,0:T(8,128)(2,1)} collective-permute-done((bf16[4096,256]{1,0:T(8,128)(2,1)S(1)}, bf16[4096,256]{1,0:T(8,128)(2,1)}, u32[]{:S(2)}, u32[]{:S(2)}) %collective-permute-start.7) | collective-permute-done | bytes 2097184 | tf_op jit(solution)/shard_map/ppermute | solution.py:34
  144.0 21.8 %collective-permute-done.14.refs_1_ = bf16[4096,256]{1,0:T(8,128)(2,1)S(1)} collective-permute-done((bf16[4096,256]{1,0:T(8,128)(2,1)S(1)}, bf16[4096,256]{1,0:T(8,128)(2,1)S(1)}, u32[]{:S(2)}, u32[]{:S(2)}) %collective-permute-start.14) | collective-permute-done | bytes 2097184 | tf_op jit(solution)/shard_map/ppermute | solution.py:34
  166.4 7.2 %shard_map.85.refs_13_.p_ref = f32[32,4096]{1,0:T(8,128)} custom-call(s32[2]{0:T(128)} %pad_add_fusion.pos_ref, f32[4,32,512]{2,1,0:T(8,128)} %copy-done.9, f32[4,32,512]{2,1,0:T(8,128)} %copy-done.18), custom_call_target="tpu_custom_call" | custom-call | flops 8000000000 | bytes 1048576 | tf_op jit(solution)/shard_map/pallas_call | solution.py:235
  173.6 14.0 %shard_map.78.refs_0_ = f32[4096,512]{1,0:T(8,128)} custom-call(s32[32]{0:T(128)} %dynamic-slice_bitcast_fusion.off_ref, f32[4096,512]{1,0:T(8,128)} %bitcast.14, bf16[4096,256]{1,0:T(8,128)(2,1)} %shard_map.76.refs_1_.g0_ref, bf16[4096,256]{1,0:T(8,128)(2,1)} %shard_map.77.refs_2_.g1_ref, bf16[4096,256]{1,0:T(8,128)(2,1)} %collective-permute-done.4.refs_3_, ...), custom_call_target="tpu_custom_call" | custom-call | flops 4294967296 | bytes 25165824 | tf_op jit(solution)/shard_map/pallas_call | solution.py:284
  187.7 17.7 %shard_map.79.refs_0_ = f32[4096,512]{1,0:T(8,128)} custom-call(s32[32]{0:T(128)} %dynamic-slice_bitcast_fusion.off_ref, f32[4096,512]{1,0:T(8,128)} %shard_map.78.refs_0_, bf16[4096,256]{1,0:T(8,128)(2,1)} %copy-done.4, bf16[4096,256]{1,0:T(8,128)(2,1)} %collective-permute-done.7.refs_2_, bf16[4096,256]{1,0:T(8,128)(2,1)} %collective-permute-done.8.refs_3_, ...), custom_call_target="tpu_custom_call" | custom-call | flops 8589934592 | bytes 33554432 | tf_op jit(solution)/shard_map/pallas_call | solution.py:284
  206.7 13.5 %shard_map.86 = (f32[4096,512]{1,0:T(8,128)}, f32[32,512]{1,0:T(8,128)}) custom-call(s32[32]{0:T(128)} %dynamic-slice_bitcast_fusion.off_ref, f32[4096,512]{1,0:T(8,128)} %shard_map.79.refs_0_, bf16[4096,256]{1,0:T(8,128)(2,1)} %copy-done.5, bf16[4096,256]{1,0:T(8,128)(2,1)} %collective-permute-done.15.refs_2_, bf16[4096,256]{1,0:T(8,128)(2,1)} %copy-done.8, ...), custom_call_target="tpu_custom_call" | custom-call | flops 4294967296 | bytes 25165824 | tf_op jit(solution)/shard_map/pallas_call | solution.py:284
  221.3 2.8 %collective-permute-start.38 = (f32[32,512]{1,0:T(8,128)}, f32[32,512]{1,0:T(8,128)S(1)}, u32[]{:S(2)}, u32[]{:S(2)}) collective-permute-start(f32[32,512]{1,0:T(8,128)} %get-tuple-element.32.q0), channel_id=1, source_target_pairs={{0,96},{32,0},{64,32},{96,64},{1,97},{33,1},{65,33},{97,65},{2,98}... | collective-permute-start | bytes 196616 | tf_op jit(solution)/shard_map/ppermute | solution.py:42
  226.4 3.6 %collective-permute-done.39.q3 = f32[32,512]{1,0:T(8,128)S(1)} collective-permute-done((f32[32,512]{1,0:T(8,128)}, f32[32,512]{1,0:T(8,128)S(1)}, u32[]{:S(2)}, u32[]{:S(2)}) %collective-permute-start.39) | collective-permute-done | bytes 65568 | tf_op jit(solution)/shard_map/ppermute | solution.py:42
  230.6 9.9 %shard_map.87 = (f32[4096,512]{1,0:T(8,128)}, f32[32,512]{1,0:T(8,128)}) custom-call(f32[4096,512]{1,0:T(8,128)} %get-tuple-element.31.m_ref, f32[32,4096]{1,0:T(8,128)} %shard_map.85.refs_13_.p_ref, f32[32,512]{1,0:T(8,128)} %get-tuple-element.32.q0, f32[32,512]{1,0:T(8,128)} %copy-done.15, f32[32,512]{1,0:T(8,128)} %copy-done.16, f32[32,512]{1,0:T(8,128)} %copy-done.17), custom_call_target="tpu_custom_call" | custom-call | flops 536870912 | bytes 16777216 | tf_op jit(solution)/shard_map/pallas_call | solution.py:305
  (114 shorter events, 58.7 us)
Async XLA Ops:
  0.6 16.3 %collective-permute-start = (bf16[128,4096]{1,0:T(8,128)(2,1)}, bf16[128,4096]{1,0:T(8,128)(2,1)S(1)}, u32[]{:S(2)}, u32[]{:S(2)}) collective-permute-start(bf16[128,4096]{1,0:T(8,128)(2,1)} %a_ref.1), channel_id=1, source_target_pairs={{0,8},{1,3},{2,10},{3,5},{4,12},{5,7},{6,14},{7,1},{8,16},{9,11},{... | collective-permute-start | bytes 3145736 | tf_op jit(solution)/shard_map/ppermute | solution.py:34
  2.3 15.1 %collective-permute-start.1 = (bf16[128,4096]{1,0:T(8,128)(2,1)}, bf16[128,4096]{1,0:T(8,128)(2,1)S(1)}, u32[]{:S(2)}, u32[]{:S(2)}) collective-permute-start(bf16[128,4096]{1,0:T(8,128)(2,1)} %a_ref.1), channel_id=1, source_target_pairs={{0,24},{1,7},{2,26},{3,1},{4,28},{5,3},{6,30},{7,5},{8,0},{9,15},{... | collective-permute-start | bytes 3145736 | tf_op jit(solution)/shard_map/ppermute | solution.py:34
  17.0 29.8 %collective-permute-start.2 = (bf16[64,4096]{1,0:T(8,128)(2,1)S(1)}, bf16[64,4096]{1,0:T(8,128)(2,1)}, u32[]{:S(2)}, u32[]{:S(2)}) collective-permute-start(bf16[64,4096]{1,0:T(8,128)(2,1)S(1)} %slice.8), channel_id=1, source_target_pairs={{0,8},{1,3},{2,10},{3,5},{4,12},{5,7},{6,14},{7,1},{8,16},{9,11},{... | collective-permute-start | bytes 1572872 | tf_op jit(solution)/shard_map/ppermute | solution.py:34
  17.4 29.3 %collective-permute-start.3 = (bf16[64,4096]{1,0:T(8,128)(2,1)S(1)}, bf16[64,4096]{1,0:T(8,128)(2,1)}, u32[]{:S(2)}, u32[]{:S(2)}) collective-permute-start(bf16[64,4096]{1,0:T(8,128)(2,1)S(1)} %slice.9), channel_id=1, source_target_pairs={{0,24},{1,7},{2,26},{3,1},{4,28},{5,3},{6,30},{7,5},{8,0},{9,15},{... | collective-permute-start | bytes 1572872 | tf_op jit(solution)/shard_map/ppermute | solution.py:34
  26.0 8.9 %collective-permute-start.18 = (f32[4,32,512]{2,1,0:T(8,128)}, f32[4,32,512]{2,1,0:T(8,128)S(1)}, u32[]{:S(2)}, u32[]{:S(2)}) collective-permute-start(f32[4,32,512]{2,1,0:T(8,128)} %get-tuple-element.20), channel_id=1, source_target_pairs={{0,1},{1,0},{2,3},{3,2},{4,5},{5,4},{6,7},{7,6},{8,9},{9,8},{10,11... | collective-permute-start | bytes 786440 | tf_op jit(solution)/shard_map/ppermute | solution.py:38
  37.3 14.3 %collective-permute-start.19 = (f32[32,512]{1,0:T(8,128)}, f32[32,512]{1,0:T(8,128)S(1)}, u32[]{:S(2)}, u32[]{:S(2)}) collective-permute-start(f32[32,512]{1,0:T(8,128)} %get-tuple-element.22), channel_id=1, source_target_pairs={{0,2},{1,9},{2,4},{3,11},{4,6},{5,13},{6,0},{7,15},{8,10},{9,17},{... | collective-permute-start | bytes 196616 | tf_op jit(solution)/shard_map/ppermute | solution.py:34
  39.0 12.6 %collective-permute-start.20 = (f32[32,512]{1,0:T(8,128)}, f32[32,512]{1,0:T(8,128)S(1)}, u32[]{:S(2)}, u32[]{:S(2)}) collective-permute-start(f32[32,512]{1,0:T(8,128)} %get-tuple-element.23), channel_id=1, source_target_pairs={{0,6},{1,25},{2,0},{3,27},{4,2},{5,29},{6,4},{7,31},{8,14},{9,1},{... | collective-permute-start | bytes 196616 | tf_op jit(solution)/shard_map/ppermute | solution.py:34
  40.5 11.1 %collective-permute-start.21 = (f32[32,512]{1,0:T(8,128)}, f32[32,512]{1,0:T(8,128)S(1)}, u32[]{:S(2)}, u32[]{:S(2)}) collective-permute-start(f32[32,512]{1,0:T(8,128)} %get-tuple-element.24), channel_id=1, source_target_pairs={{0,4},{1,17},{2,6},{3,19},{4,0},{5,21},{6,2},{7,23},{8,12},{9,25},... | collective-permute-start | bytes 196616 | tf_op jit(solution)/shard_map/ppermute | solution.py:34
  46.7 69.4 %collective-permute-start.4 = (bf16[4096,256]{1,0:T(8,128)(2,1)}, bf16[4096,256]{1,0:T(8,128)(2,1)}, u32[]{:S(2)}, u32[]{:S(2)}) collective-permute-start(bf16[4096,256]{1,0:T(8,128)(2,1)} %shard_map.76.refs_1_.g0_ref), channel_id=1, source_target_pairs={{0,1},{1,0},{2,3},{3,2},{4,5},{5,4},{6,7},{7,6},{8,9},{9,8},{10,11... | collective-permute-start | bytes 6291464 | tf_op jit(solution)/shard_map/ppermute | solution.py:38
  46.7 70.9 %collective-permute-start.6 = (bf16[4096,256]{1,0:T(8,128)(2,1)}, bf16[4096,256]{1,0:T(8,128)(2,1)S(1)}, u32[]{:S(2)}, u32[]{:S(2)}) collective-permute-start(bf16[4096,256]{1,0:T(8,128)(2,1)} %shard_map.76.refs_1_.g0_ref), channel_id=1, source_target_pairs={{0,2},{1,9},{2,4},{3,11},{4,6},{5,13},{6,0},{7,15},{8,10},{9,17},{... | collective-permute-start | bytes 6291464 | tf_op jit(solution)/shard_map/ppermute | solution.py:34
  61.2 7.1 %collective-permute-start.23 = (f32[32,512]{1,0:T(8,128)}, f32[32,512]{1,0:T(8,128)S(1)}, u32[]{:S(2)}, u32[]{:S(2)}) collective-permute-start(f32[32,512]{1,0:T(8,128)} %get-tuple-element.28), channel_id=1, source_target_pairs={{0,64},{32,96},{64,0},{96,32},{1,65},{33,97},{65,1},{97,33},{2,66}... | collective-permute-start | bytes 196616 | tf_op jit(solution)/shard_map/ppermute | solution.py:42
  73.7 6.3 %collective-permute-start.27 = (f32[32,512]{1,0:T(8,128)S(1)}, f32[32,512]{1,0:T(8,128)S(1)}, u32[]{:S(2)}, u32[]{:S(2)}) collective-permute-start(f32[32,512]{1,0:T(8,128)S(1)} %add_add_fusion.2), channel_id=1, source_target_pairs={{0,8},{1,3},{2,10},{3,5},{4,12},{5,7},{6,14},{7,1},{8,16},{9,11},{... | collective-permute-start | bytes 196616 | tf_op jit(solution)/shard_map/ppermute | solution.py:34
  77.5 40.2 %collective-permute-start.8 = (bf16[4096,256]{1,0:T(8,128)(2,1)S(1)}, bf16[4096,256]{1,0:T(8,128)(2,1)}, u32[]{:S(2)}, u32[]{:S(2)}) collective-permute-start(bf16[4096,256]{1,0:T(8,128)(2,1)S(1)} %copy-done), channel_id=1, source_target_pairs={{0,6},{1,25},{2,0},{3,27},{4,2},{5,29},{6,4},{7,31},{8,14},{9,1},{... | collective-permute-start | bytes 6291464 | tf_op jit(solution)/shard_map/ppermute | solution.py:34
  80.0 47.5 %collective-permute-start.9 = (bf16[4096,256]{1,0:T(8,128)(2,1)S(1)}, bf16[4096,256]{1,0:T(8,128)(2,1)}, u32[]{:S(2)}, u32[]{:S(2)}) collective-permute-start(bf16[4096,256]{1,0:T(8,128)(2,1)S(1)} %copy-done.1), channel_id=1, source_target_pairs={{0,6},{1,25},{2,0},{3,27},{4,2},{5,29},{6,4},{7,31},{8,14},{9,1},{... | collective-permute-start | bytes 6291464 | tf_op jit(solution)/shard_map/ppermute | solution.py:34
  116.0 15.2 %collective-permute-start.5 = (bf16[4096,256]{1,0:T(8,128)(2,1)S(1)}, bf16[4096,256]{1,0:T(8,128)(2,1)S(1)}, u32[]{:S(2)}, u32[]{:S(2)}) collective-permute-start(bf16[4096,256]{1,0:T(8,128)(2,1)S(1)} %copy-done.1), channel_id=1, source_target_pairs={{0,1},{1,0},{2,3},{3,2},{4,5},{5,4},{6,7},{7,6},{8,9},{9,8},{10,11... | collective-permute-start | bytes 6291464 | tf_op jit(solution)/shard_map/ppermute | solution.py:38
  116.2 27.4 %collective-permute-start.7 = (bf16[4096,256]{1,0:T(8,128)(2,1)S(1)}, bf16[4096,256]{1,0:T(8,128)(2,1)}, u32[]{:S(2)}, u32[]{:S(2)}) collective-permute-start(bf16[4096,256]{1,0:T(8,128)(2,1)S(1)} %copy-done.1), channel_id=1, source_target_pairs={{0,2},{1,9},{2,4},{3,11},{4,6},{5,13},{6,0},{7,15},{8,10},{9,17},{... | collective-permute-start | bytes 6291464 | tf_op jit(solution)/shard_map/ppermute | solution.py:34
  117.6 25.9 %collective-permute-start.10 = (bf16[4096,256]{1,0:T(8,128)(2,1)S(1)}, bf16[4096,256]{1,0:T(8,128)(2,1)S(1)}, u32[]{:S(2)}, u32[]{:S(2)}) collective-permute-start(bf16[4096,256]{1,0:T(8,128)(2,1)S(1)} %collective-permute-done.6.refs_1_), channel_id=1, source_target_pairs={{0,1},{1,0},{2,3},{3,2},{4,5},{5,4},{6,7},{7,6},{8,9},{9,8},{10,11... | collective-permute-start | bytes 6291464 | tf_op jit(solution)/shard_map/ppermute | solution.py:38
  117.6 48.2 %collective-permute-start.14 = (bf16[4096,256]{1,0:T(8,128)(2,1)S(1)}, bf16[4096,256]{1,0:T(8,128)(2,1)S(1)}, u32[]{:S(2)}, u32[]{:S(2)}) collective-permute-start(bf16[4096,256]{1,0:T(8,128)(2,1)S(1)} %collective-permute-done.6.refs_1_), channel_id=1, source_target_pairs={{0,2},{1,9},{2,4},{3,11},{4,6},{5,13},{6,0},{7,15},{8,10},{9,17},{... | collective-permute-start | bytes 6291464 | tf_op jit(solution)/shard_map/ppermute | solution.py:34
  127.5 38.4 %collective-permute-start.15 = (bf16[4096,256]{1,0:T(8,128)(2,1)}, bf16[4096,256]{1,0:T(8,128)(2,1)}, u32[]{:S(2)}, u32[]{:S(2)}) collective-permute-start(bf16[4096,256]{1,0:T(8,128)(2,1)} %collective-permute-done.9.refs_4_), channel_id=1, source_target_pairs={{0,6},{1,25},{2,0},{3,27},{4,2},{5,29},{6,4},{7,31},{8,14},{9,1},{... | collective-permute-start | bytes 6291464 | tf_op jit(solution)/shard_map/ppermute | solution.py:34
  131.3 56.4 %collective-permute-start.12 = (bf16[4096,256]{1,0:T(8,128)(2,1)}, bf16[4096,256]{1,0:T(8,128)(2,1)}, u32[]{:S(2)}, u32[]{:S(2)}) collective-permute-start(bf16[4096,256]{1,0:T(8,128)(2,1)} %collective-permute-done.8.refs_3_), channel_id=1, source_target_pairs={{0,1},{1,0},{2,3},{3,2},{4,5},{5,4},{6,7},{7,6},{8,9},{9,8},{10,11... | collective-permute-start | bytes 6291464 | tf_op jit(solution)/shard_map/ppermute | solution.py:38
  143.5 44.1 %collective-permute-start.13 = (bf16[4096,256]{1,0:T(8,128)(2,1)}, bf16[4096,256]{1,0:T(8,128)(2,1)}, u32[]{:S(2)}, u32[]{:S(2)}) collective-permute-start(bf16[4096,256]{1,0:T(8,128)(2,1)} %collective-permute-done.9.refs_4_), channel_id=1, source_target_pairs={{0,1},{1,0},{2,3},{3,2},{4,5},{5,4},{6,7},{7,6},{8,9},{9,8},{10,11... | collective-permute-start | bytes 6291464 | tf_op jit(solution)/shard_map/ppermute | solution.py:38
  143.5 44.1 %collective-permute-start.11 = (bf16[4096,256]{1,0:T(8,128)(2,1)}, bf16[4096,256]{1,0:T(8,128)(2,1)}, u32[]{:S(2)}, u32[]{:S(2)}) collective-permute-start(bf16[4096,256]{1,0:T(8,128)(2,1)} %collective-permute-done.7.refs_2_), channel_id=1, source_target_pairs={{0,1},{1,0},{2,3},{3,2},{4,5},{5,4},{6,7},{7,6},{8,9},{9,8},{10,11... | collective-permute-start | bytes 6291464 | tf_op jit(solution)/shard_map/ppermute | solution.py:38
  165.9 39.5 %collective-permute-start.16 = (bf16[4096,256]{1,0:T(8,128)(2,1)S(1)}, bf16[4096,256]{1,0:T(8,128)(2,1)S(1)}, u32[]{:S(2)}, u32[]{:S(2)}) collective-permute-start(bf16[4096,256]{1,0:T(8,128)(2,1)S(1)} %collective-permute-done.14.refs_1_), channel_id=1, source_target_pairs={{0,1},{1,0},{2,3},{3,2},{4,5},{5,4},{6,7},{7,6},{8,9},{9,8},{10,11... | collective-permute-start | bytes 6291464 | tf_op jit(solution)/shard_map/ppermute | solution.py:38
  165.9 39.5 %collective-permute-start.17 = (bf16[4096,256]{1,0:T(8,128)(2,1)}, bf16[4096,256]{1,0:T(8,128)(2,1)}, u32[]{:S(2)}, u32[]{:S(2)}) collective-permute-start(bf16[4096,256]{1,0:T(8,128)(2,1)} %collective-permute-done.15.refs_2_), channel_id=1, source_target_pairs={{0,1},{1,0},{2,3},{3,2},{4,5},{5,4},{6,7},{7,6},{8,9},{9,8},{10,11... | collective-permute-start | bytes 6291464 | tf_op jit(solution)/shard_map/ppermute | solution.py:38
  (35 other events, 382.6 us)

commit v2 on v0

v2 whole, which is shorter than its diff:
```python
import functools

import jax
import jax.numpy as jnp
import numpy as np
from jax import lax
from jax.experimental import pallas as pl
from jax.experimental.pallas import tpu as pltpu
from jax.sharding import PartitionSpec as P

F32, BF16 = jnp.float32, jnp.bfloat16
N, R, D, F, T = 4, 32, 4096, 512, 128
OFFSETS = (0, -1, 1, 2)
MIB = 1024 * 1024
WHOLE = pl.BlockSpec(memory_space=pltpu.VMEM)
SMEM = pl.BlockSpec(memory_space=pltpu.SMEM)
NT = (((1,), (1,)), ((), ()))
TN = (((0,), (0,)), ((), ()))


def flat(x, y, c):
    return ((x % N) * N + y % N) * 2 + c


def along(x, y, c, first, d):
    return flat(x + d, y, c) if (c == 0) == first else flat(x, y + d, c)


PLANE = [(x, y, c) for x in range(N) for y in range(N) for c in range(2)]


def hop(array, first, d):
    pairs = [(flat(*p), along(*p, first, d)) for p in PLANE]
    return lax.ppermute(array, "tensor", pairs)


def swap(array):
    return lax.ppermute(array, "tensor", [(i, i ^ 1) for i in range(2 * N * N)])


def hop_z(array, bit):
    return lax.ppermute(array, "dp", [(i, i ^ bit) for i in range(N)])


def around_z(array, d):
    return lax.ppermute(array, "dp", [(i, (i + d) % N) for i in range(N)])


def twin(array, first, bit):
    pairs = []
    for x, y, c in PLANE:
        to = (x ^ bit, y, c) if (c == 0) == first else (x, y ^ bit, c)
        pairs.append((flat(x, y, c), flat(*to)))
    return lax.ppermute(array, "tensor", pairs)


def block_tables():
    table = np.zeros((2, 2 * N * N, 2, N, N), np.int32)
    for x, y, c in PLANE:
        for k in range(2):
            colour = c ^ k
            at = y if colour == 0 else x
            for i in range(N):
                for j, first in enumerate(OFFSETS):
                    for kind, second in enumerate((OFFSETS[i], (at ^ i) - at)):
                        dx, dy = (first, second) if colour == 0 else (second, first)
                        table[kind, flat(x, y, c), k, i, j] = flat(x + dx, y + dy, colour) * T
    return np.concatenate(table.reshape(2, 2 * N * N, 2 * N * N), 1)


def split(value, parts):
    pieces = []
    for _ in range(parts):
        piece = value.astype(BF16)
        pieces.append(piece)
        value = value - piece.astype(F32)
    return pieces


def dot(a, b, dims=(((1,), (0,)), ((), ()))):
    return lax.dot_general(a, b, dims, preferred_element_type=F32)


def dot_left(value, exact, dims):
    rows = value.shape[0]
    out = dot(jnp.concatenate(split(value, 3), 0), exact, dims)
    return out[:rows] + (out[rows : 2 * rows] + out[2 * rows :])


def dot_both(value, other, dims):
    rows = value.shape[0]
    a = jnp.concatenate(split(value, 3), 0)
    b1, b2, b3 = split(other, 3)
    p1, p2, p3 = dot(a, b1, dims), dot(a[: 2 * rows], b2, dims), dot(a[:rows], b3, dims)
    low = p1[2 * rows :] + p2[rows:] + p3
    return p1[:rows] + ((p1[rows : 2 * rows] + p2[:rows]) + low)


def cost(flops, nbytes):
    return pl.CostEstimate(flops=int(flops), bytes_accessed=int(nbytes), transcendentals=0)


def shape(dims, dtype=F32):
    return jax.ShapeDtypeStruct(dims, dtype)


def run(kernel, out_shape, args, in_specs, out_specs, after=(), **kw):
    n, m = len(args), len(after)
    grid = kw.pop("grid", None)
    prefetch = kw.pop("prefetch", 0)
    options = pltpu.CompilerParams(vmem_limit_bytes=kw.pop("vmem", 16) * MIB)
    any_spec = pl.BlockSpec(memory_space=pl.ANY)
    in_specs = list(in_specs) + [any_spec] * m

    def wrapped(*refs):
        kernel(*refs[:n], *refs[n + m :])

    if prefetch:
        kw["grid_spec"] = pltpu.PrefetchScalarGridSpec(
            num_scalar_prefetch=prefetch, grid=grid, in_specs=in_specs, out_specs=out_specs
        )
    else:
        kw.update(in_specs=in_specs, out_specs=out_specs)
        if grid is not None:
            kw["grid"] = grid
    return pl.pallas_call(wrapped, out_shape=out_shape, compiler_params=options, **kw)(*args, *after)


def add3(r):
    return r[:R] + (r[R : 2 * R] + r[2 * R :])


def tokens_kernel(off_ref, q_ref, g_ref, keep_ref, send_ref, other_ref):
    q = jnp.concatenate(split(q_ref[...], 3), 0)
    outs = [keep_ref.at[0], keep_ref.at[1], send_ref.at[0], send_ref.at[1]] + [other_ref.at[i] for i in range(N)]
    for k, out in enumerate(outs):
        rows = []
        for j in range(N):
            at = pl.multiple_of(off_ref[2 * N * N + k * N + j], T)
            rows.append(g_ref[pl.ds(at, T), :])
        out[...] = add3(dot(q, jnp.concatenate(rows, 0), NT))


def tokens(off, q, g):
    return run(
        tokens_kernel,
        [shape((2, R, N * T)), shape((2, R, N * T)), shape((N, R, N * T))],
        (off, q, g),
        [SMEM, WHOLE, WHOLE],
        [WHOLE] * 3,
        cost_estimate=cost(2 * 256 * F * D, 5 << 20),
    )


def errors_kernel(q_ref, e_ref, out_ref):
    q = jnp.concatenate(split(q_ref[...], 3), 0)
    n = D // 8
    for k in range(2):
        e1, e2 = split(e_ref[k * n : (k + 1) * n, :], 2)
        r, s = dot(q, e1, NT), dot(q[: 2 * R], e2, NT)
        out_ref[k] = r[:R] + ((r[R : 2 * R] + s[:R]) + (r[2 * R :] + s[R:]))


def errors(q, e, part, after):
    return run(
        errors_kernel,
        shape((N, R, D // 8)),
        (q, e),
        [pl.BlockSpec((R, F), lambda i: (0, 0)), pl.BlockSpec((D // 4, F), lambda i: (i + 2 * part, 0))],
        pl.BlockSpec((2, R, D // 8), lambda i: (i, 0, 0)),
        after,
        grid=(2,),
        vmem=58,
        cost_estimate=cost(2 * 256 * F * D, 5 << 20),
    )


def add_kernel(n, *refs):
    for i in range(n):
        refs[2 * n + i][...] = refs[i][...] + refs[n + i][...]


def add(a, b, after=()):
    n = len(a)
    return run(
        functools.partial(add_kernel, n),
        [shape(v.shape) for v in a],
        (*a, *b),
        [WHOLE] * (2 * n),
        [WHOLE] * n,
        after,
        cost_estimate=cost(1e6, sum(3 * v.size * 4 for v in a)),
    )


def add_halves_kernel(a_ref, b_ref, got_ref, keep_ref, send_ref):
    keep_ref[...] = a_ref[...] + got_ref[:2]
    send_ref[...] = b_ref[...] + got_ref[2:]


def add_halves(a, b, got, after=()):
    return run(
        add_halves_kernel,
        [shape(a.shape)] * 2,
        (a, b, got),
        [WHOLE] * 3,
        [WHOLE] * 2,
        after,
        cost_estimate=cost(1e6, 6 * a.size * 4),
    )


def add_pair_kernel(a_ref, got_ref, keep_ref, send_ref):
    keep_ref[...] = a_ref[0] + got_ref[0]
    send_ref[...] = a_ref[1] + got_ref[1]


def add_pair(a, got, after=()):
    return run(
        add_pair_kernel,
        [shape(a.shape[1:])] * 2,
        (a, got),
        [WHOLE] * 2,
        [WHOLE] * 2,
        after,
        cost_estimate=cost(1e6, 3 * a.size * 4),
    )


def halves_kernel(a, b, top, bottom):
    h = T // 2
    top[...] = a[:h, :]
    bottom[...] = b[h:, :]


def pack0_kernel(x, a, pair):
    pair[:T, :] = x[...]
    pair[T:, :] = a[...]


def pack1_kernel(b, c, d, pair):
    h = T // 2
    pair[:T, :] = b[...]
    pair[T : T + h, :] = c[...]
    pair[T + h :, :] = d[...]


def pack(kernel, args, rows, after, steps=2):
    strip = lambda n: pl.BlockSpec((n, D // steps), lambda i: (0, i))
    return run(
        kernel,
        [shape((r, D), BF16) for r in rows],
        args,
        [strip(v.shape[0]) for v in args],
        [strip(r) for r in rows],
        after,
        grid=(steps,),
        cost_estimate=cost(1e6, 4 * sum(rows) * D),
    )


def sketch_kernel(pos_ref, h0, h1, elo_ref, ehi_ref, x_ref, a_ref, b_ref, c_ref, d_ref, keep_ref, send_ref, other_ref):
    c, z = pos_ref[0], pos_ref[1]
    h = jnp.concatenate(split(h0[...] + h1[...], 3), 0)
    n = D // 8
    outs = [keep_ref.at[0], keep_ref.at[1], send_ref.at[0], send_ref.at[1]] + [other_ref.at[i] for i in range(N)]
    for k, out in enumerate(outs):
        half, part = c ^ (k // N), z ^ (k % N)
        columns = pl.ds(pl.multiple_of((half * N + part) * n, n), n)
        x = jnp.concatenate([r[:, columns] for r in (x_ref, a_ref, b_ref, c_ref, d_ref)], 0)
        out[...] = add3(dot(h, x)) + jnp.where(half == 0, elo_ref[part], ehi_ref[part])


def sketch_part(pos, h, e, xs, after):
    return run(
        sketch_kernel,
        [shape((2, R, D // 8)), shape((2, R, D // 8)), shape((N, R, D // 8))],
        (pos, *h, *e, *xs),
        [SMEM] + [WHOLE] * 9,
        [WHOLE] * 3,
        after,
        cost_estimate=cost(2 * 256 * F * D, 6 << 20),
    )


def basis_kernel(pos_ref, mine_ref, other_ref, out_ref, s_ref):
    c, z = pos_ref[0], pos_ref[1]
    n = D // 8
    for half, ref in ((1 - c, mine_ref), (c, other_ref)):
        for i in range(N):
            chunk = half * N + (z ^ i)
            s_ref[:, pl.ds(pl.multiple_of(chunk * n, n), n)] = ref[i] * 0.25
    s = s_ref[...]
    gram = dot_both(s, s, NT)
    row = lax.broadcasted_iota(jnp.int32, (R, 2 * R), 0)
    col = lax.broadcasted_iota(jnp.int32, (R, 2 * R), 1)
    work = jnp.concatenate([gram, jnp.zeros((R, R), F32)], 1) + jnp.where(col == row + R, 1.0, 0.0)
    done = jnp.zeros((R, 2 * R), F32)
    for j in range(R):
        inv = 1.0 / jnp.sqrt(work[j : j + 1, j : j + 1])
        line = work[j : j + 1, :] * inv
        done = jnp.where(row == j, line, done)
        work = work - jnp.where(row > j, work[:, j : j + 1] * inv, 0.0) * line
    out_ref[...] = dot_both(done[:, R:], s, (((1,), (0,)), ((), ())))


def basis(pos, mine, other, after):
    return run(
        basis_kernel,
        shape((R, D)),
        (pos, mine, other),
        [SMEM, WHOLE, WHOLE],
        WHOLE,
        after,
        scratch_shapes=[pltpu.VMEM((R, D), F32)],
        cost_estimate=cost(8e9, 1 << 20),
    )


def merge_kernel(n, first, rows, from_errors, off_ref, acc_ref, *refs):
    xs, gs, out_ref = refs[:n], refs[n : 3 * n], refs[-1]
    x = jnp.concatenate([r[...] for r in xs], 0)
    g = jnp.concatenate([r[...] for r in gs], 0)
    at = pl.ds(pl.multiple_of((pl.program_id(0) + first) * rows, rows), rows)
    out_ref[at, :] = (acc_ref[...] if from_errors else acc_ref[at, :]) + dot(x, g, TN)


def merge(off, errors, acc, groups, g, lo, hi, after=(), rows=512):
    n, first = len(groups), lo // rows
    tile = pl.BlockSpec((rows, F), lambda i, off: (i + first, 0))
    at = lambda k: pl.BlockSpec((T, F), lambda i, off: (off[k] // T, 0))
    in_specs = [WHOLE if errors is None else tile]
    in_specs += [pl.BlockSpec((2 * T, rows), lambda i, off: (0, i + first))] * n
    for s, _ in groups:
        in_specs += [at(s), at(s + 1)]
    args = [off, acc if errors is None else errors] + [x for _, x in groups] + [g] * (2 * n)
    alias = {}
    if errors is None:
        alias = {1: 0}
    elif acc is not None:
        alias = {len(args): 0}
        after = (acc, *after)
    return run(
        functools.partial(merge_kernel, n, first, rows, errors is not None),
        pltpu.VMEM((D, F), F32),
        args,
        in_specs,
        WHOLE,
        after,
        prefetch=1,
        grid=((hi - lo) // rows,),
        vmem=24 if errors is None else 50,
        input_output_aliases=alias,
        cost_estimate=cost(2 * 256 * n * (hi - lo) * F, (hi - lo) * 4096 + n * (hi - lo) * 512),
    )


def right_kernel(p_ref, m_ref, q_ref):
    total, n = jnp.zeros((R, F), F32), 512
    for k in range(D // n):
        p = jnp.concatenate(split(p_ref[:, k * n : (k + 1) * n], 3), 0)
        t1, t2 = split(m_ref[k * n : (k + 1) * n, :], 2)
        a, b = dot(p, t1), dot(p[: 2 * R], t2)
        total += a[:R] + ((a[R : 2 * R] + b[:R]) + (a[2 * R :] + b[R:]))
    q_ref[...] = total


def right_part(p, merged, after):
    return run(
        right_kernel,
        shape((R, F)),
        (p, merged),
        [WHOLE] * 2,
        WHOLE,
        after,
        cost_estimate=cost(4 * 256 * D * F, 9 << 20),
    )


def right_rest_kernel(n, off_ref, p_ref, q_ref, g_ref, *refs):
    xs, out_ref = refs[:n], refs[n]
    p = jnp.concatenate(split(p_ref[...], 3), 0)
    total = q_ref[...]
    for i, (start, x) in enumerate(zip(RIGHT_STARTS, xs)):
        y = jnp.concatenate(split(add3(dot(p, x[...], NT)), 3), 0)
        rows = [g_ref[pl.ds(pl.multiple_of(off_ref[start + k], T), T), :] for k in range(2)]
        total += add3(dot(y, jnp.concatenate(rows, 0)))
    out_ref[...] = total


RIGHT_STARTS = (12, 28, 14, 30)


def right_rest(off, p, q, g, xs, after=()):
    return run(
        functools.partial(right_rest_kernel, len(xs)),
        shape((R, F)),
        (off, p, q, g, *xs),
        [SMEM] + [WHOLE] * (3 + len(xs)),
        WHOLE,
        after,
        vmem=24,
        cost_estimate=cost(2 * 256 * len(xs) * 256 * D, 14 << 20),
    )


def final_kernel(n, rows, off_ref, m_ref, *refs):
    xs, gs, (p_ref, q0, q1, q2, q3, out_ref, q_ref) = refs[:n], refs[n : 3 * n], refs[3 * n :]
    q = ((q0[...] + q1[...]) + (q2[...] + q3[...])) * 0.25
    q_ref[...] = q
    p1, p2 = split(p_ref[...], 2)
    s1, s2 = split(-q, 2)
    left = jnp.concatenate([r[...] for r in xs] + [p1, p1, p2], 0)
    right = jnp.concatenate([r[...] for r in gs] + [s1, s2, s1], 0)
    at = pl.ds(pl.multiple_of(pl.program_id(0) * rows, rows), rows)
    out_ref[...] = m_ref[at, :] + dot(left, right, TN)


def final(off, merged, groups, g, p, q, rows=512):
    n = len(groups)
    whole = pl.BlockSpec((R, F), lambda i, off: (0, 0))
    at = lambda k: pl.BlockSpec((T, F), lambda i, off: (off[k] // T, 0))
    in_specs = [WHOLE] + [pl.BlockSpec((2 * T, rows), lambda i, off: (0, i))] * n
    for s, _ in groups:
        in_specs += [at(s), at(s + 1)]
    return run(
        functools.partial(final_kernel, n, rows),
        [shape((D, F)), shape((R, F))],
        [off, merged] + [x for _, x in groups] + [g] * (2 * n) + [p, *q],
        in_specs + [pl.BlockSpec((R, rows), lambda i, off: (0, i))] + [whole] * N,
        [pl.BlockSpec((rows, F), lambda i, off: (i, 0)), whole],
        prefetch=1,
        grid=(D // rows,),
        vmem=24,
        cost_estimate=cost(2 * 256 * n * D * F, 16 << 20),
    )


def later(array, behind):
    return lax.optimization_barrier((array, behind))[0]


def body(x, g, e, q_init):
    me = lax.axis_index("tensor")
    pos = jnp.stack([me % 2, lax.axis_index("dp")]).astype(jnp.int32)
    off = lax.dynamic_index_in_dim(jnp.asarray(block_tables()), me, 0, keepdims=False)
    e, q = e[0], q_init.T

    a, b = hop(x, True, 1), hop(x, True, -1)
    keep, send, other = tokens(off, q, g)
    keep, send = add_halves(keep, send, swap(other))
    got = twin(send, False, 2)
    e_lo = errors(q, e, 0, (send,))
    h, send = add_pair(keep, got, (e_lo,))
    h_got = twin(send, False, 1)

    top, bottom = pack(halves_kernel, (a, b), (T // 2, T // 2), (send,))
    c, d = hop(top, True, 1), hop(bottom, True, -1)
    (g0,) = pack(pack0_kernel, (x, a), (2 * T,), (h_got, top))
    l0, r0 = hop(g0, False, 1), hop(g0, False, -1)
    e_hi = errors(q, e, 1, (g0,))
    keep, send, other = sketch_part(pos, (h, h_got), (e_lo, e_hi), (x, a, b, c, d), (e_hi,))
    got = swap(other)
    (g1,) = pack(pack1_kernel, (b, c, d), (2 * T,), (other,))
    l1, r1 = hop(g1, False, 1), hop(g1, False, -1)

    keep, send = add_halves(keep, send, got, (g1,))
    got = hop_z(send, 2)
    t0, t1 = swap(later(g0, send)), swap(later(g1, send))
    near = [(0, g0), (2, g1), (16, t0), (18, t1)]
    acc = merge(off, e, None, near, g, 0, 2048, (send,))
    keep, send = add_pair(keep, got, (acc,))
    got = hop_z(send, 1)
    acc = merge(off, e, acc, near, g, 2048, 4096, (send,))
    (s,) = add([keep], [got], (acc,))
    got = twin(s, True, 1)
    l0, r0 = later(l0, s), later(r0, s)
    u0, v0 = swap(l0), swap(r0)
    o0 = hop(l0, False, 1)
    (s,) = add([s], [got], ())
    got = twin(s, True, 2)
    mid = [(4, l0), (8, r0), (20, u0), (24, v0)]
    acc = merge(off, None, acc, mid, g, 0, 2048, (s,))
    (s,) = add([s], [got], (acc,))
    s = swap(s)
    got = twin(s, True, 1)
    acc = merge(off, None, acc, mid, g, 2048, 4096, (s,))
    (s,) = add([s], [got], (acc,))
    got = twin(s, True, 2)
    (s,) = add([s], [got], (acc,))
    got = hop_z(s, 1)
    l1, r1 = later(l1, s), later(r1, s)
    o1 = hop(r1, False, -1)
    u1, v1 = swap(l1), swap(r1)
    far = [(6, l1), (10, r1), (22, u1), (26, v1)]
    acc = merge(off, None, acc, far, g, 0, 2048, (s,))
    pair = later(jnp.stack([s, got]), acc)
    got = hop_z(pair, 2)
    acc = merge(off, None, acc, far, g, 2048, 4096, (pair,))
    stack = later(jnp.concatenate([pair, got]), acc)
    p = basis(pos, stack, swap(stack), (acc,))

    qp = right_part(p, acc, ())
    o0, o1 = later(o0, qp), later(o1, qp)
    last = [(12, o0), (28, swap(o0)), (14, o1), (30, swap(o1))]
    qp = right_rest(off, p, qp, g, [v for _, v in last])
    qs = (qp, around_z(qp, 2), around_z(qp, 1), around_z(qp, -1))
    err, qf = final(off, acc, last, g, p, qs)
    return err[None], p.T, qf.T


def solution(mesh):
    in_specs = (
        P(("dp", "tensor"), None),
        P("dp", "tensor"),
        P("dp", None, "tensor"),
        P("tensor", None),
    )
    out_specs = (P("dp", None, "tensor"), P(), P("tensor", None))
    return jax.shard_map(body, mesh=mesh, in_specs=in_specs, out_specs=out_specs, check_vma=False)
```

time: 387 us -> 161 us (0.42)
  waiting for transfers between devices: 304 us -> 34 us
  Pallas kernels: 0 us -> 68.5 us
  matrix products: 61.7 us -> 0 us
  starting transfers between devices: 0.3 us -> 45 us
  between operations: 13.8 us -> 1.05 us
  local copies, waits for them, and re-layouts: 0.09 us -> 11.7 us
  other arithmetic: 7.53 us -> 0.1 us
    psum x2 -> x0, waiting for transfers between devices: 184 us -> none  [the longest x1 144 us: body(): lax.psum(jnp.dot(merged, q_init, precision=highest), ('dp', 'tensor'))]
    all_gather x1 -> x0, waiting for transfers between devices: 118 us -> none  [body(): lax.all_gather(x_rows, 'tensor', axis=0, tiled=True)]
    pallas_call x0 -> x26, Pallas kernels: none -> 68.5 us  [run(): pl.pallas_call(wrapped, out_shape=out_shape, compiler_params=options, **kw)]
    dot_general x5 -> x0, matrix products: 60 us -> none  [the longest x1 28 us: body(): lax.dot_general(lax.all_gather(x_rows, 'tensor', axis=0, tiled=True), gra...]
    ppermute x0 -> x35, starting transfers between devices: none -> 45 us  [the longest x10 16.3 us: hop(): return lax.ppermute(array, 'tensor', pairs)]
    ppermute x0 -> x35, waiting for transfers between devices: none -> 34 us  [the longest x6 13.4 us: twin(): return lax.ppermute(array, 'tensor', pairs)]
    unnamed x6 -> x36, local copies, waits for them, and re-layouts: 0.02 us -> 11 us
    another operation x5 -> x2, other arithmetic: 6.68 us -> 0.08 us  [the longest x1 0.07 us: body(): pos = jnp.stack([me % 2, lax.axis_index('dp')]).astype(jnp.int32)]
  transfers between devices with their start and end apart: 3 -> 35, of which waited for: 3 -> 15; matrix products, arithmetic and copies ran while one was open for 0% -> 0% of each run, Pallas kernels for 0% -> 32%
where the time goes in v2:
time: 161 us; the launch traced here: 160 us
  Pallas kernels  68.5 us (43%)
  starting transfers between devices  45 us (28%)
  waiting for transfers between devices  34 us (21%)
  local copies, waits for them, and re-layouts  11.7 us (7%)
    pallas_call x26, Pallas kernels, run(): pl.pallas_call(wrapped, out_shape=out_shape, compiler_params=options, **kw)  68.5 us
    ppermute x10, starting transfers between devices, hop(): return lax.ppermute(array, 'tensor', pairs)  16.3 us
    ppermute x6, waiting for transfers between devices, twin(): return lax.ppermute(array, 'tensor', pairs)  13.4 us
    ppermute x4, starting transfers between devices, hop_z(): return lax.ppermute(array, 'dp', [(i, i ^ bit) for i in range(N)])  11.1 us
    ppermute x12, waiting for transfers between devices, swap(): return lax.ppermute(array, 'tensor', [(i, i ^ 1) for i in range(2 * N * N)])  11 us
    unnamed x36, local copies, waits for them, and re-layouts  11 us
    ppermute x6, starting transfers between devices, twin(): return lax.ppermute(array, 'tensor', pairs)  9.42 us
    ppermute x3, starting transfers between devices, around_z(): return lax.ppermute(array, 'dp', [(i, (i + d) % N) for i in range(N)])  5.76 us
  transfers between devices with their start and end apart: 35, of which 15 were waited for; matrix products, arithmetic and copies ran while one was open for 0% of the time, Pallas kernels for 32%

profile of v2, /device:TPU:0, one launch (start us, length us, event | category | flops | bytes accessed | tf_op | source)
XLA Modules:
  0.0 160.3 jit_solution(14224876130942259594)
XLA Ops:
  11.2 3.4 %collective-permute-start.2 = (f32[2,32,512]{2,1,0:T(8,128)S(1)}, f32[2,32,512]{2,1,0:T(8,128)S(1)}, u32[]{:S(2)}, u32[]{:S(2)}) collective-permute-start(f32[2,32,512]{2,1,0:T(8,128)S(1)} %get-tuple-element.35.refs_2_), channel_id=1, source_target_pairs={{0,4},{1,17},{2,6},{3,19},{4,0},{5,21},{6,2},{7,23},{8,12},{9,25},... | collective-permute-start | bytes 393224 | tf_op jit(solution)/shard_map/ppermute | solution.py:54
  14.6 3.8 %shard_map.78.refs_2_.refs_3_ = f32[4,32,512]{2,1,0:T(8,128)} custom-call(f32[32,512]{1,0:T(8,128)} %bitcast.12, f32[4096,512]{1,0:T(8,128)} %bitcast.16, f32[2,32,512]{2,1,0:T(8,128)} %copy-done.13), custom_call_target="tpu_custom_call" | custom-call | flops 1073741824 | bytes 5242880 | tf_op jit(solution)/shard_map/pallas_call | solution.py:126
  25.2 3.9 %collective-permute-done.3.refs_2_ = f32[32,512]{1,0:T(8,128)S(1)} collective-permute-done((f32[32,512]{1,0:T(8,128)S(1)}, f32[32,512]{1,0:T(8,128)S(1)}, u32[]{:S(2)}, u32[]{:S(2)}) %collective-permute-start.3) | collective-permute-done | bytes 65568 | tf_op jit(solution)/shard_map/ppermute | solution.py:54
  30.8 3.8 %shard_map.82.refs_4_.refs_10_ = f32[4,32,512]{2,1,0:T(8,128)} custom-call(f32[32,512]{1,0:T(8,128)} %bitcast.13, f32[4096,512]{1,0:T(8,128)} %bitcast.17, bf16[256,4096]{1,0:T(8,128)(2,1)} %copy-done.4), custom_call_target="tpu_custom_call" | custom-call | flops 1073741824 | bytes 5242880 | tf_op jit(solution)/shard_map/pallas_call | solution.py:126
  39.3 2.3 %copy-done.5 = bf16[256,4096]{1,0:T(8,128)(2,1)S(1)} copy-done((bf16[256,4096]{1,0:T(8,128)(2,1)S(1)}, bf16[256,4096]{1,0:T(8,128)(2,1)}, u32[]{:S(2)}) %copy-start.5) | copy-done | bytes 2097176
  45.3 3.9 %collective-permute-start.10 = (f32[2,32,512]{2,1,0:T(8,128)S(1)}, f32[2,32,512]{2,1,0:T(8,128)S(1)}, u32[]{:S(2)}, u32[]{:S(2)}) collective-permute-start(f32[2,32,512]{2,1,0:T(8,128)S(1)} %get-tuple-element.43.refs_14_), channel_id=1, source_target_pairs={{0,64},{32,96},{64,0},{96,32},{1,65},{33,97},{65,1},{97,33},{2,66}... | collective-permute-start | bytes 393224 | tf_op jit(solution)/shard_map/ppermute | solution.py:42
  50.5 6.7 %shard_map.86.refs_2_.refs_14_ = f32[4096,512]{1,0:T(8,128)S(1)} custom-call(s32[64]{0:T(128)} %copy-done.15, f32[4096,512]{1,0:T(8,128)} %bitcast.18, bf16[256,4096]{1,0:T(8,128)(2,1)} %copy-done.4, bf16[256,4096]{1,0:T(8,128)(2,1)} %copy-done.2, bf16[256,4096]{1,0:T(8,128)(2,1)} %copy-done.17, bf16[256,4096]{1,0:T(8,128)(2,1)} %collective-permute-done.9.refs_5_, ...), custom_call_target="tpu_custom_call" | custom-call | flops 2147483648 | bytes 12582912 | tf_op jit(solution)/shard_map/pallas_call | solution.py:126
  58.6 6.7 %shard_map.88.refs_2_.refs_1_ = f32[4096,512]{1,0:T(8,128)S(1)} custom-call(s32[64]{0:T(128)} %copy-done.15, f32[4096,512]{1,0:T(8,128)} %bitcast.19, bf16[256,4096]{1,0:T(8,128)(2,1)} %copy-done.4, bf16[256,4096]{1,0:T(8,128)(2,1)} %copy-done.2, bf16[256,4096]{1,0:T(8,128)(2,1)} %copy-done.17, ...), custom_call_target="tpu_custom_call", output_to_operand_aliasing={{}: (14, {})} | custom-call | flops 2147483648 | bytes 12582912 | tf_op jit(solution)/shard_map/pallas_call | solution.py:126
  65.4 4.0 %collective-permute-done.11.refs_2_ = bf16[256,4096]{1,0:T(8,128)(2,1)} collective-permute-done((bf16[256,4096]{1,0:T(8,128)(2,1)S(1)}, bf16[256,4096]{1,0:T(8,128)(2,1)}, u32[]{:S(2)}, u32[]{:S(2)}) %collective-permute-start.11) | collective-permute-done | bytes 2097184 | tf_op jit(solution)/shard_map/ppermute | solution.py:34
  73.3 4.9 %collective-permute-done.16.refs_1_ = f32[32,512]{1,0:T(8,128)S(1)} collective-permute-done((f32[32,512]{1,0:T(8,128)S(1)}, f32[32,512]{1,0:T(8,128)S(1)}, u32[]{:S(2)}, u32[]{:S(2)}) %collective-permute-start.16) | collective-permute-done | bytes 65568 | tf_op jit(solution)/shard_map/ppermute | solution.py:54
  80.0 5.1 %shard_map.91.refs_2_.refs_1_ = f32[4096,512]{1,0:T(8,128)S(1)} custom-call(s32[64]{0:T(128)S(1)} %copy-done.16, f32[4096,512]{1,0:T(8,128)S(1)} %shard_map.88.refs_2_.refs_1_, bf16[256,4096]{1,0:T(8,128)(2,1)} %collective-permute-done.11.refs_2_, bf16[256,4096]{1,0:T(8,128)(2,1)} %collective-permute-done.13.refs_3_, ...), custom_call_target="tpu_custom_call", output_to_operand_aliasing={{}: (1, {})} | custom-call | flops 2147483648 | bytes 12582912 | tf_op jit(solution)/shard_map/pallas_call | solution.py:126
  87.4 5.0 %shard_map.93.refs_2_.refs_1_ = f32[4096,512]{1,0:T(8,128)S(1)} custom-call(s32[64]{0:T(128)S(1)} %copy-done.16, f32[4096,512]{1,0:T(8,128)S(1)} %shard_map.91.refs_2_.refs_1_, bf16[256,4096]{1,0:T(8,128)(2,1)} %collective-permute-done.11.refs_2_, bf16[256,4096]{1,0:T(8,128)(2,1)} %collective-permute-done.13.refs_3_, ...), custom_call_target="tpu_custom_call", output_to_operand_aliasing={{}: (1, {})} | custom-call | flops 2147483648 | bytes 12582912 | tf_op jit(solution)/shard_map/pallas_call | solution.py:126
  94.6 4.5 %collective-permute-done.21.refs_1_ = f32[32,512]{1,0:T(8,128)S(1)} collective-permute-done((f32[32,512]{1,0:T(8,128)S(1)}, f32[32,512]{1,0:T(8,128)S(1)}, u32[]{:S(2)}, u32[]{:S(2)}) %collective-permute-start.21) | collective-permute-done | bytes 65568 | tf_op jit(solution)/shard_map/ppermute | solution.py:54
  100.5 3.2 %collective-permute-start.30 = (bf16[256,4096]{1,0:T(8,128)(2,1)S(1)}, bf16[256,4096]{1,0:T(8,128)(2,1)S(1)}, u32[]{:S(2)}, u32[]{:S(2)}) collective-permute-start(bf16[256,4096]{1,0:T(8,128)(2,1)S(1)} %collective-permute-done.22.refs_3_), channel_id=1, source_target_pairs={{0,6},{1,25},{2,0},{3,27},{4,2},{5,29},{6,4},{7,31},{8,14},{9,1},{... | collective-permute-start | bytes 6291464 | tf_op jit(solution)/shard_map/ppermute | solution.py:34
  105.7 2.4 %collective-permute-done.25 = f32[32,512]{1,0:T(8,128)S(1)} collective-permute-done((f32[32,512]{1,0:T(8,128)S(1)}, f32[32,512]{1,0:T(8,128)S(1)}, u32[]{:S(2)}, u32[]{:S(2)}) %collective-permute-start.25) | collective-permute-done | bytes 65568 | tf_op jit(solution)/shard_map/ppermute | solution.py:42
  108.1 4.0 %shard_map.96.refs_1_ = f32[4096,512]{1,0:T(8,128)S(1)} custom-call(s32[64]{0:T(128)S(1)} %copy-done.16, f32[4096,512]{1,0:T(8,128)S(1)} %shard_map.93.refs_2_.refs_1_, bf16[256,4096]{1,0:T(8,128)(2,1)S(1)} %collective-permute-done.19.refs_2_, bf16[256,4096]{1,0:T(8,128)(2,1)S(1)} %collective-permute-done.22.refs_3_, ...), custom_call_target="tpu_custom_call", output_to_operand_aliasing={{}: (1, {})} | custom-call | flops 2147483648 | bytes 12582912 | tf_op jit(solution)/shard_map/pallas_call | solution.py:126
  112.1 3.9 %collective-permute-start.27 = (f32[2,32,512]{2,1,0:T(8,128)S(1)}, f32[2,32,512]{2,1,0:T(8,128)S(1)}, u32[]{:S(2)}, u32[]{:S(2)}) collective-permute-start(f32[2,32,512]{2,1,0:T(8,128)S(1)} %pad_maximum_fusion.1.refs_14_), channel_id=1, source_target_pairs={{0,64},{32,96},{64,0},{96,32},{1,65},{33,97},{65,1},{97,33},{2,66}... | collective-permute-start | bytes 393224 | tf_op jit(solution)/shard_map/ppermute | solution.py:42
  116.0 4.0 %shard_map.97.refs_3_.refs_1_ = f32[4096,512]{1,0:T(8,128)S(1)} custom-call(s32[64]{0:T(128)S(1)} %copy-done.16, f32[4096,512]{1,0:T(8,128)S(1)} %shard_map.96.refs_1_, bf16[256,4096]{1,0:T(8,128)(2,1)S(1)} %collective-permute-done.19.refs_2_, bf16[256,4096]{1,0:T(8,128)(2,1)S(1)} %collective-permute-done.22.refs_3_, ...), custom_call_target="tpu_custom_call", output_to_operand_aliasing={{}: (1, {})} | custom-call | flops 2147483648 | bytes 12582912 | tf_op jit(solution)/shard_map/pallas_call | solution.py:126
  121.7 6.5 %shard_map.98.refs_0_.refs_1_.refs_14_ = f32[32,4096]{1,0:T(8,128)} custom-call(s32[2]{0:T(128)S(1)} %pad_add_fusion.refs_0_, f32[4,32,512]{2,1,0:T(8,128)S(1)} %pad_maximum_fusion.refs_1_, f32[4,32,512]{2,1,0:T(8,128)S(1)} %collective-permute-done.28.refs_2_, f32[4096,512]{1,0:T(8,128)S(1)} %shard_map.97.refs_3_.refs_1_), custom_call_target="tpu_custom_call" | custom-call | flops 8000000000 | bytes 1048576 | tf_op jit(solution)/shard_map/pallas_call | solution.py:126
  131.6 3.6 %collective-permute-done.29.refs_5_.refs_3_ = bf16[256,4096]{1,0:T(8,128)(2,1)S(1)} collective-permute-done((bf16[256,4096]{1,0:T(8,128)(2,1)S(1)}, bf16[256,4096]{1,0:T(8,128)(2,1)S(1)}, u32[]{:S(2)}, u32[]{:S(2)}) %collective-permute-start.29) | collective-permute-done | bytes 2097184 | tf_op jit(solution)/shard_map/ppermute | solution.py:38
  135.3 3.0 %collective-permute-done.31.refs_7_.refs_5_ = bf16[256,4096]{1,0:T(8,128)(2,1)S(1)} collective-permute-done((bf16[256,4096]{1,0:T(8,128)(2,1)S(1)}, bf16[256,4096]{1,0:T(8,128)(2,1)S(1)}, u32[]{:S(2)}, u32[]{:S(2)}) %collective-permute-start.31) | collective-permute-done | bytes 2097184 | tf_op jit(solution)/shard_map/ppermute | solution.py:38
  138.3 4.6 %shard_map.100.refs_15_ = f32[32,512]{1,0:T(8,128)S(1)} custom-call(s32[64]{0:T(128)S(1)} %copy-done.16, f32[32,4096]{1,0:T(8,128)S(1)} %copy-done.6, f32[32,512]{1,0:T(8,128)S(1)} %shard_map.99.refs_2_, bf16[4096,512]{1,0:T(8,128)(2,1)S(1)} %copy-done.1, bf16[256,4096]{1,0:T(8,128)(2,1)S(1)} %collective-permute-done.26.refs_4_.refs_2_, ...), custom_call_target="tpu_custom_call" | custom-call | flops 2147483648 | bytes 14680064 | tf_op jit(solution)/shard_map/pallas_call | solution.py:126
  142.8 2.5 %collective-permute-start.32 = (f32[32,512]{1,0:T(8,128)S(1)}, f32[32,512]{1,0:T(8,128)S(1)}, u32[]{:S(2)}, u32[]{:S(2)}) collective-permute-start(f32[32,512]{1,0:T(8,128)S(1)} %shard_map.100.refs_15_), channel_id=1, source_target_pairs={{0,64},{32,96},{64,0},{96,32},{1,65},{33,97},{65,1},{97,33},{2,66}... | collective-permute-start | bytes 196616 | tf_op jit(solution)/shard_map/ppermute | solution.py:46
  150.8 9.5 %shard_map.101 = (f32[4096,512]{1,0:T(8,128)}, f32[32,512]{1,0:T(8,128)}) custom-call(s32[64]{0:T(128)S(1)} %copy-done.16, f32[4096,512]{1,0:T(8,128)S(1)} %shard_map.97.refs_3_.refs_1_, bf16[256,4096]{1,0:T(8,128)(2,1)S(1)} %collective-permute-done.26.refs_4_.refs_2_, bf16[256,4096]{1,0:T(8,128)(2,1)S(1)} %collective-permute-done.29.refs_5_.refs_3_, ...), custom_call_target="tpu_custom_call" | custom-call | flops 4294967296 | bytes 16777216 | tf_op jit(solution)/shard_map/pallas_call | solution.py:126
  (112 shorter events, 54.1 us)
Async XLA Ops:
  0.6 18.9 %collective-permute-start = (bf16[128,4096]{1,0:T(8,128)(2,1)}, bf16[128,4096]{1,0:T(8,128)(2,1)S(1)}, u32[]{:S(2)}, u32[]{:S(2)}) collective-permute-start(bf16[128,4096]{1,0:T(8,128)(2,1)} %refs_5_.1), channel_id=1, source_target_pairs={{0,8},{1,3},{2,10},{3,5},{4,12},{5,7},{6,14},{7,1},{8,16},{9,11},{... | collective-permute-start | bytes 3145736 | tf_op jit(solution)/shard_map/ppermute | solution.py:34
  2.3 17.3 %collective-permute-start.4 = (bf16[128,4096]{1,0:T(8,128)(2,1)}, bf16[128,4096]{1,0:T(8,128)(2,1)S(1)}, u32[]{:S(2)}, u32[]{:S(2)}) collective-permute-start(bf16[128,4096]{1,0:T(8,128)(2,1)} %refs_5_.1), channel_id=1, source_target_pairs={{0,24},{1,7},{2,26},{3,1},{4,28},{5,3},{6,30},{7,5},{8,0},{9,15},{... | collective-permute-start | bytes 3145736 | tf_op jit(solution)/shard_map/ppermute | solution.py:34
  11.2 7.3 %collective-permute-start.2 = (f32[2,32,512]{2,1,0:T(8,128)S(1)}, f32[2,32,512]{2,1,0:T(8,128)S(1)}, u32[]{:S(2)}, u32[]{:S(2)}) collective-permute-start(f32[2,32,512]{2,1,0:T(8,128)S(1)} %get-tuple-element.35.refs_2_), channel_id=1, source_target_pairs={{0,4},{1,17},{2,6},{3,19},{4,0},{5,21},{6,2},{7,23},{8,12},{9,25},... | collective-permute-start | bytes 393224 | tf_op jit(solution)/shard_map/ppermute | solution.py:54
  20.8 13.9 %collective-permute-start.5 = (bf16[64,4096]{1,0:T(8,128)(2,1)}, bf16[64,4096]{1,0:T(8,128)(2,1)}, u32[]{:S(2)}, u32[]{:S(2)}) collective-permute-start(bf16[64,4096]{1,0:T(8,128)(2,1)} %get-tuple-element.37.refs_3_), channel_id=1, source_target_pairs={{0,8},{1,3},{2,10},{3,5},{4,12},{5,7},{6,14},{7,1},{8,16},{9,11},{... | collective-permute-start | bytes 1572872 | tf_op jit(solution)/shard_map/ppermute | solution.py:34
  22.1 12.6 %collective-permute-start.6 = (bf16[64,4096]{1,0:T(8,128)(2,1)}, bf16[64,4096]{1,0:T(8,128)(2,1)}, u32[]{:S(2)}, u32[]{:S(2)}) collective-permute-start(bf16[64,4096]{1,0:T(8,128)(2,1)} %get-tuple-element.38), channel_id=1, source_target_pairs={{0,24},{1,7},{2,26},{3,1},{4,28},{5,3},{6,30},{7,5},{8,0},{9,15},{... | collective-permute-start | bytes 1572872 | tf_op jit(solution)/shard_map/ppermute | solution.py:34
  41.5 7.6 %collective-permute-start.8 = (bf16[256,4096]{1,0:T(8,128)(2,1)S(1)}, bf16[256,4096]{1,0:T(8,128)(2,1)S(1)}, u32[]{:S(2)}, u32[]{:S(2)}) collective-permute-start(bf16[256,4096]{1,0:T(8,128)(2,1)S(1)} %copy-done.5), channel_id=1, source_target_pairs={{0,1},{1,0},{2,3},{3,2},{4,5},{5,4},{6,7},{7,6},{8,9},{9,8},{10,11... | collective-permute-start | bytes 6291464 | tf_op jit(solution)/shard_map/ppermute | solution.py:38
  42.0 8.5 %collective-permute-start.9 = (bf16[256,4096]{1,0:T(8,128)(2,1)S(1)}, bf16[256,4096]{1,0:T(8,128)(2,1)}, u32[]{:S(2)}, u32[]{:S(2)}) collective-permute-start(bf16[256,4096]{1,0:T(8,128)(2,1)S(1)} %shard_map.84.refs_3_), channel_id=1, source_target_pairs={{0,1},{1,0},{2,3},{3,2},{4,5},{5,4},{6,7},{7,6},{8,9},{9,8},{10,11... | collective-permute-start | bytes 6291464 | tf_op jit(solution)/shard_map/ppermute | solution.py:38
  42.1 27.4 %collective-permute-start.11 = (bf16[256,4096]{1,0:T(8,128)(2,1)S(1)}, bf16[256,4096]{1,0:T(8,128)(2,1)}, u32[]{:S(2)}, u32[]{:S(2)}) collective-permute-start(bf16[256,4096]{1,0:T(8,128)(2,1)S(1)} %copy-done.5), channel_id=1, source_target_pairs={{0,2},{1,9},{2,4},{3,11},{4,6},{5,13},{6,0},{7,15},{8,10},{9,17},{... | collective-permute-start | bytes 6291464 | tf_op jit(solution)/shard_map/ppermute | solution.py:34
  43.1 26.3 %collective-permute-start.13 = (bf16[256,4096]{1,0:T(8,128)(2,1)S(1)}, bf16[256,4096]{1,0:T(8,128)(2,1)}, u32[]{:S(2)}, u32[]{:S(2)}) collective-permute-start(bf16[256,4096]{1,0:T(8,128)(2,1)S(1)} %copy-done.5), channel_id=1, source_target_pairs={{0,6},{1,25},{2,0},{3,27},{4,2},{5,29},{6,4},{7,31},{8,14},{9,1},{... | collective-permute-start | bytes 6291464 | tf_op jit(solution)/shard_map/ppermute | solution.py:34
  45.3 11.9 %collective-permute-start.10 = (f32[2,32,512]{2,1,0:T(8,128)S(1)}, f32[2,32,512]{2,1,0:T(8,128)S(1)}, u32[]{:S(2)}, u32[]{:S(2)}) collective-permute-start(f32[2,32,512]{2,1,0:T(8,128)S(1)} %get-tuple-element.43.refs_14_), channel_id=1, source_target_pairs={{0,64},{32,96},{64,0},{96,32},{1,65},{33,97},{65,1},{97,33},{2,66}... | collective-permute-start | bytes 393224 | tf_op jit(solution)/shard_map/ppermute | solution.py:42
  57.2 8.1 %collective-permute-start.12 = (f32[32,512]{1,0:T(8,128)S(1)}, f32[32,512]{1,0:T(8,128)S(1)}, u32[]{:S(2)}, u32[]{:S(2)}) collective-permute-start(f32[32,512]{1,0:T(8,128)S(1)} %get-tuple-element.47.refs_15_), channel_id=1, source_target_pairs={{0,32},{32,0},{64,96},{96,64},{1,33},{33,1},{65,97},{97,65},{2,34}... | collective-permute-start | bytes 196616 | tf_op jit(solution)/shard_map/ppermute | solution.py:42
  69.4 10.6 %collective-permute-start.14 = (bf16[256,4096]{1,0:T(8,128)(2,1)}, bf16[256,4096]{1,0:T(8,128)(2,1)S(1)}, u32[]{:S(2)}, u32[]{:S(2)}) collective-permute-start(bf16[256,4096]{1,0:T(8,128)(2,1)} %collective-permute-done.11.refs_2_), channel_id=1, source_target_pairs={{0,1},{1,0},{2,3},{3,2},{4,5},{5,4},{6,7},{7,6},{8,9},{9,8},{10,11... | collective-permute-start | bytes 6291464 | tf_op jit(solution)/shard_map/ppermute | solution.py:38
  69.4 10.6 %collective-permute-start.15 = (bf16[256,4096]{1,0:T(8,128)(2,1)}, bf16[256,4096]{1,0:T(8,128)(2,1)S(1)}, u32[]{:S(2)}, u32[]{:S(2)}) collective-permute-start(bf16[256,4096]{1,0:T(8,128)(2,1)} %collective-permute-done.13.refs_3_), channel_id=1, source_target_pairs={{0,1},{1,0},{2,3},{3,2},{4,5},{5,4},{6,7},{7,6},{8,9},{9,8},{10,11... | collective-permute-start | bytes 6291464 | tf_op jit(solution)/shard_map/ppermute | solution.py:38
  69.9 29.2 %collective-permute-start.19 = (bf16[256,4096]{1,0:T(8,128)(2,1)S(1)}, bf16[256,4096]{1,0:T(8,128)(2,1)S(1)}, u32[]{:S(2)}, u32[]{:S(2)}) collective-permute-start(bf16[256,4096]{1,0:T(8,128)(2,1)S(1)} %copy-done.3), channel_id=1, source_target_pairs={{0,2},{1,9},{2,4},{3,11},{4,6},{5,13},{6,0},{7,15},{8,10},{9,17},{... | collective-permute-start | bytes 6291464 | tf_op jit(solution)/shard_map/ppermute | solution.py:34
  71.2 28.8 %collective-permute-start.22 = (bf16[256,4096]{1,0:T(8,128)(2,1)S(1)}, bf16[256,4096]{1,0:T(8,128)(2,1)S(1)}, u32[]{:S(2)}, u32[]{:S(2)}) collective-permute-start(bf16[256,4096]{1,0:T(8,128)(2,1)S(1)} %copy-done.3), channel_id=1, source_target_pairs={{0,6},{1,25},{2,0},{3,27},{4,2},{5,29},{6,4},{7,31},{8,14},{9,1},{... | collective-permute-start | bytes 6291464 | tf_op jit(solution)/shard_map/ppermute | solution.py:34
  78.2 6.9 %collective-permute-start.17 = (f32[32,512]{1,0:T(8,128)S(1)}, f32[32,512]{1,0:T(8,128)S(1)}, u32[]{:S(2)}, u32[]{:S(2)}) collective-permute-start(f32[32,512]{1,0:T(8,128)S(1)} %shard_map.90.refs_14_.refs_0_), channel_id=1, source_target_pairs={{0,16},{1,5},{2,18},{3,7},{4,20},{5,1},{6,22},{7,3},{8,24},{9,13},... | collective-permute-start | bytes 196616 | tf_op jit(solution)/shard_map/ppermute | solution.py:54
  92.4 6.6 %collective-permute-start.21 = (f32[32,512]{1,0:T(8,128)S(1)}, f32[32,512]{1,0:T(8,128)S(1)}, u32[]{:S(2)}, u32[]{:S(2)}) collective-permute-start(f32[32,512]{1,0:T(8,128)S(1)} %shard_map.94.refs_0_), channel_id=1, source_target_pairs={{0,16},{1,5},{2,18},{3,7},{4,20},{5,1},{6,22},{7,3},{8,24},{9,13},... | collective-permute-start | bytes 196616 | tf_op jit(solution)/shard_map/ppermute | solution.py:54
  100.0 8.0 %collective-permute-start.23 = (bf16[256,4096]{1,0:T(8,128)(2,1)S(1)}, bf16[256,4096]{1,0:T(8,128)(2,1)S(1)}, u32[]{:S(2)}, u32[]{:S(2)}) collective-permute-start(bf16[256,4096]{1,0:T(8,128)(2,1)S(1)} %collective-permute-done.19.refs_2_), channel_id=1, source_target_pairs={{0,1},{1,0},{2,3},{3,2},{4,5},{5,4},{6,7},{7,6},{8,9},{9,8},{10,11... | collective-permute-start | bytes 6291464 | tf_op jit(solution)/shard_map/ppermute | solution.py:38
  100.0 8.0 %collective-permute-start.24 = (bf16[256,4096]{1,0:T(8,128)(2,1)S(1)}, bf16[256,4096]{1,0:T(8,128)(2,1)S(1)}, u32[]{:S(2)}, u32[]{:S(2)}) collective-permute-start(bf16[256,4096]{1,0:T(8,128)(2,1)S(1)} %collective-permute-done.22.refs_3_), channel_id=1, source_target_pairs={{0,1},{1,0},{2,3},{3,2},{4,5},{5,4},{6,7},{7,6},{8,9},{9,8},{10,11... | collective-permute-start | bytes 6291464 | tf_op jit(solution)/shard_map/ppermute | solution.py:38
  100.5 30.5 %collective-permute-start.26 = (bf16[256,4096]{1,0:T(8,128)(2,1)}, bf16[256,4096]{1,0:T(8,128)(2,1)S(1)}, u32[]{:S(2)}, u32[]{:S(2)}) collective-permute-start(bf16[256,4096]{1,0:T(8,128)(2,1)} %collective-permute-done.11.refs_2_), channel_id=1, source_target_pairs={{0,2},{1,9},{2,4},{3,11},{4,6},{5,13},{6,0},{7,15},{8,10},{9,17},{... | collective-permute-start | bytes 6291464 | tf_op jit(solution)/shard_map/ppermute | solution.py:34
  100.5 30.7 %collective-permute-start.30 = (bf16[256,4096]{1,0:T(8,128)(2,1)S(1)}, bf16[256,4096]{1,0:T(8,128)(2,1)S(1)}, u32[]{:S(2)}, u32[]{:S(2)}) collective-permute-start(bf16[256,4096]{1,0:T(8,128)(2,1)S(1)} %collective-permute-done.22.refs_3_), channel_id=1, source_target_pairs={{0,6},{1,25},{2,0},{3,27},{4,2},{5,29},{6,4},{7,31},{8,14},{9,1},{... | collective-permute-start | bytes 6291464 | tf_op jit(solution)/shard_map/ppermute | solution.py:34
  112.1 8.0 %collective-permute-start.27 = (f32[2,32,512]{2,1,0:T(8,128)S(1)}, f32[2,32,512]{2,1,0:T(8,128)S(1)}, u32[]{:S(2)}, u32[]{:S(2)}) collective-permute-start(f32[2,32,512]{2,1,0:T(8,128)S(1)} %pad_maximum_fusion.1.refs_14_), channel_id=1, source_target_pairs={{0,64},{32,96},{64,0},{96,32},{1,65},{33,97},{65,1},{97,33},{2,66}... | collective-permute-start | bytes 393224 | tf_op jit(solution)/shard_map/ppermute | solution.py:42
  131.3 7.0 %collective-permute-start.31 = (bf16[256,4096]{1,0:T(8,128)(2,1)S(1)}, bf16[256,4096]{1,0:T(8,128)(2,1)S(1)}, u32[]{:S(2)}, u32[]{:S(2)}) collective-permute-start(bf16[256,4096]{1,0:T(8,128)(2,1)S(1)} %collective-permute-done.30.refs_6_.refs_4_), channel_id=1, source_target_pairs={{0,1},{1,0},{2,3},{3,2},{4,5},{5,4},{6,7},{7,6},{8,9},{9,8},{10,11... | collective-permute-start | bytes 6291464 | tf_op jit(solution)/shard_map/ppermute | solution.py:38
  142.8 6.1 %collective-permute-start.32 = (f32[32,512]{1,0:T(8,128)S(1)}, f32[32,512]{1,0:T(8,128)S(1)}, u32[]{:S(2)}, u32[]{:S(2)}) collective-permute-start(f32[32,512]{1,0:T(8,128)S(1)} %shard_map.100.refs_15_), channel_id=1, source_target_pairs={{0,64},{32,96},{64,0},{96,32},{1,65},{33,97},{65,1},{97,33},{2,66}... | collective-permute-start | bytes 196616 | tf_op jit(solution)/shard_map/ppermute | solution.py:46
  (29 other events, 132.4 us)

commit v3 on v0

v3 whole, which is shorter than its diff:
```python
import functools

import jax
import jax.numpy as jnp
import numpy as np
from jax import lax
from jax.experimental import pallas as pl
from jax.experimental.pallas import tpu as pltpu
from jax.sharding import PartitionSpec as P

F32, BF16 = jnp.float32, jnp.bfloat16
N, R, D, F, T = 4, 32, 4096, 512, 128
OFFSETS = (0, -1, 1, 2)
MIB = 1024 * 1024
WHOLE = pl.BlockSpec(memory_space=pltpu.VMEM)
SMEM = pl.BlockSpec(memory_space=pltpu.SMEM)
HBM = pl.BlockSpec(memory_space=pltpu.HBM)
NT = (((1,), (1,)), ((), ()))
TN = (((0,), (0,)), ((), ()))


def flat(x, y, c):
    return ((x % N) * N + y % N) * 2 + c


def along(x, y, c, first, d):
    return flat(x + d, y, c) if (c == 0) == first else flat(x, y + d, c)


PLANE = [(x, y, c) for x in range(N) for y in range(N) for c in range(2)]


def hop(array, first, d):
    pairs = [(flat(*p), along(*p, first, d)) for p in PLANE]
    return lax.ppermute(array, "tensor", pairs)


def swap(array):
    return lax.ppermute(array, "tensor", [(i, i ^ 1) for i in range(2 * N * N)])


def hop_z(array, bit):
    return lax.ppermute(array, "dp", [(i, i ^ bit) for i in range(N)])


def around_z(array, d):
    return lax.ppermute(array, "dp", [(i, (i + d) % N) for i in range(N)])


def twin(array, first, bit):
    pairs = []
    for x, y, c in PLANE:
        to = (x ^ bit, y, c) if (c == 0) == first else (x, y ^ bit, c)
        pairs.append((flat(x, y, c), flat(*to)))
    return lax.ppermute(array, "tensor", pairs)


def block_tables():
    offsets = np.zeros((2 * N * N, 2, N, N, 2), np.int32)
    moved = np.zeros((2 * N * N, N * N * 2), np.int32)
    for x, y, c in PLANE:
        at = y if c == 0 else x
        for i in range(N):
            for j, first in enumerate(OFFSETS):
                for kind, second in enumerate((OFFSETS[i], (at ^ i) - at)):
                    dx, dy = (first, second) if c == 0 else (second, first)
                    for m in range(2):
                        offsets[flat(x, y, c), kind, i, j, m] = flat(x + dx, y + dy, c ^ m) * T
    for x, y, c in PLANE:
        here = offsets[flat(x, y, c), 1].reshape(-1).tolist()
        there = offsets[flat(x, y, 1 - c), 1].reshape(-1).tolist()
        moved[flat(x, y, c)] = [here.index(row) for row in there]
    return np.concatenate([offsets.reshape(2 * N * N, -1), moved], 1)


def split(value, parts):
    pieces = []
    for _ in range(parts):
        piece = value.astype(BF16)
        pieces.append(piece)
        value = value - piece.astype(F32)
    return pieces


def dot(a, b, dims=(((1,), (0,)), ((), ()))):
    return lax.dot_general(a, b, dims, preferred_element_type=F32)


def dot_left(value, exact, dims):
    rows = value.shape[0]
    out = dot(jnp.concatenate(split(value, 3), 0), exact, dims)
    return out[:rows] + (out[rows : 2 * rows] + out[2 * rows :])


def dot_both(value, other, dims):
    rows = value.shape[0]
    a = jnp.concatenate(split(value, 3), 0)
    b1, b2, b3 = split(other, 3)
    p1, p2, p3 = dot(a, b1, dims), dot(a[: 2 * rows], b2, dims), dot(a[:rows], b3, dims)
    low = p1[2 * rows :] + p2[rows:] + p3
    return p1[:rows] + ((p1[rows : 2 * rows] + p2[:rows]) + low)


def shape(dims, dtype=F32):
    return jax.ShapeDtypeStruct(dims, dtype)


def run(kernel, out_shape, args, in_specs, out_specs, after=(), **kw):
    n, m = len(args), len(after)
    grid = kw.pop("grid", None)
    kw["cost_estimate"] = pl.CostEstimate(flops=1000, bytes_accessed=1000, transcendentals=0)
    prefetch = kw.pop("prefetch", 0)
    options = pltpu.CompilerParams(vmem_limit_bytes=kw.pop("vmem", 16) * MIB)
    any_spec = pl.BlockSpec(memory_space=pl.ANY)
    in_specs = list(in_specs) + [any_spec] * m

    def wrapped(*refs):
        kernel(*refs[:n], *refs[n + m :])

    if prefetch:
        kw["grid_spec"] = pltpu.PrefetchScalarGridSpec(
            num_scalar_prefetch=prefetch,
            grid=grid,
            in_specs=in_specs,
            out_specs=out_specs,
            scratch_shapes=kw.pop("scratch_shapes", ()),
        )
    else:
        kw.update(in_specs=in_specs, out_specs=out_specs)
        if grid is not None:
            kw["grid"] = grid
    return pl.pallas_call(wrapped, out_shape=out_shape, compiler_params=options, **kw)(*args, *after)


def add3(r):
    return r[:R] + (r[R : 2 * R] + r[2 * R :])


H = D // 2
B = 2 * N * N


def tokens_kernel(off_ref, q_ref, g_ref, keep_ref, send_ref, other_ref, h_ref):
    q = jnp.concatenate(split(q_ref[...], 3), 0)
    for k in range(N * 2):
        rows = [g_ref[pl.ds(pl.multiple_of(off_ref[B + k * N + j], T), T), :] for j in range(N)]
        r = add3(dot(q, jnp.concatenate(rows, 0), NT))
        for j in range(N):
            h_ref[k * N + j] = r[:, j * T : (j + 1) * T]
    for i in range(N):
        out = (keep_ref if i < 2 else send_ref).at[i % 2]
        for k in range(2 * N):
            out[:, k * T : (k + 1) * T] = h_ref[i * 2 * N + k]
            other_ref[i, :, k * T : (k + 1) * T] = h_ref[off_ref[2 * B + i * 2 * N + k]]


def tokens(off, q, g, after):
    w = 2 * N * T
    return run(
        tokens_kernel,
        [shape((2, R, w)), shape((2, R, w)), shape((N, R, w))],
        (off, q, g),
        [SMEM, WHOLE, WHOLE],
        [WHOLE] * 3,
        after,
        scratch_shapes=[pltpu.VMEM((B, R, T), F32)],
    )


def fetches(e_ref, half, buf_ref, sems, parts=range(N)):
    n = H // N
    return [
        pltpu.make_async_copy(
            e_ref.at[pl.ds(pl.multiple_of(half * H + k * n, n), n), :], buf_ref.at[pl.ds(k * n, n), :], sems.at[k]
        )
        for k in parts
    ]


FETCH = [pltpu.VMEM((H, F), F32), pltpu.SemaphoreType.DMA((N,))]


def errors_kernel(other, pos_ref, q_ref, e_ref, out_ref, buf_ref, sems):
    copies = fetches(e_ref, pos_ref[0] ^ other, buf_ref, sems)
    for copy in copies:
        copy.start()
    q = jnp.concatenate(split(q_ref[...], 3), 0)
    n = H // N
    for k in range(N):
        copies[k].wait()
        e1, e2 = split(buf_ref[k * n : (k + 1) * n, :], 2)
        r, s = dot(q, e1, NT), dot(q[: 2 * R], e2, NT)
        out_ref[k] = r[:R] + ((r[R : 2 * R] + s[:R]) + (r[2 * R :] + s[R:]))


def errors(pos, q, e, other, after):
    return run(
        functools.partial(errors_kernel, other),
        shape((N, R, D // 8)),
        (pos, q, e),
        [SMEM, WHOLE, HBM],
        WHOLE,
        after,
        scratch_shapes=FETCH,
    )


def add_kernel(n, *refs):
    for i in range(n):
        refs[2 * n + i][...] = refs[i][...] + refs[n + i][...]


def add(a, b, after=()):
    n = len(a)
    return run(
        functools.partial(add_kernel, n),
        [shape(v.shape) for v in a],
        (*a, *b),
        [WHOLE] * (2 * n),
        [WHOLE] * n,
        after,
    )


def add_halves_kernel(a_ref, b_ref, got_ref, keep_ref, send_ref):
    keep_ref[...] = a_ref[...] + got_ref[:2]
    send_ref[...] = b_ref[...] + got_ref[2:]


def add_halves(a, b, got, after=()):
    return run(
        add_halves_kernel,
        [shape(a.shape)] * 2,
        (a, b, got),
        [WHOLE] * 3,
        [WHOLE] * 2,
        after,
    )


def add_pair_kernel(a_ref, got_ref, keep_ref, send_ref):
    keep_ref[...] = a_ref[0] + got_ref[0]
    send_ref[...] = a_ref[1] + got_ref[1]


def add_pair(a, got, after=()):
    return run(
        add_pair_kernel,
        [shape(a.shape[1:])] * 2,
        (a, got),
        [WHOLE] * 2,
        [WHOLE] * 2,
        after,
    )


def cut_kernel(pos_ref, x_ref, mine_ref, send_ref):
    at = pl.multiple_of(pos_ref[0] * H, H)
    mine_ref[...] = x_ref[:, pl.ds(at, H)]
    send_ref[...] = x_ref[:, pl.ds(H - at, H)]


def cut(pos, x):
    return run(cut_kernel, [shape((T, H), BF16)] * 2, (pos, x), [SMEM, WHOLE], [WHOLE] * 2)


def halves_kernel(a, b, top, bottom):
    top[...] = a[:T, :]
    bottom[...] = b[T:, :]


def stack_kernel(*refs):
    *parts, out = refs
    at = 0
    for part in parts:
        out[at : at + part.shape[0], :] = part[...]
        at += part.shape[0]


def pack(kernel, args, rows, after):
    return run(kernel, [shape((r, H), BF16) for r in rows], args, [WHOLE] * len(args), [WHOLE] * len(rows), after)


def held_kernel(in_ref, out_ref):
    out_ref[...] = in_ref[...]


def held(array, after):
    return run(held_kernel, pltpu.VMEM(array.shape, array.dtype), (array,), [WHOLE], WHOLE, after)


def sketch_kernel(pos_ref, h0, h1, e0_ref, e1_ref, x0_ref, x1_ref, keep_ref, send_ref):
    z = pos_ref[1]
    h = jnp.concatenate(split(h0[...] + h1[...], 3), 0)
    n = D // 8
    for i in range(N):
        part = z ^ i
        columns = pl.ds(pl.multiple_of(part * n, n), n)
        x = jnp.concatenate([x0_ref[:, columns], x1_ref[:, columns]], 0)
        (keep_ref if i < 2 else send_ref)[i % 2] = add3(dot(h, x)) + (e0_ref[part] + e1_ref[part])


def sketch_part(pos, h, e, xs, after):
    return run(
        sketch_kernel,
        [shape((2, R, D // 8))] * 2,
        (pos, *h, *e, *xs),
        [SMEM] + [WHOLE] * 6,
        [WHOLE] * 2,
        after,
    )


def basis_kernel(pos_ref, mine_ref, other_ref, out_ref, s_ref):
    c, z = pos_ref[0], pos_ref[1]
    n = D // 8
    for half, ref in ((1 - c, mine_ref), (c, other_ref)):
        for i in range(N):
            chunk = half * N + (z ^ i)
            s_ref[:, pl.ds(pl.multiple_of(chunk * n, n), n)] = ref[i] * 0.25
    s = s_ref[...]
    gram = dot_both(s, s, NT)
    row = lax.broadcasted_iota(jnp.int32, (R, 2 * R), 0)
    col = lax.broadcasted_iota(jnp.int32, (R, 2 * R), 1)
    work = jnp.concatenate([gram, jnp.zeros((R, R), F32)], 1) + jnp.where(col == row + R, 1.0, 0.0)
    for j in range(R - 1):
        column = jnp.broadcast_to(work[:, j : j + 1], (R, 2 * R))
        line = work[j : j + 1, :] / column[j : j + 1, :]
        work = work - jnp.where(row > j, column, 0.0) * line
    pivot = jnp.sum(jnp.where(row == col, work, 0.0), 1, keepdims=True)
    done = work / jnp.sqrt(pivot)
    out_ref[...] = dot_both(done[:, R:], s, (((1,), (0,)), ((), ())))


def basis(pos, mine, other, after):
    return run(
        basis_kernel,
        pltpu.VMEM((R, D), F32),
        (pos, mine, other),
        [SMEM, WHOLE, WHOLE],
        WHOLE,
        after,
        scratch_shapes=[pltpu.VMEM((R, D), F32)],
    )


def block_rows(off_ref, g_ref, starts):
    rows = [pl.ds(pl.multiple_of(off_ref[start + k], T), T) for start in starts for k in range(4)]
    return jnp.concatenate([g_ref[at, :] for at in rows], 0)


def merge_kernel(starts, lo, hi, has_errors, has_acc, off_ref, pos_ref, g_ref, go_ref, *refs):
    n, step = len(starts), H // N
    xs, refs = refs[:n], list(refs[n:])
    e_ref = refs.pop(0) if has_errors else None
    own_in, other_in = (refs.pop(0), refs.pop(0)) if has_acc else (None, None)
    own_ref, other_ref = refs[:2]
    if has_errors:
        copies = fetches(e_ref, pos_ref[0], refs[2], refs[3], range(lo // step, hi // step))
        for copy in copies:
            copy.start()
    rows = jnp.concatenate([block_rows(off_ref, g_ref, starts), block_rows(off_ref, go_ref, starts)], 1)
    for k in range((hi - lo) // step):
        at = slice(lo + k * step, lo + (k + 1) * step)
        product = dot(jnp.concatenate([r[:, at] for r in xs], 0), rows, TN)
        if has_errors:
            copies[k].wait()
            own_ref[at, :] = refs[2][at, :] + product[:, :F]
            other_ref[at, :] = product[:, F:]
        else:
            own_ref[at, :] = own_in[at, :] + product[:, :F]
            other_ref[at, :] = other_in[at, :] + product[:, F:]


def merge(off, pos, g, g_other, groups, lo, hi, errors=None, acc=None, after=()):
    starts, xs = [start for start, _ in groups], [x for _, x in groups]
    args = [off, pos, g, g_other, *xs] + ([] if errors is None else [errors]) + ([] if acc is None else [*acc])
    specs = [SMEM] * 2 + [WHOLE] * (2 + len(xs)) + ([] if errors is None else [HBM]) + [WHOLE] * (2 if acc else 0)
    return run(
        functools.partial(merge_kernel, starts, lo, hi, errors is not None, acc is not None),
        [pltpu.VMEM((H, F), F32)] * 2,
        args,
        specs,
        [WHOLE] * 2,
        after,
        scratch_shapes=() if errors is None else FETCH,
        input_output_aliases={} if acc is None else {len(args) - 2: 0, len(args) - 1: 1},
    )


def last_other_kernel(starts, off_ref, acc_ref, g_ref, *refs):
    *xs, out_ref = refs
    rows, step = block_rows(off_ref, g_ref, starts), H // N
    for k in range(N):
        at = slice(k * step, (k + 1) * step)
        out_ref[at, :] = acc_ref[at, :] + dot(jnp.concatenate([r[:, at] for r in xs], 0), rows, TN)


def last_other(off, acc, groups, g, after):
    return run(
        functools.partial(last_other_kernel, [start for start, _ in groups]),
        pltpu.VMEM((H, F), F32),
        (off, acc, g, *[x for _, x in groups]),
        [SMEM] + [WHOLE] * (2 + len(groups)),
        WHOLE,
        after,
    )


def p_times(p, m):
    t1, t2 = split(m, 2)
    a, b = dot(p, t1), dot(p[: 2 * R], t2)
    return a[:R] + ((a[R : 2 * R] + b[:R]) + (a[2 * R :] + b[R:]))


def right_kernel(pos_ref, p_ref, own_ref, other_ref, e_ref, q_ref, send_ref, buf_ref, sems):
    copies = fetches(e_ref, 1 - pos_ref[0], buf_ref, sems)
    for copy in copies:
        copy.start()
    n = H // N
    q, send = jnp.zeros((R, F), F32), jnp.zeros((R, F), F32)
    for k in range(N):
        at = pl.ds(pl.multiple_of(pos_ref[0] * H + k * n, n), n)
        p = jnp.concatenate(split(p_ref[:, at], 3), 0)
        q += p_times(p, own_ref[k * n : (k + 1) * n, :])
        send += p_times(p, other_ref[k * n : (k + 1) * n, :])
    for k in range(N):
        at = pl.ds(pl.multiple_of((1 - pos_ref[0]) * H + k * n, n), n)
        p = jnp.concatenate(split(p_ref[:, at], 3), 0)
        copies[k].wait()
        q += p_times(p, buf_ref[k * n : (k + 1) * n, :])
    q_ref[...] = q
    send_ref[...] = send


def right_part(pos, p, acc, e, after):
    return run(
        right_kernel,
        [shape((R, F))] * 2,
        (pos, p, *acc, e),
        [SMEM] + [WHOLE] * 3 + [HBM],
        [WHOLE] * 2,
        after,
        scratch_shapes=FETCH,
    )


def right_rest_kernel(starts, off_ref, pos_ref, p_ref, q_ref, send_ref, g_ref, go_ref, *refs):
    n = len(starts)
    xs, (out_ref, out_send_ref) = refs[:n], refs[n:]
    here = pl.ds(pl.multiple_of(pos_ref[0] * H, H), H)
    p = jnp.concatenate(split(p_ref[:, here], 3), 0)
    total, send = q_ref[...], send_ref[...]
    for start, x in zip(starts, xs):
        y = dot(x[...], p, NT)
        y = jnp.concatenate(split(y[:, :R] + (y[:, R : 2 * R] + y[:, 2 * R :]), 3), 1)
        rows = [pl.ds(pl.multiple_of(off_ref[start + k], T), T) for k in range(4)]
        total += add3(dot(y, jnp.concatenate([g_ref[at, :] for at in rows], 0), TN))
        send += add3(dot(y, jnp.concatenate([go_ref[at, :] for at in rows], 0), TN))
    out_ref[...] = total
    out_send_ref[...] = send


def right_rest(off, pos, p, q, send, g, g_other, groups):
    return run(
        functools.partial(right_rest_kernel, [start for start, _ in groups]),
        [shape((R, F))] * 2,
        (off, pos, p, q, send, g, g_other, *[x for _, x in groups]),
        [SMEM] * 2 + [WHOLE] * (5 + len(groups)),
        [WHOLE] * 2,
        vmem=24,
    )


def final_kernel(n, rows, starts, pos_ref, off_ref, m_ref, e_ref, got_ref, g_ref, *refs):
    xs, (p_ref, q0, q1, q2, q3, out_ref, q_ref, right_ref, buf_ref, sems) = refs[:n], refs[n:]
    copies = fetches(e_ref, 1 - pos_ref[0], buf_ref, sems)
    i, steps = pl.program_id(0), H // rows
    k = n * 4 * T

    @pl.when(i == 0)
    def _():
        for copy in copies:
            copy.start()
        q = ((q0[...] + q1[...]) + (q2[...] + q3[...])) * 0.25
        q_ref[...] = q
        s1, s2 = split(-q, 2)
        for j, start in enumerate(starts):
            for b in range(4):
                at = pl.ds(pl.multiple_of(off_ref[start + b], T), T)
                right_ref[(4 * j + b) * T : (4 * j + b + 1) * T, :] = g_ref[at, :]
        right_ref[k:, :] = jnp.concatenate([s1, s2, s1], 0)

    half = jnp.where(i < steps, pos_ref[0], 1 - pos_ref[0])
    step = lax.rem(i, steps)
    p1, p2 = split(p_ref[:, pl.ds(pl.multiple_of(half * H + step * rows, rows), rows)], 2)
    p = jnp.concatenate([p1, p1, p2], 0)
    at = pl.ds(pl.multiple_of(step * rows, rows), rows)

    @pl.when(i < steps)
    def _():
        left = jnp.concatenate([r[:, at] for r in xs] + [p], 0)
        out_ref[...] = m_ref[at, :] + dot(left, right_ref[...], TN)

    for j, copy in enumerate(copies):
        pl.when(i == steps + j * steps // N)(copy.wait)

    @pl.when(i >= steps)
    def _():
        out_ref[...] = (buf_ref[at, :] + got_ref[at, :]) + dot(p, right_ref[k:, :], TN)


def final(off, pos, own, e, got, groups, g, p, q, rows=H // 2):
    n, steps = len(groups), H // rows
    half = lambda i, pos: jnp.where(i < steps, pos[0], 1 - pos[0])
    return run(
        functools.partial(final_kernel, n, rows, [start for start, _ in groups]),
        [shape((D, F)), shape((R, F))],
        [pos, off, own, e, got, g] + [x for _, x in groups] + [p, *q],
        [
            SMEM,
            WHOLE,
            HBM,
        ]
        + [WHOLE] * (n + 3 + N),
        [
            pl.BlockSpec((rows, F), lambda i, pos: (half(i, pos) * steps + lax.rem(i, steps), 0)),
            pl.BlockSpec((R, F), lambda i, pos: (0, 0)),
        ],
        prefetch=1,
        grid=(2 * steps,),
        vmem=24,
        scratch_shapes=[pltpu.VMEM((n * 4 * T + 3 * R, F), BF16)] + FETCH,
    )


def later(array, behind):
    return lax.optimization_barrier((array, behind))[0]


def body(x, g, e, q_init):
    me = lax.axis_index("tensor")
    pos = jnp.stack([me % 2, lax.axis_index("dp")]).astype(jnp.int32)
    off = lax.dynamic_index_in_dim(jnp.asarray(block_tables()), me, 0, keepdims=False)
    e, q = pltpu.with_memory_space_constraint(e[0], pltpu.HBM), q_init.T

    mine, send = cut(pos, x)
    (x0,) = pack(stack_kernel, (mine, swap(send)), (2 * T,), ())
    a, b = hop(x0, True, 1), hop(x0, True, -1)
    g_other = swap(later(g, x0))
    keep, send, other = tokens(off, q, g, (x0,))
    got = swap(other)
    keep, send = add_halves(keep, send, got, ())
    got = twin(send, False, 2)
    e_other = errors(pos, q, e, 1, (send,))
    g_other = held(g_other, (e_other,))
    h, send = add_pair(keep, got, (g_other,))
    h_got = twin(send, False, 1)
    top, bottom = pack(halves_kernel, (a, b), (T, T), (send,))
    c, d = hop(top, True, 1), hop(bottom, True, -1)
    e_got = swap(later(e_other, top))
    e_own = errors(pos, q, e, 0, (top,))

    (g0,) = pack(stack_kernel, (x0, a), (4 * T,), (h_got, e_own))
    l0, r0 = hop(g0, False, 1), hop(g0, False, -1)
    (g1,) = pack(stack_kernel, (b, c, d), (4 * T,), (g0,))
    l1, r1 = hop(g1, False, 1), hop(g1, False, -1)

    keep, send = sketch_part(pos, (h, h_got), (e_own, e_got), (g0, g1), ())
    got = hop_z(send, 2)
    near = [(0, g0), (4, g1)]
    acc = merge(off, pos, g, g_other, near, 0, H // 2, e, None, (send,))
    keep, send = add_pair(keep, got, (acc[0],))
    got = hop_z(send, 1)
    acc = merge(off, pos, g, g_other, near, H // 2, H, e, acc, (send,))
    (s,) = add([keep], [got], (acc[0],))
    got = twin(s, True, 1)
    (s,) = add([s], [got], ())
    got = twin(s, True, 2)
    l0, r0 = later(l0, s), later(r0, s)
    o0 = hop(l0, False, 1)
    mid = [(8, l0), (16, r0)]
    acc = merge(off, pos, g, g_other, mid, 0, H // 2, None, acc, (s,))
    (s,) = add([s], [got], (acc[0],))
    s = swap(s)
    got = twin(s, True, 1)
    acc = merge(off, pos, g, g_other, mid, H // 2, H, None, acc, (s,))
    (s,) = add([s], [got], (acc[0],))
    got = twin(s, True, 2)
    (s,) = add([s], [got], ())
    got = hop_z(s, 1)
    l1, r1 = later(l1, s), later(r1, s)
    o1 = hop(r1, False, -1)
    far = [(12, l1), (20, r1)]
    acc = merge(off, pos, g, g_other, far, 0, H // 2, None, acc, (s,))
    pair = jnp.stack([later(s, acc[0]), got])
    got = hop_z(pair, 2)
    acc = merge(off, pos, g, g_other, far, H // 2, H, None, acc, (pair,))
    stack = jnp.concatenate([later(pair, acc[0]), got])
    p = basis(pos, stack, swap(stack), (acc[0],))

    last = [(24, later(o0, p)), (28, later(o1, p))]
    qp, q_send = right_part(pos, p, acc, e, ())
    qp, q_send = right_rest(off, pos, p, qp, q_send, g, g_other, last)
    q_got = swap(q_send)
    out = last_other(off, acc[1], last, g_other, (q_send,))
    (qp,) = add([qp], [q_got], (out,))
    out = swap(later(out, qp))
    qs = (qp, around_z(qp, 2), around_z(qp, 1), around_z(qp, -1))
    err, qf = final(off, pos, acc[0], e, out, last, g, p, qs)
    return err[None], p.T, qf.T


def solution(mesh):
    in_specs = (
        P(("dp", "tensor"), None),
        P("dp", "tensor"),
        P("dp", None, "tensor"),
        P("tensor", None),
    )
    out_specs = (P("dp", None, "tensor"), P(), P("tensor", None))
    return jax.shard_map(body, mesh=mesh, in_specs=in_specs, out_specs=out_specs, check_vma=False)
```

time: 387 us -> 139 us (0.36)
  waiting for transfers between devices: 304 us -> 26.7 us
  matrix products: 61.7 us -> 0 us
  Pallas kernels: 0 us -> 58.8 us
  starting transfers between devices: 0.3 us -> 45.9 us
  between operations: 13.8 us -> 1.15 us
  other arithmetic: 7.53 us -> 0.09 us
  local copies, waits for them, and re-layouts: 0.09 us -> 5.77 us
    psum x2 -> x0, waiting for transfers between devices: 184 us -> none  [the longest x1 144 us: body(): lax.psum(jnp.dot(merged, q_init, precision=highest), ('dp', 'tensor'))]
    all_gather x1 -> x0, waiting for transfers between devices: 118 us -> none  [body(): lax.all_gather(x_rows, 'tensor', axis=0, tiled=True)]
    dot_general x5 -> x0, matrix products: 60 us -> none  [the longest x1 28 us: body(): lax.dot_general(lax.all_gather(x_rows, 'tensor', axis=0, tiled=True), gra...]
    pallas_call x0 -> x30, Pallas kernels: none -> 58.8 us  [run(): pl.pallas_call(wrapped, out_shape=out_shape, compiler_params=options, **kw)]
    ppermute x0 -> x31, starting transfers between devices: none -> 45.9 us  [the longest x10 13.3 us: hop(): return lax.ppermute(array, 'tensor', pairs)]
    ppermute x0 -> x31, waiting for transfers between devices: none -> 26.7 us  [the longest x6 10.8 us: twin(): return lax.ppermute(array, 'tensor', pairs)]
    another operation x5 -> x2, other arithmetic: 6.68 us -> 0.09 us  [the longest x1 0.08 us: body(): pos = jnp.stack([me % 2, lax.axis_index('dp')]).astype(jnp.int32)]
    unnamed x6 -> x12, local copies, waits for them, and re-layouts: 0.02 us -> 5.06 us
  transfers between devices with their start and end apart: 3 -> 31, of which waited for: 3 -> 15; matrix products, arithmetic and copies ran while one was open for 0% -> 1% of each run, Pallas kernels for 0% -> 34%
where the time goes in v3:
time: 139 us; the launch traced here: 138 us
  Pallas kernels  58.8 us (42%)
  starting transfers between devices  45.9 us (33%)
  waiting for transfers between devices  26.7 us (19%)
  local copies, waits for them, and re-layouts  5.77 us (4%)
    pallas_call x30, Pallas kernels, run(): pl.pallas_call(wrapped, out_shape=out_shape, compiler_params=options, **kw)  58.8 us
    ppermute x10, starting transfers between devices, hop(): return lax.ppermute(array, 'tensor', pairs)  13.3 us
    ppermute x6, starting transfers between devices, twin(): return lax.ppermute(array, 'tensor', pairs)  12.6 us
    ppermute x4, starting transfers between devices, hop_z(): return lax.ppermute(array, 'dp', [(i, i ^ bit) for i in range(N)])  11.1 us
    ppermute x6, waiting for transfers between devices, twin(): return lax.ppermute(array, 'tensor', pairs)  10.8 us
    ppermute x8, waiting for transfers between devices, swap(): return lax.ppermute(array, 'tensor', [(i, i ^ 1) for i in range(2 * N * N)])  7.76 us
    ppermute x3, starting transfers between devices, around_z(): return lax.ppermute(array, 'dp', [(i, (i + d) % N) for i in range(N)])  7.12 us
    ppermute x10, waiting for transfers between devices, hop(): return lax.ppermute(array, 'tensor', pairs)  6.73 us
  transfers between devices with their start and end apart: 31, of which 15 were waited for; matrix products, arithmetic and copies ran while one was open for 1% of the time, Pallas kernels for 34%

profile of v3, /device:TPU:0, one launch (start us, length us, event | category | flops | bytes accessed | tf_op | source)
XLA Modules:
  0.0 138.5 jit_solution(17978821331851403554)
XLA Ops:
  15.4 3.3 %collective-permute-start.5 = (f32[2,32,1024]{2,1,0:T(8,128)S(1)}, f32[2,32,1024]{2,1,0:T(8,128)S(1)}, u32[]{:S(2)}, u32[]{:S(2)}) collective-permute-start(f32[2,32,1024]{2,1,0:T(8,128)S(1)} %get-tuple-element.53.refs_3_), channel_id=1, source_target_pairs={{0,4},{1,17},{2,6},{3,19},{4,0},{5,21},{6,2},{7,23},{8,12},{9,25},... | collective-permute-start | bytes 786440 | tf_op jit(solution)/shard_map/ppermute | solution.py:55
  18.7 3.6 %shard_map.80.refs_1_ = f32[4,32,512]{2,1,0:T(8,128)S(1)} custom-call(s32[2]{0:T(128)S(1)} %pad_add_fusion.refs_0_.refs_1_, f32[32,512]{1,0:T(8,128)S(1)} %bitcast.13, f32[4096,512]{1,0:T(8,128)} %bitcast.16, f32[2,32,1024]{2,1,0:T(8,128)S(1)} %get-tuple-element.53.refs_3_), custom_call_target="tpu_custom_call" | custom-call | flops 1000 | bytes 1000 | tf_op jit(solution)/shard_map/pallas_call | solution.py:132
  26.7 3.2 %collective-permute-start.7 = (bf16[128,2048]{1,0:T(8,128)(2,1)S(1)}, bf16[128,2048]{1,0:T(8,128)(2,1)S(1)}, u32[]{:S(2)}, u32[]{:S(2)}) collective-permute-start(bf16[128,2048]{1,0:T(8,128)(2,1)S(1)} %get-tuple-element.57), channel_id=1, source_target_pairs={{0,24},{1,7},{2,26},{3,1},{4,28},{5,3},{6,30},{7,5},{8,0},{9,15},{... | collective-permute-start | bytes 1572872 | tf_op jit(solution)/shard_map/ppermute | solution.py:35
  31.5 3.6 %shard_map.84.refs_3_ = f32[4,32,512]{2,1,0:T(8,128)S(1)} custom-call(s32[2]{0:T(128)S(1)} %pad_add_fusion.refs_0_.refs_1_, f32[32,512]{1,0:T(8,128)S(1)} %bitcast.14, f32[4096,512]{1,0:T(8,128)} %bitcast.17, bf16[128,2048]{1,0:T(8,128)(2,1)S(1)} %get-tuple-element.56.refs_3_), custom_call_target="tpu_custom_call" | custom-call | flops 1000 | bytes 1000 | tf_op jit(solution)/shard_map/pallas_call | solution.py:132
  38.7 3.3 %collective-permute-start.20 = (bf16[512,2048]{1,0:T(8,128)(2,1)S(1)}, bf16[512,2048]{1,0:T(8,128)(2,1)S(1)}, u32[]{:S(2)}, u32[]{:S(2)}) collective-permute-start(bf16[512,2048]{1,0:T(8,128)(2,1)S(1)} %shard_map.86.refs_6_.refs_5_), channel_id=1, source_target_pairs={{0,6},{1,25},{2,0},{3,27},{4,2},{5,29},{6,4},{7,31},{8,14},{9,1},{... | collective-permute-start | bytes 6291464 | tf_op jit(solution)/shard_map/ppermute | solution.py:35
  44.9 3.9 %collective-permute-start.11 = (f32[2,32,512]{2,1,0:T(8,128)S(1)}, f32[2,32,512]{2,1,0:T(8,128)S(1)}, u32[]{:S(2)}, u32[]{:S(2)}) collective-permute-start(f32[2,32,512]{2,1,0:T(8,128)S(1)} %get-tuple-element.61.refs_7_), channel_id=1, source_target_pairs={{0,64},{32,96},{64,0},{96,32},{1,65},{33,97},{65,1},{97,33},{2,66}... | collective-permute-start | bytes 393224 | tf_op jit(solution)/shard_map/ppermute | solution.py:43
  48.8 3.8 %shard_map.88 = (f32[2048,512]{1,0:T(8,128)S(1)}, f32[2048,512]{1,0:T(8,128)S(1)}) custom-call(s32[96]{0:T(128)S(1)} %dynamic-slice_bitcast_fusion.refs_0_.refs_1_, s32[2]{0:T(128)S(1)} %pad_add_fusion.refs_0_.refs_1_, bf16[4096,512]{1,0:T(8,128)(2,1)S(1)} %copy-done.1, bf16[4096,512]{1,0:T(8,128)(2,1)S(1)} %shard_map.81.refs_2_.refs_3_.refs_6_, ...), custom_call_target="tpu_custom_call" | custom-call | flops 1000 | bytes 1000 | tf_op jit(solution)/shard_map/pallas_call | solution.py:132
  54.1 3.9 %shard_map.90 = (f32[2048,512]{1,0:T(8,128)S(1)}, f32[2048,512]{1,0:T(8,128)S(1)}) custom-call(s32[96]{0:T(128)S(1)} %dynamic-slice_bitcast_fusion.refs_0_.refs_1_, s32[2]{0:T(128)S(1)} %pad_add_fusion.refs_0_.refs_1_, bf16[4096,512]{1,0:T(8,128)(2,1)S(1)} %copy-done.1, ...), custom_call_target="tpu_custom_call", output_to_operand_aliasing={{0}: (7, {}), {1}: (8, {})} | custom-call | flops 1000 | bytes 1000 | tf_op jit(solution)/shard_map/pallas_call | solution.py:132
  58.3 4.9 %collective-permute-done.13.refs_1_ = f32[32,512]{1,0:T(8,128)S(1)} collective-permute-done((f32[32,512]{1,0:T(8,128)S(1)}, f32[32,512]{1,0:T(8,128)S(1)}, u32[]{:S(2)}, u32[]{:S(2)}) %collective-permute-start.13) | collective-permute-done | bytes 65568 | tf_op jit(solution)/shard_map/ppermute | solution.py:55
  63.2 3.2 %collective-permute-start.14 = (f32[32,512]{1,0:T(8,128)S(1)}, f32[32,512]{1,0:T(8,128)S(1)}, u32[]{:S(2)}, u32[]{:S(2)}) collective-permute-start(f32[32,512]{1,0:T(8,128)S(1)} %shard_map.92.refs_8_.refs_0_), channel_id=1, source_target_pairs={{0,16},{1,5},{2,18},{3,7},{4,20},{5,1},{6,22},{7,3},{8,24},{9,13},... | collective-permute-start | bytes 196616 | tf_op jit(solution)/shard_map/ppermute | solution.py:55
  66.4 3.1 %shard_map.93 = (f32[2048,512]{1,0:T(8,128)S(1)}, f32[2048,512]{1,0:T(8,128)S(1)}) custom-call(s32[96]{0:T(128)S(1)} %dynamic-slice_bitcast_fusion.refs_0_.refs_1_, s32[2]{0:T(128)S(1)} %pad_add_fusion.refs_0_.refs_1_, bf16[4096,512]{1,0:T(8,128)(2,1)S(1)} %copy-done.1, ...), custom_call_target="tpu_custom_call", output_to_operand_aliasing={{0}: (6, {}), {1}: (7, {})} | custom-call | flops 1000 | bytes 1000 | tf_op jit(solution)/shard_map/pallas_call | solution.py:132
  72.3 3.1 %shard_map.95 = (f32[2048,512]{1,0:T(8,128)S(1)}, f32[2048,512]{1,0:T(8,128)S(1)}) custom-call(s32[96]{0:T(128)S(1)} %dynamic-slice_bitcast_fusion.refs_0_.refs_1_, s32[2]{0:T(128)S(1)} %pad_add_fusion.refs_0_.refs_1_, bf16[4096,512]{1,0:T(8,128)(2,1)S(1)} %copy-done.1, ...), custom_call_target="tpu_custom_call", output_to_operand_aliasing={{0}: (6, {}), {1}: (7, {})} | custom-call | flops 1000 | bytes 1000 | tf_op jit(solution)/shard_map/pallas_call | solution.py:132
  76.2 3.3 %collective-permute-start.19 = (f32[32,512]{1,0:T(8,128)S(1)}, f32[32,512]{1,0:T(8,128)S(1)}, u32[]{:S(2)}, u32[]{:S(2)}) collective-permute-start(f32[32,512]{1,0:T(8,128)S(1)} %shard_map.96.refs_0_), channel_id=1, source_target_pairs={{0,16},{1,5},{2,18},{3,7},{4,20},{5,1},{6,22},{7,3},{8,24},{9,13},... | collective-permute-start | bytes 196616 | tf_op jit(solution)/shard_map/ppermute | solution.py:55
  79.5 3.3 %collective-permute-done.19.refs_1_ = f32[32,512]{1,0:T(8,128)S(1)} collective-permute-done((f32[32,512]{1,0:T(8,128)S(1)}, f32[32,512]{1,0:T(8,128)S(1)}, u32[]{:S(2)}, u32[]{:S(2)}) %collective-permute-start.19) | collective-permute-done | bytes 65568 | tf_op jit(solution)/shard_map/ppermute | solution.py:55
  82.9 5.0 %collective-permute-done.20.refs_5_ = bf16[512,2048]{1,0:T(8,128)(2,1)S(1)} collective-permute-done((bf16[512,2048]{1,0:T(8,128)(2,1)S(1)}, bf16[512,2048]{1,0:T(8,128)(2,1)S(1)}, u32[]{:S(2)}, u32[]{:S(2)}) %collective-permute-start.20) | collective-permute-done | bytes 2097184 | tf_op jit(solution)/shard_map/ppermute | solution.py:35
  91.6 3.1 %shard_map.98 = (f32[2048,512]{1,0:T(8,128)S(1)}, f32[2048,512]{1,0:T(8,128)S(1)}) custom-call(s32[96]{0:T(128)S(1)} %dynamic-slice_bitcast_fusion.refs_0_.refs_1_, s32[2]{0:T(128)S(1)} %pad_add_fusion.refs_0_.refs_1_, bf16[4096,512]{1,0:T(8,128)(2,1)S(1)} %copy-done.1, ...), custom_call_target="tpu_custom_call", output_to_operand_aliasing={{0}: (6, {}), {1}: (7, {})} | custom-call | flops 1000 | bytes 1000 | tf_op jit(solution)/shard_map/pallas_call | solution.py:132
  94.7 3.8 %collective-permute-start.23 = (f32[2,32,512]{2,1,0:T(8,128)S(1)}, f32[2,32,512]{2,1,0:T(8,128)S(1)}, u32[]{:S(2)}, u32[]{:S(2)}) collective-permute-start(f32[2,32,512]{2,1,0:T(8,128)S(1)} %pad_maximum_fusion.refs_8_), channel_id=1, source_target_pairs={{0,64},{32,96},{64,0},{96,32},{1,65},{33,97},{65,1},{97,33},{2,66}... | collective-permute-start | bytes 393224 | tf_op jit(solution)/shard_map/ppermute | solution.py:43
  98.5 3.1 %shard_map.99 = (f32[2048,512]{1,0:T(8,128)S(1)}, f32[2048,512]{1,0:T(8,128)S(1)}) custom-call(s32[96]{0:T(128)S(1)} %dynamic-slice_bitcast_fusion.refs_0_.refs_1_, s32[2]{0:T(128)S(1)} %pad_add_fusion.refs_0_.refs_1_, bf16[4096,512]{1,0:T(8,128)(2,1)S(1)} %copy-done.1, ...), custom_call_target="tpu_custom_call", output_to_operand_aliasing={{0}: (6, {}), {1}: (7, {})} | custom-call | flops 1000 | bytes 1000 | tf_op jit(solution)/shard_map/pallas_call | solution.py:132
  103.5 5.3 %shard_map.100.refs_1_.refs_2_.refs_8_ = f32[32,4096]{1,0:T(8,128)S(1)} custom-call(s32[2]{0:T(128)S(1)} %pad_add_fusion.refs_0_.refs_1_, f32[4,32,512]{2,1,0:T(8,128)S(1)} %constant_dynamic-update-slice_fusion.refs_1_, f32[4,32,512]{2,1,0:T(8,128)S(1)} %collective-permute-done.24.refs_2_, f32[2048,512]{1,0:T(8,128)S(1)} %get-tuple-element.79.refs_3_.refs_2_), custom_call_target="tpu_custom_call" | custom-call | flops 1000 | bytes 1000 | tf_op jit(solution)/shard_map/pallas_call | solution.py:132
  108.8 4.8 %shard_map.101 = (f32[32,512]{1,0:T(8,128)S(1)}, f32[32,512]{1,0:T(8,128)S(1)}) custom-call(s32[2]{0:T(128)S(1)} %pad_add_fusion.refs_0_.refs_1_, f32[32,4096]{1,0:T(8,128)S(1)} %shard_map.100.refs_1_.refs_2_.refs_8_, f32[2048,512]{1,0:T(8,128)S(1)} %get-tuple-element.79.refs_3_.refs_2_, f32[2048,512]{1,0:T(8,128)S(1)} %get-tuple-element.80.refs_3_.refs_1_, ...), custom_call_target="tpu_custom_call" | custom-call | flops 1000 | bytes 1000 | tf_op jit(solution)/shard_map/pallas_call | solution.py:132
  113.9 3.7 %shard_map.102 = (f32[32,512]{1,0:T(8,128)S(1)}, f32[32,512]{1,0:T(8,128)S(1)}) custom-call(s32[96]{0:T(128)S(1)} %dynamic-slice_bitcast_fusion.refs_0_.refs_1_, s32[2]{0:T(128)S(1)} %pad_add_fusion.refs_0_.refs_1_, f32[32,4096]{1,0:T(8,128)S(1)} %shard_map.100.refs_1_.refs_2_.refs_8_, f32[32,512]{1,0:T(8,128)S(1)} %get-tuple-element.84.refs_3_, ...), custom_call_target="tpu_custom_call" | custom-call | flops 1000 | bytes 1000 | tf_op jit(solution)/shard_map/pallas_call | solution.py:132
  117.7 2.9 %shard_map.103.refs_2_ = f32[2048,512]{1,0:T(8,128)S(1)} custom-call(s32[96]{0:T(128)S(1)} %dynamic-slice_bitcast_fusion.refs_0_.refs_1_, f32[2048,512]{1,0:T(8,128)S(1)} %get-tuple-element.80.refs_3_.refs_1_, bf16[4096,512]{1,0:T(8,128)(2,1)S(1)} %shard_map.81.refs_2_.refs_3_.refs_6_, bf16[512,2048]{1,0:T(8,128)(2,1)S(1)} %collective-permute-done.22.refs_7_.refs_3_.refs_6_, ...), custom_call_target="tpu_custom_call" | custom-call | flops 1000 | bytes 1000 | tf_op jit(solution)/shard_map/pallas_call | solution.py:132
  121.2 3.9 %collective-permute-start.28 = (f32[32,512]{1,0:T(8,128)S(1)}, f32[32,512]{1,0:T(8,128)S(1)}, u32[]{:S(2)}, u32[]{:S(2)}) collective-permute-start(f32[32,512]{1,0:T(8,128)S(1)} %shard_map.104.refs_9_), channel_id=1, source_target_pairs={{0,64},{32,96},{64,0},{96,32},{1,65},{33,97},{65,1},{97,33},{2,66}... | collective-permute-start | bytes 196616 | tf_op jit(solution)/shard_map/ppermute | solution.py:47
  130.6 7.7 %shard_map.105 = (f32[4096,512]{1,0:T(8,128)}, f32[32,512]{1,0:T(8,128)}) custom-call(s32[2]{0:T(128)S(1)} %pad_add_fusion.refs_0_.refs_1_, s32[96]{0:T(128)S(1)} %dynamic-slice_bitcast_fusion.refs_0_.refs_1_, f32[2048,512]{1,0:T(8,128)S(1)} %get-tuple-element.79.refs_3_.refs_2_, f32[4096,512]{1,0:T(8,128)} %bitcast.21, ...), custom_call_target="tpu_custom_call" | custom-call | flops 1000 | bytes 1000 | tf_op jit(solution)/shard_map/pallas_call | solution.py:132
  (84 shorter events, 44.5 us)
Async XLA Ops:
  4.6 17.7 %collective-permute-start.1 = (bf16[4096,512]{1,0:T(8,128)(2,1)}, bf16[4096,512]{1,0:T(8,128)(2,1)}, u32[]{:S(2)}, u32[]{:S(2)}) collective-permute-start(bf16[4096,512]{1,0:T(8,128)(2,1)} %refs_5_.3), channel_id=1, source_target_pairs={{0,1},{1,0},{2,3},{3,2},{4,5},{5,4},{6,7},{7,6},{8,9},{9,8},{10,11... | collective-permute-start | bytes 12582920 | tf_op jit(solution)/shard_map/ppermute | solution.py:39
  4.8 20.2 %collective-permute-start.3 = (bf16[256,2048]{1,0:T(8,128)(2,1)S(1)}, bf16[256,2048]{1,0:T(8,128)(2,1)S(1)}, u32[]{:S(2)}, u32[]{:S(2)}) collective-permute-start(bf16[256,2048]{1,0:T(8,128)(2,1)S(1)} %shard_map.77.refs_3_.refs_0_), channel_id=1, source_target_pairs={{0,24},{1,7},{2,26},{3,1},{4,28},{5,3},{6,30},{7,5},{8,0},{9,15},{... | collective-permute-start | bytes 3145736 | tf_op jit(solution)/shard_map/ppermute | solution.py:35
  7.7 18.8 %collective-permute-start.4 = (bf16[256,2048]{1,0:T(8,128)(2,1)S(1)}, bf16[256,2048]{1,0:T(8,128)(2,1)S(1)}, u32[]{:S(2)}, u32[]{:S(2)}) collective-permute-start(bf16[256,2048]{1,0:T(8,128)(2,1)S(1)} %shard_map.77.refs_3_.refs_0_), channel_id=1, source_target_pairs={{0,8},{1,3},{2,10},{3,5},{4,12},{5,7},{6,14},{7,1},{8,16},{9,11},{... | collective-permute-start | bytes 3145736 | tf_op jit(solution)/shard_map/ppermute | solution.py:35
  15.4 9.5 %collective-permute-start.5 = (f32[2,32,1024]{2,1,0:T(8,128)S(1)}, f32[2,32,1024]{2,1,0:T(8,128)S(1)}, u32[]{:S(2)}, u32[]{:S(2)}) collective-permute-start(f32[2,32,1024]{2,1,0:T(8,128)S(1)} %get-tuple-element.53.refs_3_), channel_id=1, source_target_pairs={{0,4},{1,17},{2,6},{3,19},{4,0},{5,21},{6,2},{7,23},{8,12},{9,25},... | collective-permute-start | bytes 786440 | tf_op jit(solution)/shard_map/ppermute | solution.py:55
  26.6 12.0 %collective-permute-start.6 = (bf16[128,2048]{1,0:T(8,128)(2,1)S(1)}, bf16[128,2048]{1,0:T(8,128)(2,1)S(1)}, u32[]{:S(2)}, u32[]{:S(2)}) collective-permute-start(bf16[128,2048]{1,0:T(8,128)(2,1)S(1)} %get-tuple-element.56.refs_3_), channel_id=1, source_target_pairs={{0,8},{1,3},{2,10},{3,5},{4,12},{5,7},{6,14},{7,1},{8,16},{9,11},{... | collective-permute-start | bytes 1572872 | tf_op jit(solution)/shard_map/ppermute | solution.py:35
  26.7 11.9 %collective-permute-start.7 = (bf16[128,2048]{1,0:T(8,128)(2,1)S(1)}, bf16[128,2048]{1,0:T(8,128)(2,1)S(1)}, u32[]{:S(2)}, u32[]{:S(2)}) collective-permute-start(bf16[128,2048]{1,0:T(8,128)(2,1)S(1)} %get-tuple-element.57), channel_id=1, source_target_pairs={{0,24},{1,7},{2,26},{3,1},{4,28},{5,3},{6,30},{7,5},{8,0},{9,15},{... | collective-permute-start | bytes 1572872 | tf_op jit(solution)/shard_map/ppermute | solution.py:35
  29.9 6.4 %collective-permute-start.8 = (f32[32,1024]{1,0:T(8,128)S(1)}, f32[32,1024]{1,0:T(8,128)S(1)}, u32[]{:S(2)}, u32[]{:S(2)}) collective-permute-start(f32[32,1024]{1,0:T(8,128)S(1)} %get-tuple-element.55.refs_2_), channel_id=1, source_target_pairs={{0,2},{1,9},{2,0},{3,11},{4,6},{5,13},{6,4},{7,15},{8,10},{9,1},{1... | collective-permute-start | bytes 393224 | tf_op jit(solution)/shard_map/ppermute | solution.py:55
  36.5 29.9 %collective-permute-start.16 = (bf16[512,2048]{1,0:T(8,128)(2,1)S(1)}, bf16[512,2048]{1,0:T(8,128)(2,1)S(1)}, u32[]{:S(2)}, u32[]{:S(2)}) collective-permute-start(bf16[512,2048]{1,0:T(8,128)(2,1)S(1)} %shard_map.85.refs_3_.refs_5_.refs_4_), channel_id=1, source_target_pairs={{0,6},{1,25},{2,0},{3,27},{4,2},{5,29},{6,4},{7,31},{8,14},{9,1},{... | collective-permute-start | bytes 6291464 | tf_op jit(solution)/shard_map/ppermute | solution.py:35
  38.5 27.9 %collective-permute-start.15 = (bf16[512,2048]{1,0:T(8,128)(2,1)S(1)}, bf16[512,2048]{1,0:T(8,128)(2,1)S(1)}, u32[]{:S(2)}, u32[]{:S(2)}) collective-permute-start(bf16[512,2048]{1,0:T(8,128)(2,1)S(1)} %shard_map.85.refs_3_.refs_5_.refs_4_), channel_id=1, source_target_pairs={{0,2},{1,9},{2,4},{3,11},{4,6},{5,13},{6,0},{7,15},{8,10},{9,17},{... | collective-permute-start | bytes 6291464 | tf_op jit(solution)/shard_map/ppermute | solution.py:35
  38.7 49.1 %collective-permute-start.20 = (bf16[512,2048]{1,0:T(8,128)(2,1)S(1)}, bf16[512,2048]{1,0:T(8,128)(2,1)S(1)}, u32[]{:S(2)}, u32[]{:S(2)}) collective-permute-start(bf16[512,2048]{1,0:T(8,128)(2,1)S(1)} %shard_map.86.refs_6_.refs_5_), channel_id=1, source_target_pairs={{0,6},{1,25},{2,0},{3,27},{4,2},{5,29},{6,4},{7,31},{8,14},{9,1},{... | collective-permute-start | bytes 6291464 | tf_op jit(solution)/shard_map/ppermute | solution.py:35
  42.0 49.6 %collective-permute-start.9 = (bf16[512,2048]{1,0:T(8,128)(2,1)S(1)}, bf16[512,2048]{1,0:T(8,128)(2,1)S(1)}, u32[]{:S(2)}, u32[]{:S(2)}) collective-permute-start(bf16[512,2048]{1,0:T(8,128)(2,1)S(1)} %shard_map.86.refs_6_.refs_5_), channel_id=1, source_target_pairs={{0,2},{1,9},{2,4},{3,11},{4,6},{5,13},{6,0},{7,15},{8,10},{9,17},{... | collective-permute-start | bytes 6291464 | tf_op jit(solution)/shard_map/ppermute | solution.py:35
  44.9 7.7 %collective-permute-start.11 = (f32[2,32,512]{2,1,0:T(8,128)S(1)}, f32[2,32,512]{2,1,0:T(8,128)S(1)}, u32[]{:S(2)}, u32[]{:S(2)}) collective-permute-start(f32[2,32,512]{2,1,0:T(8,128)S(1)} %get-tuple-element.61.refs_7_), channel_id=1, source_target_pairs={{0,64},{32,96},{64,0},{96,32},{1,65},{33,97},{65,1},{97,33},{2,66}... | collective-permute-start | bytes 393224 | tf_op jit(solution)/shard_map/ppermute | solution.py:43
  52.6 5.5 %collective-permute-start.12 = (f32[32,512]{1,0:T(8,128)S(1)}, f32[32,512]{1,0:T(8,128)S(1)}, u32[]{:S(2)}, u32[]{:S(2)}) collective-permute-start(f32[32,512]{1,0:T(8,128)S(1)} %get-tuple-element.64.refs_9_), channel_id=1, source_target_pairs={{0,32},{32,0},{64,96},{96,64},{1,33},{33,1},{65,97},{97,65},{2,34}... | collective-permute-start | bytes 196616 | tf_op jit(solution)/shard_map/ppermute | solution.py:43
  58.1 5.1 %collective-permute-start.13 = (f32[32,512]{1,0:T(8,128)S(1)}, f32[32,512]{1,0:T(8,128)S(1)}, u32[]{:S(2)}, u32[]{:S(2)}) collective-permute-start(f32[32,512]{1,0:T(8,128)S(1)} %shard_map.91.refs_0_), channel_id=1, source_target_pairs={{0,8},{1,3},{2,10},{3,1},{4,12},{5,7},{6,14},{7,5},{8,0},{9,11},{1... | collective-permute-start | bytes 196616 | tf_op jit(solution)/shard_map/ppermute | solution.py:55
  63.2 6.6 %collective-permute-start.14 = (f32[32,512]{1,0:T(8,128)S(1)}, f32[32,512]{1,0:T(8,128)S(1)}, u32[]{:S(2)}, u32[]{:S(2)}) collective-permute-start(f32[32,512]{1,0:T(8,128)S(1)} %shard_map.92.refs_8_.refs_0_), channel_id=1, source_target_pairs={{0,16},{1,5},{2,18},{3,7},{4,20},{5,1},{6,22},{7,3},{8,24},{9,13},... | collective-permute-start | bytes 196616 | tf_op jit(solution)/shard_map/ppermute | solution.py:55
  71.2 5.0 %collective-permute-start.18 = (f32[32,512]{1,0:T(8,128)S(1)}, f32[32,512]{1,0:T(8,128)S(1)}, u32[]{:S(2)}, u32[]{:S(2)}) collective-permute-start(f32[32,512]{1,0:T(8,128)S(1)} %collective-permute-done.17.refs_8_.refs_0_), channel_id=1, source_target_pairs={{0,8},{1,3},{2,10},{3,1},{4,12},{5,7},{6,14},{7,5},{8,0},{9,11},{1... | collective-permute-start | bytes 196616 | tf_op jit(solution)/shard_map/ppermute | solution.py:55
  76.2 6.6 %collective-permute-start.19 = (f32[32,512]{1,0:T(8,128)S(1)}, f32[32,512]{1,0:T(8,128)S(1)}, u32[]{:S(2)}, u32[]{:S(2)}) collective-permute-start(f32[32,512]{1,0:T(8,128)S(1)} %shard_map.96.refs_0_), channel_id=1, source_target_pairs={{0,16},{1,5},{2,18},{3,7},{4,20},{5,1},{6,22},{7,3},{8,24},{9,13},... | collective-permute-start | bytes 196616 | tf_op jit(solution)/shard_map/ppermute | solution.py:55
  79.5 34.2 %collective-permute-start.22 = (bf16[512,2048]{1,0:T(8,128)(2,1)S(1)}, bf16[512,2048]{1,0:T(8,128)(2,1)S(1)}, u32[]{:S(2)}, u32[]{:S(2)}) collective-permute-start(bf16[512,2048]{1,0:T(8,128)(2,1)S(1)} %collective-permute-done.15.refs_4_), channel_id=1, source_target_pairs={{0,2},{1,9},{2,4},{3,11},{4,6},{5,13},{6,0},{7,15},{8,10},{9,17},{... | collective-permute-start | bytes 6291464 | tf_op jit(solution)/shard_map/ppermute | solution.py:35
  87.9 26.0 %collective-permute-start.25 = (bf16[512,2048]{1,0:T(8,128)(2,1)S(1)}, bf16[512,2048]{1,0:T(8,128)(2,1)S(1)}, u32[]{:S(2)}, u32[]{:S(2)}) collective-permute-start(bf16[512,2048]{1,0:T(8,128)(2,1)S(1)} %collective-permute-done.20.refs_5_), channel_id=1, source_target_pairs={{0,6},{1,25},{2,0},{3,27},{4,2},{5,29},{6,4},{7,31},{8,14},{9,1},{... | collective-permute-start | bytes 6291464 | tf_op jit(solution)/shard_map/ppermute | solution.py:35
  89.7 5.0 %collective-permute-start.21 = (f32[32,512]{1,0:T(8,128)S(1)}, f32[32,512]{1,0:T(8,128)S(1)}, u32[]{:S(2)}, u32[]{:S(2)}) collective-permute-start(f32[32,512]{1,0:T(8,128)S(1)} %shard_map.97.refs_8_), channel_id=1, source_target_pairs={{0,32},{32,0},{64,96},{96,64},{1,33},{33,1},{65,97},{97,65},{2,34}... | collective-permute-start | bytes 196616 | tf_op jit(solution)/shard_map/ppermute | solution.py:43
  94.7 6.9 %collective-permute-start.23 = (f32[2,32,512]{2,1,0:T(8,128)S(1)}, f32[2,32,512]{2,1,0:T(8,128)S(1)}, u32[]{:S(2)}, u32[]{:S(2)}) collective-permute-start(f32[2,32,512]{2,1,0:T(8,128)S(1)} %pad_maximum_fusion.refs_8_), channel_id=1, source_target_pairs={{0,64},{32,96},{64,0},{96,32},{1,65},{33,97},{65,1},{97,33},{2,66}... | collective-permute-start | bytes 393224 | tf_op jit(solution)/shard_map/ppermute | solution.py:43
  120.7 9.9 %collective-permute-start.27 = (f32[2048,512]{1,0:T(8,128)S(1)}, f32[2048,512]{1,0:T(8,128)S(1)}, u32[]{:S(2)}, u32[]{:S(2)}) collective-permute-start(f32[2048,512]{1,0:T(8,128)S(1)} %shard_map.103.refs_2_), channel_id=1, source_target_pairs={{0,1},{1,0},{2,3},{3,2},{4,5},{5,4},{6,7},{7,6},{8,9},{9,8},{10,11... | collective-permute-start | bytes 12582920 | tf_op jit(solution)/shard_map/ppermute | solution.py:39
  121.2 7.9 %collective-permute-start.28 = (f32[32,512]{1,0:T(8,128)S(1)}, f32[32,512]{1,0:T(8,128)S(1)}, u32[]{:S(2)}, u32[]{:S(2)}) collective-permute-start(f32[32,512]{1,0:T(8,128)S(1)} %shard_map.104.refs_9_), channel_id=1, source_target_pairs={{0,64},{32,96},{64,0},{96,32},{1,65},{33,97},{65,1},{97,33},{2,66}... | collective-permute-start | bytes 196616 | tf_op jit(solution)/shard_map/ppermute | solution.py:47
  125.1 5.5 %collective-permute-start.29 = (f32[32,512]{1,0:T(8,128)S(1)}, f32[32,512]{1,0:T(8,128)S(1)}, u32[]{:S(2)}, u32[]{:S(2)}) collective-permute-start(f32[32,512]{1,0:T(8,128)S(1)} %shard_map.104.refs_9_), channel_id=1, source_target_pairs={{0,32},{32,64},{64,96},{96,0},{1,33},{33,65},{65,97},{97,1},{2,34}... | collective-permute-start | bytes 196616 | tf_op jit(solution)/shard_map/ppermute | solution.py:47
  (12 other events, 46.9 us)

commit v4 on v3

--- a/solution.py
+++ b/solution.py
@@ -11,6 +11,7 @@
 F32, BF16 = jnp.float32, jnp.bfloat16
 N, R, D, F, T = 4, 32, 4096, 512, 128
 OFFSETS = (0, -1, 1, 2)
+BITS = (0, 2, 1, 3)
 MIB = 1024 * 1024
 WHOLE = pl.BlockSpec(memory_space=pltpu.VMEM)
 SMEM = pl.BlockSpec(memory_space=pltpu.SMEM)
@@ -62,7 +63,7 @@
         at = y if c == 0 else x
         for i in range(N):
             for j, first in enumerate(OFFSETS):
-                for kind, second in enumerate((OFFSETS[i], (at ^ i) - at)):
+                for kind, second in enumerate((OFFSETS[i], (at ^ BITS[i]) - at)):
                     dx, dy = (first, second) if c == 0 else (second, first)
                     for m in range(2):
                         offsets[flat(x, y, c), kind, i, j, m] = flat(x + dx, y + dy, c ^ m) * T
@@ -140,7 +141,7 @@
 B = 2 * N * N
 
 
-def tokens_kernel(off_ref, q_ref, g_ref, keep_ref, send_ref, other_ref, h_ref):
+def tokens_kernel(off_ref, q_ref, g_ref, own_ref, other_ref, h_ref):
     q = jnp.concatenate(split(q_ref[...], 3), 0)
     for k in range(N * 2):
         rows = [g_ref[pl.ds(pl.multiple_of(off_ref[B + k * N + j], T), T), :] for j in range(N)]
@@ -148,9 +149,8 @@
         for j in range(N):
             h_ref[k * N + j] = r[:, j * T : (j + 1) * T]
     for i in range(N):
-        out = (keep_ref if i < 2 else send_ref).at[i % 2]
         for k in range(2 * N):
-            out[:, k * T : (k + 1) * T] = h_ref[i * 2 * N + k]
+            own_ref[i, :, k * T : (k + 1) * T] = h_ref[i * 2 * N + k]
             other_ref[i, :, k * T : (k + 1) * T] = h_ref[off_ref[2 * B + i * 2 * N + k]]
 
 
@@ -158,10 +158,10 @@
     w = 2 * N * T
     return run(
         tokens_kernel,
-        [shape((2, R, w)), shape((2, R, w)), shape((N, R, w))],
+        [shape((N, R, w))] * 2,
         (off, q, g),
         [SMEM, WHOLE, WHOLE],
-        [WHOLE] * 3,
+        [WHOLE] * 2,
         after,
         scratch_shapes=[pltpu.VMEM((B, R, T), F32)],
     )
@@ -222,20 +222,13 @@
     )
 
 
-def add_halves_kernel(a_ref, b_ref, got_ref, keep_ref, send_ref):
-    keep_ref[...] = a_ref[...] + got_ref[:2]
-    send_ref[...] = b_ref[...] + got_ref[2:]
-
-
-def add_halves(a, b, got, after=()):
-    return run(
-        add_halves_kernel,
-        [shape(a.shape)] * 2,
-        (a, b, got),
-        [WHOLE] * 3,
-        [WHOLE] * 2,
-        after,
-    )
+def add_parts_kernel(a_ref, b_ref, *outs):
+    for i, out in enumerate(outs):
+        out[...] = a_ref[i] + b_ref[i]
+
+
+def add_parts(a, b, after=()):
+    return run(add_parts_kernel, [shape(a.shape[1:])] * a.shape[0], (a, b), [WHOLE] * 2, [WHOLE] * a.shape[0], after)
 
 
 def add_pair_kernel(a_ref, got_ref, keep_ref, send_ref):
@@ -289,12 +282,12 @@
     return run(held_kernel, pltpu.VMEM(array.shape, array.dtype), (array,), [WHOLE], WHOLE, after)
 
 
-def sketch_kernel(pos_ref, h0, h1, e0_ref, e1_ref, x0_ref, x1_ref, keep_ref, send_ref):
+def sketch_kernel(pos_ref, h0, h1, h2, h3, e0_ref, e1_ref, x0_ref, x1_ref, keep_ref, send_ref):
     z = pos_ref[1]
-    h = jnp.concatenate(split(h0[...] + h1[...], 3), 0)
+    h = jnp.concatenate(split((h0[...] + h1[...]) + (h2[...] + h3[...]), 3), 0)
     n = D // 8
     for i in range(N):
-        part = z ^ i
+        part = z ^ BITS[i]
         columns = pl.ds(pl.multiple_of(part * n, n), n)
         x = jnp.concatenate([x0_ref[:, columns], x1_ref[:, columns]], 0)
         (keep_ref if i < 2 else send_ref)[i % 2] = add3(dot(h, x)) + (e0_ref[part] + e1_ref[part])
@@ -305,7 +298,7 @@
         sketch_kernel,
         [shape((2, R, D // 8))] * 2,
         (pos, *h, *e, *xs),
-        [SMEM] + [WHOLE] * 6,
+        [SMEM] + [WHOLE] * 8,
         [WHOLE] * 2,
         after,
     )
@@ -316,7 +309,7 @@
     n = D // 8
     for half, ref in ((1 - c, mine_ref), (c, other_ref)):
         for i in range(N):
-            chunk = half * N + (z ^ i)
+            chunk = half * N + (z ^ BITS[i])
             s_ref[:, pl.ds(pl.multiple_of(chunk * n, n), n)] = ref[i] * 0.25
     s = s_ref[...]
     gram = dot_both(s, s, NT)
@@ -436,12 +429,12 @@
 def right_part(pos, p, acc, e, after):
     return run(
         right_kernel,
-        [shape((R, F))] * 2,
+        [shape((R, F))] * 2 + [FETCH[0]],
         (pos, p, *acc, e),
         [SMEM] + [WHOLE] * 3 + [HBM],
-        [WHOLE] * 2,
-        after,
-        scratch_shapes=FETCH,
+        [WHOLE] * 3,
+        after,
+        scratch_shapes=FETCH[1:],
     )
 
 
@@ -472,65 +465,43 @@
     )
 
 
-def final_kernel(n, rows, starts, pos_ref, off_ref, m_ref, e_ref, got_ref, g_ref, *refs):
-    xs, (p_ref, q0, q1, q2, q3, out_ref, q_ref, right_ref, buf_ref, sems) = refs[:n], refs[n:]
-    copies = fetches(e_ref, 1 - pos_ref[0], buf_ref, sems)
-    i, steps = pl.program_id(0), H // rows
-    k = n * 4 * T
-
-    @pl.when(i == 0)
-    def _():
-        for copy in copies:
-            copy.start()
-        q = ((q0[...] + q1[...]) + (q2[...] + q3[...])) * 0.25
-        q_ref[...] = q
-        s1, s2 = split(-q, 2)
-        for j, start in enumerate(starts):
-            for b in range(4):
-                at = pl.ds(pl.multiple_of(off_ref[start + b], T), T)
-                right_ref[(4 * j + b) * T : (4 * j + b + 1) * T, :] = g_ref[at, :]
-        right_ref[k:, :] = jnp.concatenate([s1, s2, s1], 0)
-
-    half = jnp.where(i < steps, pos_ref[0], 1 - pos_ref[0])
-    step = lax.rem(i, steps)
-    p1, p2 = split(p_ref[:, pl.ds(pl.multiple_of(half * H + step * rows, rows), rows)], 2)
-    p = jnp.concatenate([p1, p1, p2], 0)
-    at = pl.ds(pl.multiple_of(step * rows, rows), rows)
-
-    @pl.when(i < steps)
-    def _():
-        left = jnp.concatenate([r[:, at] for r in xs] + [p], 0)
-        out_ref[...] = m_ref[at, :] + dot(left, right_ref[...], TN)
-
-    for j, copy in enumerate(copies):
-        pl.when(i == steps + j * steps // N)(copy.wait)
-
-    @pl.when(i >= steps)
-    def _():
-        out_ref[...] = (buf_ref[at, :] + got_ref[at, :]) + dot(p, right_ref[k:, :], TN)
-
-
-def final(off, pos, own, e, got, groups, g, p, q, rows=H // 2):
-    n, steps = len(groups), H // rows
-    half = lambda i, pos: jnp.where(i < steps, pos[0], 1 - pos[0])
-    return run(
-        functools.partial(final_kernel, n, rows, [start for start, _ in groups]),
+def final_kernel(starts, pos_ref, off_ref, m_ref, e_ref, got_ref, g_ref, *refs):
+    n, step = len(starts), H // N
+    xs, refs = refs[:n], refs[n:]
+    p_ref, q0, q1, q2, q3, out_ref, q_ref, made_ref, out_sems = refs
+    c = pos_ref[0]
+    q = ((q0[...] + q1[...]) + (q2[...] + q3[...])) * 0.25
+    q_ref[...] = q
+    s1, s2 = split(-q, 2)
+    low = jnp.concatenate([s1, s2, s1], 0)
+    rows = jnp.concatenate([block_rows(off_ref, g_ref, starts), low], 0)
+    sent = []
+    for k in range(2 * N):
+        own, at = k < N, slice(k % N * step, (k % N + 1) * step)
+        first = pl.multiple_of((c if own else 1 - c) * H + k % N * step, step)
+        p1, p2 = split(p_ref[:, pl.ds(first, step)], 2)
+        p = jnp.concatenate([p1, p1, p2], 0)
+        here = made_ref.at[pl.ds(k * step, step), :]
+        if own:
+            here[...] = m_ref[at, :] + dot(jnp.concatenate([r[:, at] for r in xs] + [p], 0), rows, TN)
+        else:
+            here[...] = (e_ref[at, :] + got_ref[at, :]) + dot(p, low, TN)
+        sent.append(pltpu.make_async_copy(here, out_ref.at[pl.ds(first, step), :], out_sems.at[k]))
+        sent[-1].start()
+    for copy in sent:
+        copy.wait()
+
+
+def final(off, pos, own, e, got, groups, g, p, q):
+    n = len(groups)
+    return run(
+        functools.partial(final_kernel, [start for start, _ in groups]),
         [shape((D, F)), shape((R, F))],
         [pos, off, own, e, got, g] + [x for _, x in groups] + [p, *q],
-        [
-            SMEM,
-            WHOLE,
-            HBM,
-        ]
-        + [WHOLE] * (n + 3 + N),
-        [
-            pl.BlockSpec((rows, F), lambda i, pos: (half(i, pos) * steps + lax.rem(i, steps), 0)),
-            pl.BlockSpec((R, F), lambda i, pos: (0, 0)),
-        ],
-        prefetch=1,
-        grid=(2 * steps,),
+        [SMEM, SMEM] + [WHOLE] * (n + 5 + N),
+        [HBM, WHOLE],
         vmem=24,
-        scratch_shapes=[pltpu.VMEM((n * 4 * T + 3 * R, F), BF16)] + FETCH,
+        scratch_shapes=[pltpu.VMEM((D, F), F32), pltpu.SemaphoreType.DMA((2 * N,))],
     )
 
 
@@ -548,66 +519,62 @@
     (x0,) = pack(stack_kernel, (mine, swap(send)), (2 * T,), ())
     a, b = hop(x0, True, 1), hop(x0, True, -1)
     g_other = swap(later(g, x0))
-    keep, send, other = tokens(off, q, g, (x0,))
+    own, other = tokens(off, q, g, (x0,))
     got = swap(other)
-    keep, send = add_halves(keep, send, got, ())
-    got = twin(send, False, 2)
-    e_other = errors(pos, q, e, 1, (send,))
-    g_other = held(g_other, (e_other,))
-    h, send = add_pair(keep, got, (g_other,))
-    h_got = twin(send, False, 1)
-    top, bottom = pack(halves_kernel, (a, b), (T, T), (send,))
+    g_other = held(g_other, (own,))
+    h = add_parts(own, got, (g_other,))
+    h = [h[0]] + [twin(v, False, bit) for v, bit in zip(h[1:], BITS[1:])]
+    e_other = errors(pos, q, e, 1, (h[0],))
+    top, bottom = pack(halves_kernel, (a, b), (T, T), (e_other, *h[1:]))
     c, d = hop(top, True, 1), hop(bottom, True, -1)
-    e_got = swap(later(e_other, top))
-    e_own = errors(pos, q, e, 0, (top,))
-
-    (g0,) = pack(stack_kernel, (x0, a), (4 * T,), (h_got, e_own))
+
+    (g0,) = pack(stack_kernel, (x0, a), (4 * T,), (top,))
     l0, r0 = hop(g0, False, 1), hop(g0, False, -1)
-    (g1,) = pack(stack_kernel, (b, c, d), (4 * T,), (g0,))
+    e_got = swap(later(e_other, g0))
+    e_own = errors(pos, q, e, 0, (g0,))
+    (g1,) = pack(stack_kernel, (b, c, d), (4 * T,), (e_own,))
     l1, r1 = hop(g1, False, 1), hop(g1, False, -1)
 
-    keep, send = sketch_part(pos, (h, h_got), (e_own, e_got), (g0, g1), ())
-    got = hop_z(send, 2)
+    keep, send = sketch_part(pos, h, (e_own, e_got), (g0, g1), ())
+    got = hop_z(send, 1)
     near = [(0, g0), (4, g1)]
     acc = merge(off, pos, g, g_other, near, 0, H // 2, e, None, (send,))
     keep, send = add_pair(keep, got, (acc[0],))
-    got = hop_z(send, 1)
+    got = hop_z(send, 2)
     acc = merge(off, pos, g, g_other, near, H // 2, H, e, acc, (send,))
     (s,) = add([keep], [got], (acc[0],))
     got = twin(s, True, 1)
-    (s,) = add([s], [got], ())
-    got = twin(s, True, 2)
     l0, r0 = later(l0, s), later(r0, s)
     o0 = hop(l0, False, 1)
     mid = [(8, l0), (16, r0)]
     acc = merge(off, pos, g, g_other, mid, 0, H // 2, None, acc, (s,))
     (s,) = add([s], [got], (acc[0],))
-    s = swap(s)
-    got = twin(s, True, 1)
+    got = twin(s, True, 2)
     acc = merge(off, pos, g, g_other, mid, H // 2, H, None, acc, (s,))
     (s,) = add([s], [got], (acc[0],))
-    got = twin(s, True, 2)
-    (s,) = add([s], [got], ())
-    got = hop_z(s, 1)
+    s = swap(s)
+    (s,) = add([s], [twin(s, True, 1)], ())
+    (s,) = add([s], [twin(s, True, 2)], ())
+    got = hop_z(s, 2)
     l1, r1 = later(l1, s), later(r1, s)
     o1 = hop(r1, False, -1)
     far = [(12, l1), (20, r1)]
     acc = merge(off, pos, g, g_other, far, 0, H // 2, None, acc, (s,))
     pair = jnp.stack([later(s, acc[0]), got])
-    got = hop_z(pair, 2)
+    got = hop_z(pair, 1)
     acc = merge(off, pos, g, g_other, far, H // 2, H, None, acc, (pair,))
     stack = jnp.concatenate([later(pair, acc[0]), got])
     p = basis(pos, stack, swap(stack), (acc[0],))
 
     last = [(24, later(o0, p)), (28, later(o1, p))]
-    qp, q_send = right_part(pos, p, acc, e, ())
+    qp, q_send, e_rest = right_part(pos, p, acc, e, ())
     qp, q_send = right_rest(off, pos, p, qp, q_send, g, g_other, last)
     q_got = swap(q_send)
     out = last_other(off, acc[1], last, g_other, (q_send,))
     (qp,) = add([qp], [q_got], (out,))
     out = swap(later(out, qp))
     qs = (qp, around_z(qp, 2), around_z(qp, 1), around_z(qp, -1))
-    err, qf = final(off, pos, acc[0], e, out, last, g, p, qs)
+    err, qf = final(off, pos, acc[0], e_rest, out, last, g, p, qs)
     return err[None], p.T, qf.T
 
 

time: 139 us -> 135 us (0.971)
  starting transfers between devices: 45.9 us -> 42.5 us
    ppermute x10, waiting for transfers between devices: 6.73 us -> 9.63 us  [hop(): return lax.ppermute(array, 'tensor', pairs)]
    ppermute x6 -> x7, waiting for transfers between devices: 10.8 us -> 8.66 us  [twin(): return lax.ppermute(array, 'tensor', pairs)]
    ppermute x3, starting transfers between devices: 7.12 us -> 5.56 us  [around_z(): return lax.ppermute(array, 'dp', [(i, (i + d) % N) for i in range(N)])]
    ppermute x8, waiting for transfers between devices: 7.76 us -> 6.2 us  [swap(): return lax.ppermute(array, 'tensor', [(i, i ^ 1) for i in range(2 * N * N)])]
    ppermute x4, starting transfers between devices: 11.1 us -> 9.57 us  [hop_z(): return lax.ppermute(array, 'dp', [(i, i ^ bit) for i in range(N)])]
    pallas_call x30 -> x29, Pallas kernels: 58.8 us -> 57.7 us  [run(): pl.pallas_call(wrapped, out_shape=out_shape, compiler_params=options, **kw)]
    ppermute x6 -> x7, starting transfers between devices: 12.6 us -> 12.4 us  [twin(): return lax.ppermute(array, 'tensor', pairs)]
  transfers between devices with their start and end apart: 31 -> 32, of which waited for: 15 -> 16; matrix products, arithmetic and copies ran while one was open for 1% -> 1% of each run, Pallas kernels for 34% -> 35%
where the time goes in v4:
time: 135 us; the launch traced here: 134 us
  Pallas kernels  57.7 us (43%)
  starting transfers between devices  42.5 us (31%)
  waiting for transfers between devices  26.7 us (20%)
  local copies, waits for them, and re-layouts  5.77 us (4%)
    pallas_call x29, Pallas kernels, run(): pl.pallas_call(wrapped, out_shape=out_shape, compiler_params=options, **kw)  57.7 us
    ppermute x10, starting transfers between devices, hop(): return lax.ppermute(array, 'tensor', pairs)  13.2 us
    ppermute x7, starting transfers between devices, twin(): return lax.ppermute(array, 'tensor', pairs)  12.4 us
    ppermute x10, waiting for transfers between devices, hop(): return lax.ppermute(array, 'tensor', pairs)  9.63 us
    ppermute x4, starting transfers between devices, hop_z(): return lax.ppermute(array, 'dp', [(i, i ^ bit) for i in range(N)])  9.57 us
    ppermute x7, waiting for transfers between devices, twin(): return lax.ppermute(array, 'tensor', pairs)  8.66 us
    ppermute x8, waiting for transfers between devices, swap(): return lax.ppermute(array, 'tensor', [(i, i ^ 1) for i in range(2 * N * N)])  6.2 us
    ppermute x3, starting transfers between devices, around_z(): return lax.ppermute(array, 'dp', [(i, (i + d) % N) for i in range(N)])  5.56 us
  transfers between devices with their start and end apart: 32, of which 16 were waited for; matrix products, arithmetic and copies ran while one was open for 1% of the time, Pallas kernels for 35%

profile of v4, /device:TPU:0, one launch (start us, length us, event | category | flops | bytes accessed | tf_op | source)
XLA Modules:
  0.0 133.9 jit_solution(9416254477626685662)
XLA Ops:
  4.8 2.8 %collective-permute-start.2 = (bf16[256,2048]{1,0:T(8,128)(2,1)S(1)}, bf16[256,2048]{1,0:T(8,128)(2,1)S(1)}, u32[]{:S(2)}, u32[]{:S(2)}) collective-permute-start(bf16[256,2048]{1,0:T(8,128)(2,1)S(1)} %shard_map.77.refs_3_.refs_0_), channel_id=1, source_target_pairs={{0,24},{1,7},{2,26},{3,1},{4,28},{5,3},{6,30},{7,5},{8,0},{9,15},{... | collective-permute-start | bytes 3145736 | tf_op jit(solution)/shard_map/ppermute | solution.py:36
  16.4 2.9 %collective-permute-start.5 = (f32[32,1024]{1,0:T(8,128)S(1)}, f32[32,1024]{1,0:T(8,128)S(1)}, u32[]{:S(2)}, u32[]{:S(2)}) collective-permute-start(f32[32,1024]{1,0:T(8,128)S(1)} %get-tuple-element.53), channel_id=1, source_target_pairs={{0,4},{1,17},{2,6},{3,19},{4,0},{5,21},{6,2},{7,23},{8,12},{9,25},... | collective-permute-start | bytes 393224 | tf_op jit(solution)/shard_map/ppermute | solution.py:56
  20.5 3.6 %shard_map.81.refs_2_ = f32[4,32,512]{2,1,0:T(8,128)S(1)} custom-call(s32[2]{0:T(128)S(1)} %pad_add_fusion.refs_0_.refs_1_, f32[32,512]{1,0:T(8,128)S(1)} %bitcast.13, f32[4096,512]{1,0:T(8,128)} %bitcast.16, f32[32,1024]{1,0:T(8,128)S(1)} %get-tuple-element.52.refs_3_.refs_1_), custom_call_target="tpu_custom_call" | custom-call | flops 1000 | bytes 1000 | tf_op jit(solution)/shard_map/pallas_call | solution.py:133
  30.0 2.9 %collective-permute-start.16 = (bf16[512,2048]{1,0:T(8,128)(2,1)S(1)}, bf16[512,2048]{1,0:T(8,128)(2,1)S(1)}, u32[]{:S(2)}, u32[]{:S(2)}) collective-permute-start(bf16[512,2048]{1,0:T(8,128)(2,1)S(1)} %shard_map.83.refs_3_.refs_7_.refs_4_), channel_id=1, source_target_pairs={{0,6},{1,25},{2,0},{3,27},{4,2},{5,29},{6,4},{7,31},{8,14},{9,1},{... | collective-permute-start | bytes 6291464 | tf_op jit(solution)/shard_map/ppermute | solution.py:36
  32.8 3.6 %shard_map.84.refs_3_.refs_5_ = f32[4,32,512]{2,1,0:T(8,128)S(1)} custom-call(s32[2]{0:T(128)S(1)} %pad_add_fusion.refs_0_.refs_1_, f32[32,512]{1,0:T(8,128)S(1)} %bitcast.14, f32[4096,512]{1,0:T(8,128)} %bitcast.17, bf16[512,2048]{1,0:T(8,128)(2,1)S(1)} %shard_map.83.refs_3_.refs_7_.refs_4_), custom_call_target="tpu_custom_call" | custom-call | flops 1000 | bytes 1000 | tf_op jit(solution)/shard_map/pallas_call | solution.py:133
  36.4 3.8 %collective-permute-done.8.refs_1_ = bf16[128,2048]{1,0:T(8,128)(2,1)S(1)} collective-permute-done((bf16[128,2048]{1,0:T(8,128)(2,1)S(1)}, bf16[128,2048]{1,0:T(8,128)(2,1)S(1)}, u32[]{:S(2)}, u32[]{:S(2)}) %collective-permute-start.8) | collective-permute-done | bytes 524320 | tf_op jit(solution)/shard_map/ppermute | solution.py:36
  42.5 2.7 %collective-permute-start.21 = (bf16[512,2048]{1,0:T(8,128)(2,1)S(1)}, bf16[512,2048]{1,0:T(8,128)(2,1)S(1)}, u32[]{:S(2)}, u32[]{:S(2)}) collective-permute-start(bf16[512,2048]{1,0:T(8,128)(2,1)S(1)} %shard_map.85.refs_8_.refs_5_), channel_id=1, source_target_pairs={{0,6},{1,25},{2,0},{3,27},{4,2},{5,29},{6,4},{7,31},{8,14},{9,1},{... | collective-permute-start | bytes 6291464 | tf_op jit(solution)/shard_map/ppermute | solution.py:36
  50.0 3.8 %shard_map.87 = (f32[2048,512]{1,0:T(8,128)S(1)}, f32[2048,512]{1,0:T(8,128)S(1)}) custom-call(s32[96]{0:T(128)S(1)} %dynamic-slice_bitcast_fusion.refs_0_.refs_1_, s32[2]{0:T(128)S(1)} %pad_add_fusion.refs_0_.refs_1_, bf16[4096,512]{1,0:T(8,128)(2,1)S(1)} %copy-done.1, bf16[4096,512]{1,0:T(8,128)(2,1)S(1)} %shard_map.79.refs_2_.refs_3_.refs_6_, ...), custom_call_target="tpu_custom_call" | custom-call | flops 1000 | bytes 1000 | tf_op jit(solution)/shard_map/pallas_call | solution.py:133
  53.9 3.9 %collective-permute-start.13 = (f32[32,512]{1,0:T(8,128)S(1)}, f32[32,512]{1,0:T(8,128)S(1)}, u32[]{:S(2)}, u32[]{:S(2)}) collective-permute-start(f32[32,512]{1,0:T(8,128)S(1)} %get-tuple-element.63.refs_9_), channel_id=1, source_target_pairs={{0,64},{32,96},{64,0},{96,32},{1,65},{33,97},{65,1},{97,33},{2,66}... | collective-permute-start | bytes 196616 | tf_op jit(solution)/shard_map/ppermute | solution.py:44
  57.8 3.9 %shard_map.89 = (f32[2048,512]{1,0:T(8,128)S(1)}, f32[2048,512]{1,0:T(8,128)S(1)}) custom-call(s32[96]{0:T(128)S(1)} %dynamic-slice_bitcast_fusion.refs_0_.refs_1_, s32[2]{0:T(128)S(1)} %pad_add_fusion.refs_0_.refs_1_, bf16[4096,512]{1,0:T(8,128)(2,1)S(1)} %copy-done.1, ...), custom_call_target="tpu_custom_call", output_to_operand_aliasing={{0}: (7, {}), {1}: (8, {})} | custom-call | flops 1000 | bytes 1000 | tf_op jit(solution)/shard_map/pallas_call | solution.py:133
  62.3 3.1 %shard_map.91 = (f32[2048,512]{1,0:T(8,128)S(1)}, f32[2048,512]{1,0:T(8,128)S(1)}) custom-call(s32[96]{0:T(128)S(1)} %dynamic-slice_bitcast_fusion.refs_0_.refs_1_, s32[2]{0:T(128)S(1)} %pad_add_fusion.refs_0_.refs_1_, bf16[4096,512]{1,0:T(8,128)(2,1)S(1)} %copy-done.1, ...), custom_call_target="tpu_custom_call", output_to_operand_aliasing={{0}: (6, {}), {1}: (7, {})} | custom-call | flops 1000 | bytes 1000 | tf_op jit(solution)/shard_map/pallas_call | solution.py:133
  66.9 3.3 %collective-permute-start.17 = (f32[32,512]{1,0:T(8,128)S(1)}, f32[32,512]{1,0:T(8,128)S(1)}, u32[]{:S(2)}, u32[]{:S(2)}) collective-permute-start(f32[32,512]{1,0:T(8,128)S(1)} %shard_map.92.refs_8_.refs_0_), channel_id=1, source_target_pairs={{0,16},{1,5},{2,18},{3,7},{4,20},{5,1},{6,22},{7,3},{8,24},{9,13},... | collective-permute-start | bytes 196616 | tf_op jit(solution)/shard_map/ppermute | solution.py:56
  70.2 3.1 %shard_map.93 = (f32[2048,512]{1,0:T(8,128)S(1)}, f32[2048,512]{1,0:T(8,128)S(1)}) custom-call(s32[96]{0:T(128)S(1)} %dynamic-slice_bitcast_fusion.refs_0_.refs_1_, s32[2]{0:T(128)S(1)} %pad_add_fusion.refs_0_.refs_1_, bf16[4096,512]{1,0:T(8,128)(2,1)S(1)} %copy-done.1, ...), custom_call_target="tpu_custom_call", output_to_operand_aliasing={{0}: (6, {}), {1}: (7, {})} | custom-call | flops 1000 | bytes 1000 | tf_op jit(solution)/shard_map/pallas_call | solution.py:133
  76.0 3.9 %collective-permute-done.19.refs_1_ = f32[32,512]{1,0:T(8,128)S(1)} collective-permute-done((f32[32,512]{1,0:T(8,128)S(1)}, f32[32,512]{1,0:T(8,128)S(1)}, u32[]{:S(2)}, u32[]{:S(2)}) %collective-permute-start.19) | collective-permute-done | bytes 65568 | tf_op jit(solution)/shard_map/ppermute | solution.py:56
  79.9 3.3 %collective-permute-start.20 = (f32[32,512]{1,0:T(8,128)S(1)}, f32[32,512]{1,0:T(8,128)S(1)}, u32[]{:S(2)}, u32[]{:S(2)}) collective-permute-start(f32[32,512]{1,0:T(8,128)S(1)} %shard_map.95.refs_0_), channel_id=1, source_target_pairs={{0,16},{1,5},{2,18},{3,7},{4,20},{5,1},{6,22},{7,3},{8,24},{9,13},... | collective-permute-start | bytes 196616 | tf_op jit(solution)/shard_map/ppermute | solution.py:56
  83.2 2.8 %collective-permute-done.20.refs_1_ = f32[32,512]{1,0:T(8,128)S(1)} collective-permute-done((f32[32,512]{1,0:T(8,128)S(1)}, f32[32,512]{1,0:T(8,128)S(1)}, u32[]{:S(2)}, u32[]{:S(2)}) %collective-permute-start.20) | collective-permute-done | bytes 65568 | tf_op jit(solution)/shard_map/ppermute | solution.py:56
  87.6 2.5 %collective-permute-start.22 = (f32[32,512]{1,0:T(8,128)S(1)}, f32[32,512]{1,0:T(8,128)S(1)}, u32[]{:S(2)}, u32[]{:S(2)}) collective-permute-start(f32[32,512]{1,0:T(8,128)S(1)} %shard_map.96.refs_8_), channel_id=1, source_target_pairs={{0,64},{32,96},{64,0},{96,32},{1,65},{33,97},{65,1},{97,33},{2,66}... | collective-permute-start | bytes 196616 | tf_op jit(solution)/shard_map/ppermute | solution.py:44
  90.1 3.2 %shard_map.97 = (f32[2048,512]{1,0:T(8,128)S(1)}, f32[2048,512]{1,0:T(8,128)S(1)}) custom-call(s32[96]{0:T(128)S(1)} %dynamic-slice_bitcast_fusion.refs_0_.refs_1_, s32[2]{0:T(128)S(1)} %pad_add_fusion.refs_0_.refs_1_, bf16[4096,512]{1,0:T(8,128)(2,1)S(1)} %copy-done.1, ...), custom_call_target="tpu_custom_call", output_to_operand_aliasing={{0}: (6, {}), {1}: (7, {})} | custom-call | flops 1000 | bytes 1000 | tf_op jit(solution)/shard_map/pallas_call | solution.py:133
  94.6 3.1 %shard_map.98 = (f32[2048,512]{1,0:T(8,128)S(1)}, f32[2048,512]{1,0:T(8,128)S(1)}) custom-call(s32[96]{0:T(128)S(1)} %dynamic-slice_bitcast_fusion.refs_0_.refs_1_, s32[2]{0:T(128)S(1)} %pad_add_fusion.refs_0_.refs_1_, bf16[4096,512]{1,0:T(8,128)(2,1)S(1)} %copy-done.1, ...), custom_call_target="tpu_custom_call", output_to_operand_aliasing={{0}: (6, {}), {1}: (7, {})} | custom-call | flops 1000 | bytes 1000 | tf_op jit(solution)/shard_map/pallas_call | solution.py:133
  100.3 5.3 %shard_map.99.refs_1_.refs_2_.refs_8_ = f32[32,4096]{1,0:T(8,128)S(1)} custom-call(s32[2]{0:T(128)S(1)} %pad_add_fusion.refs_0_.refs_1_, f32[4,32,512]{2,1,0:T(8,128)S(1)} %constant_dynamic-update-slice_fusion.refs_1_, f32[4,32,512]{2,1,0:T(8,128)S(1)} %collective-permute-done.24.refs_2_, f32[2048,512]{1,0:T(8,128)S(1)} %get-tuple-element.78.refs_3_.refs_2_), custom_call_target="tpu_custom_call" | custom-call | flops 1000 | bytes 1000 | tf_op jit(solution)/shard_map/pallas_call | solution.py:133
  105.6 4.9 %shard_map.100 = (f32[32,512]{1,0:T(8,128)S(1)}, f32[32,512]{1,0:T(8,128)S(1)}, f32[2048,512]{1,0:T(8,128)S(1)}) custom-call(s32[2]{0:T(128)S(1)} %pad_add_fusion.refs_0_.refs_1_, f32[32,4096]{1,0:T(8,128)S(1)} %shard_map.99.refs_1_.refs_2_.refs_8_, f32[2048,512]{1,0:T(8,128)S(1)} %get-tuple-element.78.refs_3_.refs_2_, ...), custom_call_target="tpu_custom_call" | custom-call | flops 1000 | bytes 1000 | tf_op jit(solution)/shard_map/pallas_call | solution.py:133
  112.1 3.7 %shard_map.101 = (f32[32,512]{1,0:T(8,128)S(1)}, f32[32,512]{1,0:T(8,128)S(1)}) custom-call(s32[96]{0:T(128)S(1)} %dynamic-slice_bitcast_fusion.refs_0_.refs_1_, s32[2]{0:T(128)S(1)} %pad_add_fusion.refs_0_.refs_1_, f32[32,4096]{1,0:T(8,128)S(1)} %shard_map.99.refs_1_.refs_2_.refs_8_, f32[32,512]{1,0:T(8,128)S(1)} %get-tuple-element.84.refs_3_, ...), custom_call_target="tpu_custom_call" | custom-call | flops 1000 | bytes 1000 | tf_op jit(solution)/shard_map/pallas_call | solution.py:133
  116.0 2.9 %shard_map.102.refs_2_ = f32[2048,512]{1,0:T(8,128)S(1)} custom-call(s32[96]{0:T(128)S(1)} %dynamic-slice_bitcast_fusion.refs_0_.refs_1_, f32[2048,512]{1,0:T(8,128)S(1)} %get-tuple-element.80.refs_3_.refs_1_, bf16[4096,512]{1,0:T(8,128)(2,1)S(1)} %shard_map.79.refs_2_.refs_3_.refs_6_, bf16[512,2048]{1,0:T(8,128)(2,1)S(1)} %collective-permute-done.25.refs_7_.refs_3_.refs_6_, ...), custom_call_target="tpu_custom_call" | custom-call | flops 1000 | bytes 1000 | tf_op jit(solution)/shard_map/pallas_call | solution.py:133
  127.3 6.5 %shard_map.104 = (f32[4096,512]{1,0:T(8,128)}, f32[32,512]{1,0:T(8,128)}) custom-call(s32[2]{0:T(128)S(1)} %pad_add_fusion.refs_0_.refs_1_, s32[96]{0:T(128)S(1)} %dynamic-slice_bitcast_fusion.refs_0_.refs_1_, f32[2048,512]{1,0:T(8,128)S(1)} %get-tuple-element.78.refs_3_.refs_2_, f32[2048,512]{1,0:T(8,128)S(1)} %get-tuple-element.81.refs_3_, ...), custom_call_target="tpu_custom_call" | custom-call | flops 1000 | bytes 1000 | tf_op jit(solution)/shard_map/pallas_call | solution.py:133
  (85 shorter events, 47.2 us)
Async XLA Ops:
  4.6 9.2 %collective-permute-start.1 = (bf16[4096,512]{1,0:T(8,128)(2,1)}, bf16[4096,512]{1,0:T(8,128)(2,1)}, u32[]{:S(2)}, u32[]{:S(2)}) collective-permute-start(bf16[4096,512]{1,0:T(8,128)(2,1)} %refs_5_.3), channel_id=1, source_target_pairs={{0,1},{1,0},{2,3},{3,2},{4,5},{5,4},{6,7},{7,6},{8,9},{9,8},{10,11... | collective-permute-start | bytes 12582920 | tf_op jit(solution)/shard_map/ppermute | solution.py:40
  4.8 19.3 %collective-permute-start.2 = (bf16[256,2048]{1,0:T(8,128)(2,1)S(1)}, bf16[256,2048]{1,0:T(8,128)(2,1)S(1)}, u32[]{:S(2)}, u32[]{:S(2)}) collective-permute-start(bf16[256,2048]{1,0:T(8,128)(2,1)S(1)} %shard_map.77.refs_3_.refs_0_), channel_id=1, source_target_pairs={{0,24},{1,7},{2,26},{3,1},{4,28},{5,3},{6,30},{7,5},{8,0},{9,15},{... | collective-permute-start | bytes 3145736 | tf_op jit(solution)/shard_map/ppermute | solution.py:36
  7.7 18.5 %collective-permute-start.3 = (bf16[256,2048]{1,0:T(8,128)(2,1)S(1)}, bf16[256,2048]{1,0:T(8,128)(2,1)S(1)}, u32[]{:S(2)}, u32[]{:S(2)}) collective-permute-start(bf16[256,2048]{1,0:T(8,128)(2,1)S(1)} %shard_map.77.refs_3_.refs_0_), channel_id=1, source_target_pairs={{0,8},{1,3},{2,10},{3,5},{4,12},{5,7},{6,14},{7,1},{8,16},{9,11},{... | collective-permute-start | bytes 3145736 | tf_op jit(solution)/shard_map/ppermute | solution.py:36
  16.4 9.8 %collective-permute-start.5 = (f32[32,1024]{1,0:T(8,128)S(1)}, f32[32,1024]{1,0:T(8,128)S(1)}, u32[]{:S(2)}, u32[]{:S(2)}) collective-permute-start(f32[32,1024]{1,0:T(8,128)S(1)} %get-tuple-element.53), channel_id=1, source_target_pairs={{0,4},{1,17},{2,6},{3,19},{4,0},{5,21},{6,2},{7,23},{8,12},{9,25},... | collective-permute-start | bytes 393224 | tf_op jit(solution)/shard_map/ppermute | solution.py:56
  19.3 6.9 %collective-permute-start.6 = (f32[32,1024]{1,0:T(8,128)S(1)}, f32[32,1024]{1,0:T(8,128)S(1)}, u32[]{:S(2)}, u32[]{:S(2)}) collective-permute-start(f32[32,1024]{1,0:T(8,128)S(1)} %get-tuple-element.54), channel_id=1, source_target_pairs={{0,2},{1,9},{2,0},{3,11},{4,6},{5,13},{6,4},{7,15},{8,10},{9,1},{1... | collective-permute-start | bytes 393224 | tf_op jit(solution)/shard_map/ppermute | solution.py:56
  20.3 6.2 %collective-permute-start.7 = (f32[32,1024]{1,0:T(8,128)S(1)}, f32[32,1024]{1,0:T(8,128)S(1)}, u32[]{:S(2)}, u32[]{:S(2)}) collective-permute-start(f32[32,1024]{1,0:T(8,128)S(1)} %get-tuple-element.55), channel_id=1, source_target_pairs={{0,6},{1,25},{2,4},{3,27},{4,2},{5,29},{6,0},{7,31},{8,14},{9,17},... | collective-permute-start | bytes 393224 | tf_op jit(solution)/shard_map/ppermute | solution.py:56
  26.5 13.7 %collective-permute-start.8 = (bf16[128,2048]{1,0:T(8,128)(2,1)S(1)}, bf16[128,2048]{1,0:T(8,128)(2,1)S(1)}, u32[]{:S(2)}, u32[]{:S(2)}) collective-permute-start(bf16[128,2048]{1,0:T(8,128)(2,1)S(1)} %get-tuple-element.56.refs_2_), channel_id=1, source_target_pairs={{0,8},{1,3},{2,10},{3,5},{4,12},{5,7},{6,14},{7,1},{8,16},{9,11},{... | collective-permute-start | bytes 1572872 | tf_op jit(solution)/shard_map/ppermute | solution.py:36
  28.1 14.3 %collective-permute-start.9 = (bf16[128,2048]{1,0:T(8,128)(2,1)S(1)}, bf16[128,2048]{1,0:T(8,128)(2,1)S(1)}, u32[]{:S(2)}, u32[]{:S(2)}) collective-permute-start(bf16[128,2048]{1,0:T(8,128)(2,1)S(1)} %get-tuple-element.57), channel_id=1, source_target_pairs={{0,24},{1,7},{2,26},{3,1},{4,28},{5,3},{6,30},{7,5},{8,0},{9,15},{... | collective-permute-start | bytes 1572872 | tf_op jit(solution)/shard_map/ppermute | solution.py:36
  30.0 32.3 %collective-permute-start.16 = (bf16[512,2048]{1,0:T(8,128)(2,1)S(1)}, bf16[512,2048]{1,0:T(8,128)(2,1)S(1)}, u32[]{:S(2)}, u32[]{:S(2)}) collective-permute-start(bf16[512,2048]{1,0:T(8,128)(2,1)S(1)} %shard_map.83.refs_3_.refs_7_.refs_4_), channel_id=1, source_target_pairs={{0,6},{1,25},{2,0},{3,27},{4,2},{5,29},{6,4},{7,31},{8,14},{9,1},{... | collective-permute-start | bytes 6291464 | tf_op jit(solution)/shard_map/ppermute | solution.py:36
  32.8 29.5 %collective-permute-start.15 = (bf16[512,2048]{1,0:T(8,128)(2,1)S(1)}, bf16[512,2048]{1,0:T(8,128)(2,1)S(1)}, u32[]{:S(2)}, u32[]{:S(2)}) collective-permute-start(bf16[512,2048]{1,0:T(8,128)(2,1)S(1)} %shard_map.83.refs_3_.refs_7_.refs_4_), channel_id=1, source_target_pairs={{0,2},{1,9},{2,4},{3,11},{4,6},{5,13},{6,0},{7,15},{8,10},{9,17},{... | collective-permute-start | bytes 6291464 | tf_op jit(solution)/shard_map/ppermute | solution.py:36
  42.5 43.5 %collective-permute-start.21 = (bf16[512,2048]{1,0:T(8,128)(2,1)S(1)}, bf16[512,2048]{1,0:T(8,128)(2,1)S(1)}, u32[]{:S(2)}, u32[]{:S(2)}) collective-permute-start(bf16[512,2048]{1,0:T(8,128)(2,1)S(1)} %shard_map.85.refs_8_.refs_5_), channel_id=1, source_target_pairs={{0,6},{1,25},{2,0},{3,27},{4,2},{5,29},{6,4},{7,31},{8,14},{9,1},{... | collective-permute-start | bytes 6291464 | tf_op jit(solution)/shard_map/ppermute | solution.py:36
  45.2 44.9 %collective-permute-start.10 = (bf16[512,2048]{1,0:T(8,128)(2,1)S(1)}, bf16[512,2048]{1,0:T(8,128)(2,1)S(1)}, u32[]{:S(2)}, u32[]{:S(2)}) collective-permute-start(bf16[512,2048]{1,0:T(8,128)(2,1)S(1)} %shard_map.85.refs_8_.refs_5_), channel_id=1, source_target_pairs={{0,2},{1,9},{2,4},{3,11},{4,6},{5,13},{6,0},{7,15},{8,10},{9,17},{... | collective-permute-start | bytes 6291464 | tf_op jit(solution)/shard_map/ppermute | solution.py:36
  48.1 5.8 %collective-permute-start.12 = (f32[2,32,512]{2,1,0:T(8,128)S(1)}, f32[2,32,512]{2,1,0:T(8,128)S(1)}, u32[]{:S(2)}, u32[]{:S(2)}) collective-permute-start(f32[2,32,512]{2,1,0:T(8,128)S(1)} %get-tuple-element.60.refs_7_), channel_id=1, source_target_pairs={{0,32},{32,0},{64,96},{96,64},{1,33},{33,1},{65,97},{97,65},{2,34}... | collective-permute-start | bytes 393224 | tf_op jit(solution)/shard_map/ppermute | solution.py:44
  53.9 7.9 %collective-permute-start.13 = (f32[32,512]{1,0:T(8,128)S(1)}, f32[32,512]{1,0:T(8,128)S(1)}, u32[]{:S(2)}, u32[]{:S(2)}) collective-permute-start(f32[32,512]{1,0:T(8,128)S(1)} %get-tuple-element.63.refs_9_), channel_id=1, source_target_pairs={{0,64},{32,96},{64,0},{96,32},{1,65},{33,97},{65,1},{97,33},{2,66}... | collective-permute-start | bytes 196616 | tf_op jit(solution)/shard_map/ppermute | solution.py:44
  61.8 5.1 %collective-permute-start.14 = (f32[32,512]{1,0:T(8,128)S(1)}, f32[32,512]{1,0:T(8,128)S(1)}, u32[]{:S(2)}, u32[]{:S(2)}) collective-permute-start(f32[32,512]{1,0:T(8,128)S(1)} %shard_map.90.refs_8_.refs_0_), channel_id=1, source_target_pairs={{0,8},{1,3},{2,10},{3,1},{4,12},{5,7},{6,14},{7,5},{8,0},{9,11},{1... | collective-permute-start | bytes 196616 | tf_op jit(solution)/shard_map/ppermute | solution.py:56
  66.9 6.6 %collective-permute-start.17 = (f32[32,512]{1,0:T(8,128)S(1)}, f32[32,512]{1,0:T(8,128)S(1)}, u32[]{:S(2)}, u32[]{:S(2)}) collective-permute-start(f32[32,512]{1,0:T(8,128)S(1)} %shard_map.92.refs_8_.refs_0_), channel_id=1, source_target_pairs={{0,16},{1,5},{2,18},{3,7},{4,20},{5,1},{6,22},{7,3},{8,24},{9,13},... | collective-permute-start | bytes 196616 | tf_op jit(solution)/shard_map/ppermute | solution.py:56
  79.9 6.1 %collective-permute-start.20 = (f32[32,512]{1,0:T(8,128)S(1)}, f32[32,512]{1,0:T(8,128)S(1)}, u32[]{:S(2)}, u32[]{:S(2)}) collective-permute-start(f32[32,512]{1,0:T(8,128)S(1)} %shard_map.95.refs_0_), channel_id=1, source_target_pairs={{0,16},{1,5},{2,18},{3,7},{4,20},{5,1},{6,22},{7,3},{8,24},{9,13},... | collective-permute-start | bytes 196616 | tf_op jit(solution)/shard_map/ppermute | solution.py:56
  83.2 27.3 %collective-permute-start.25 = (bf16[512,2048]{1,0:T(8,128)(2,1)S(1)}, bf16[512,2048]{1,0:T(8,128)(2,1)S(1)}, u32[]{:S(2)}, u32[]{:S(2)}) collective-permute-start(bf16[512,2048]{1,0:T(8,128)(2,1)S(1)} %collective-permute-done.15.refs_4_), channel_id=1, source_target_pairs={{0,2},{1,9},{2,4},{3,11},{4,6},{5,13},{6,0},{7,15},{8,10},{9,17},{... | collective-permute-start | bytes 6291464 | tf_op jit(solution)/shard_map/ppermute | solution.py:36
  86.0 26.1 %collective-permute-start.26 = (bf16[512,2048]{1,0:T(8,128)(2,1)S(1)}, bf16[512,2048]{1,0:T(8,128)(2,1)S(1)}, u32[]{:S(2)}, u32[]{:S(2)}) collective-permute-start(bf16[512,2048]{1,0:T(8,128)(2,1)S(1)} %collective-permute-done.21.refs_5_), channel_id=1, source_target_pairs={{0,6},{1,25},{2,0},{3,27},{4,2},{5,29},{6,4},{7,31},{8,14},{9,1},{... | collective-permute-start | bytes 6291464 | tf_op jit(solution)/shard_map/ppermute | solution.py:36
  87.6 5.8 %collective-permute-start.22 = (f32[32,512]{1,0:T(8,128)S(1)}, f32[32,512]{1,0:T(8,128)S(1)}, u32[]{:S(2)}, u32[]{:S(2)}) collective-permute-start(f32[32,512]{1,0:T(8,128)S(1)} %shard_map.96.refs_8_), channel_id=1, source_target_pairs={{0,64},{32,96},{64,0},{96,32},{1,65},{33,97},{65,1},{97,33},{2,66}... | collective-permute-start | bytes 196616 | tf_op jit(solution)/shard_map/ppermute | solution.py:44
  93.4 5.0 %collective-permute-start.23 = (f32[2,32,512]{2,1,0:T(8,128)S(1)}, f32[2,32,512]{2,1,0:T(8,128)S(1)}, u32[]{:S(2)}, u32[]{:S(2)}) collective-permute-start(f32[2,32,512]{2,1,0:T(8,128)S(1)} %pad_maximum_fusion.refs_8_), channel_id=1, source_target_pairs={{0,32},{32,0},{64,96},{96,64},{1,33},{33,1},{65,97},{97,65},{2,34}... | collective-permute-start | bytes 393224 | tf_op jit(solution)/shard_map/ppermute | solution.py:44
  118.9 8.4 %collective-permute-start.28 = (f32[2048,512]{1,0:T(8,128)S(1)}, f32[2048,512]{1,0:T(8,128)S(1)}, u32[]{:S(2)}, u32[]{:S(2)}) collective-permute-start(f32[2048,512]{1,0:T(8,128)S(1)} %shard_map.102.refs_2_), channel_id=1, source_target_pairs={{0,1},{1,0},{2,3},{3,2},{4,5},{5,4},{6,7},{7,6},{8,9},{9,8},{10,11... | collective-permute-start | bytes 12582920 | tf_op jit(solution)/shard_map/ppermute | solution.py:40
  119.5 6.4 %collective-permute-start.29 = (f32[32,512]{1,0:T(8,128)S(1)}, f32[32,512]{1,0:T(8,128)S(1)}, u32[]{:S(2)}, u32[]{:S(2)}) collective-permute-start(f32[32,512]{1,0:T(8,128)S(1)} %shard_map.103.refs_9_), channel_id=1, source_target_pairs={{0,64},{32,96},{64,0},{96,32},{1,65},{33,97},{65,1},{97,33},{2,66}... | collective-permute-start | bytes 196616 | tf_op jit(solution)/shard_map/ppermute | solution.py:48
  121.8 5.5 %collective-permute-start.30 = (f32[32,512]{1,0:T(8,128)S(1)}, f32[32,512]{1,0:T(8,128)S(1)}, u32[]{:S(2)}, u32[]{:S(2)}) collective-permute-start(f32[32,512]{1,0:T(8,128)S(1)} %shard_map.103.refs_9_), channel_id=1, source_target_pairs={{0,32},{32,64},{64,96},{96,0},{1,33},{33,65},{65,97},{97,1},{2,34}... | collective-permute-start | bytes 196616 | tf_op jit(solution)/shard_map/ppermute | solution.py:48
  (13 other events, 44.2 us)

commit v5 on v4

--- a/solution.py
+++ b/solution.py
@@ -468,14 +468,15 @@
 def final_kernel(starts, pos_ref, off_ref, m_ref, e_ref, got_ref, g_ref, *refs):
     n, step = len(starts), H // N
     xs, refs = refs[:n], refs[n:]
-    p_ref, q0, q1, q2, q3, out_ref, q_ref, made_ref, out_sems = refs
+    p_ref, q0, q1, q2, q3, out_ref, q_ref, p_out_ref, made_ref, out_sems = refs
     c = pos_ref[0]
     q = ((q0[...] + q1[...]) + (q2[...] + q3[...])) * 0.25
     q_ref[...] = q
     s1, s2 = split(-q, 2)
     low = jnp.concatenate([s1, s2, s1], 0)
     rows = jnp.concatenate([block_rows(off_ref, g_ref, starts), low], 0)
-    sent = []
+    sent = [pltpu.make_async_copy(p_ref, p_out_ref, out_sems.at[2 * N])]
+    sent[0].start()
     for k in range(2 * N):
         own, at = k < N, slice(k % N * step, (k % N + 1) * step)
         first = pl.multiple_of((c if own else 1 - c) * H + k % N * step, step)
@@ -496,12 +497,12 @@
     n = len(groups)
     return run(
         functools.partial(final_kernel, [start for start, _ in groups]),
-        [shape((D, F)), shape((R, F))],
+        [shape((D, F)), shape((R, F)), shape((R, D))],
         [pos, off, own, e, got, g] + [x for _, x in groups] + [p, *q],
         [SMEM, SMEM] + [WHOLE] * (n + 5 + N),
-        [HBM, WHOLE],
+        [HBM, WHOLE, HBM],
         vmem=24,
-        scratch_shapes=[pltpu.VMEM((D, F), F32), pltpu.SemaphoreType.DMA((2 * N,))],
+        scratch_shapes=[pltpu.VMEM((D, F), F32), pltpu.SemaphoreType.DMA((2 * N + 1,))],
     )
 
 
@@ -566,16 +567,19 @@
     stack = jnp.concatenate([later(pair, acc[0]), got])
     p = basis(pos, stack, swap(stack), (acc[0],))
 
-    last = [(24, later(o0, p)), (28, later(o1, p))]
+    o0 = later(o0, p)
     qp, q_send, e_rest = right_part(pos, p, acc, e, ())
-    qp, q_send = right_rest(off, pos, p, qp, q_send, g, g_other, last)
+    qp, q_send = right_rest(off, pos, p, qp, q_send, g, g_other, [(24, o0)])
+    o1 = later(o1, qp)
+    last = [(24, o0), (28, o1)]
+    qp, q_send = right_rest(off, pos, p, qp, q_send, g, g_other, last[1:])
     q_got = swap(q_send)
     out = last_other(off, acc[1], last, g_other, (q_send,))
     (qp,) = add([qp], [q_got], (out,))
     out = swap(later(out, qp))
     qs = (qp, around_z(qp, 2), around_z(qp, 1), around_z(qp, -1))
-    err, qf = final(off, pos, acc[0], e_rest, out, last, g, p, qs)
-    return err[None], p.T, qf.T
+    err, qf, pf = final(off, pos, acc[0], e_rest, out, last, g, p, qs)
+    return err[None], pf.T, qf.T
 
 
 def solution(mesh):

time: 135 us -> 134 us (level)
    ppermute x10, waiting for transfers between devices: 9.63 us -> 8.04 us  [hop(): return lax.ppermute(array, 'tensor', pairs)]
    unnamed x12 -> x11, local copies, waits for them, and re-layouts: 5.07 us -> 4.27 us
    pallas_call x29 -> x30, Pallas kernels: 57.7 us -> 57.9 us  [run(): pl.pallas_call(wrapped, out_shape=out_shape, compiler_params=options, **kw)]
  transfers between devices with their start and end apart: 32 -> 32, of which waited for: 16 -> 16; matrix products, arithmetic and copies ran while one was open for 1% -> 1% of each run, Pallas kernels for 35% -> 37%
where the time goes in v5:
time: 134 us; the launch traced here: 133 us
  Pallas kernels  57.9 us (43%)
  starting transfers between devices  43 us (32%)
  waiting for transfers between devices  25.6 us (19%)
  local copies, waits for them, and re-layouts  4.98 us (4%)
    pallas_call x30, Pallas kernels, run(): pl.pallas_call(wrapped, out_shape=out_shape, compiler_params=options, **kw)  57.9 us
    ppermute x10, starting transfers between devices, hop(): return lax.ppermute(array, 'tensor', pairs)  13.2 us
    ppermute x7, starting transfers between devices, twin(): return lax.ppermute(array, 'tensor', pairs)  12.6 us
    ppermute x4, starting transfers between devices, hop_z(): return lax.ppermute(array, 'dp', [(i, i ^ bit) for i in range(N)])  9.66 us
    ppermute x7, waiting for transfers between devices, twin(): return lax.ppermute(array, 'tensor', pairs)  8.35 us
    ppermute x10, waiting for transfers between devices, hop(): return lax.ppermute(array, 'tensor', pairs)  8.04 us
    ppermute x8, waiting for transfers between devices, swap(): return lax.ppermute(array, 'tensor', [(i, i ^ 1) for i in range(2 * N * N)])  6.2 us
    ppermute x3, starting transfers between devices, around_z(): return lax.ppermute(array, 'dp', [(i, (i + d) % N) for i in range(N)])  5.71 us
  transfers between devices with their start and end apart: 32, of which 16 were waited for; matrix products, arithmetic and copies ran while one was open for 1% of the time, Pallas kernels for 37%

profile of v5, /device:TPU:0, one launch (start us, length us, event | category | flops | bytes accessed | tf_op | source)
XLA Modules:
  0.0 132.7 jit_solution(308853982869448345)
XLA Ops:
  4.8 2.8 %collective-permute-start.2 = (bf16[256,2048]{1,0:T(8,128)(2,1)S(1)}, bf16[256,2048]{1,0:T(8,128)(2,1)S(1)}, u32[]{:S(2)}, u32[]{:S(2)}) collective-permute-start(bf16[256,2048]{1,0:T(8,128)(2,1)S(1)} %shard_map.77.refs_3_.refs_0_), channel_id=1, source_target_pairs={{0,24},{1,7},{2,26},{3,1},{4,28},{5,3},{6,30},{7,5},{8,0},{9,15},{... | collective-permute-start | bytes 3145736 | tf_op jit(solution)/shard_map/ppermute | solution.py:36
  16.4 2.9 %collective-permute-start.5 = (f32[32,1024]{1,0:T(8,128)S(1)}, f32[32,1024]{1,0:T(8,128)S(1)}, u32[]{:S(2)}, u32[]{:S(2)}) collective-permute-start(f32[32,1024]{1,0:T(8,128)S(1)} %get-tuple-element.56), channel_id=1, source_target_pairs={{0,4},{1,17},{2,6},{3,19},{4,0},{5,21},{6,2},{7,23},{8,12},{9,25},... | collective-permute-start | bytes 393224 | tf_op jit(solution)/shard_map/ppermute | solution.py:56
  20.5 3.6 %shard_map.81.refs_2_ = f32[4,32,512]{2,1,0:T(8,128)S(1)} custom-call(s32[2]{0:T(128)S(1)} %pad_add_fusion.refs_0_.refs_1_, f32[32,512]{1,0:T(8,128)S(1)} %bitcast.12, f32[4096,512]{1,0:T(8,128)} %bitcast.15, f32[32,1024]{1,0:T(8,128)S(1)} %get-tuple-element.55.refs_3_.refs_1_), custom_call_target="tpu_custom_call" | custom-call | flops 1000 | bytes 1000 | tf_op jit(solution)/shard_map/pallas_call | solution.py:133
  30.0 2.9 %collective-permute-start.16 = (bf16[512,2048]{1,0:T(8,128)(2,1)S(1)}, bf16[512,2048]{1,0:T(8,128)(2,1)S(1)}, u32[]{:S(2)}, u32[]{:S(2)}) collective-permute-start(bf16[512,2048]{1,0:T(8,128)(2,1)S(1)} %shard_map.83.refs_3_.refs_7_.refs_4_), channel_id=1, source_target_pairs={{0,6},{1,25},{2,0},{3,27},{4,2},{5,29},{6,4},{7,31},{8,14},{9,1},{... | collective-permute-start | bytes 6291464 | tf_op jit(solution)/shard_map/ppermute | solution.py:36
  32.8 3.6 %shard_map.84.refs_3_.refs_5_ = f32[4,32,512]{2,1,0:T(8,128)S(1)} custom-call(s32[2]{0:T(128)S(1)} %pad_add_fusion.refs_0_.refs_1_, f32[32,512]{1,0:T(8,128)S(1)} %bitcast.13, f32[4096,512]{1,0:T(8,128)} %bitcast.16, bf16[512,2048]{1,0:T(8,128)(2,1)S(1)} %shard_map.83.refs_3_.refs_7_.refs_4_), custom_call_target="tpu_custom_call" | custom-call | flops 1000 | bytes 1000 | tf_op jit(solution)/shard_map/pallas_call | solution.py:133
  36.4 3.8 %collective-permute-done.8.refs_1_ = bf16[128,2048]{1,0:T(8,128)(2,1)S(1)} collective-permute-done((bf16[128,2048]{1,0:T(8,128)(2,1)S(1)}, bf16[128,2048]{1,0:T(8,128)(2,1)S(1)}, u32[]{:S(2)}, u32[]{:S(2)}) %collective-permute-start.8) | collective-permute-done | bytes 524320 | tf_op jit(solution)/shard_map/ppermute | solution.py:36
  42.5 2.7 %collective-permute-start.21 = (bf16[512,2048]{1,0:T(8,128)(2,1)S(1)}, bf16[512,2048]{1,0:T(8,128)(2,1)S(1)}, u32[]{:S(2)}, u32[]{:S(2)}) collective-permute-start(bf16[512,2048]{1,0:T(8,128)(2,1)S(1)} %shard_map.85.refs_8_.refs_5_), channel_id=1, source_target_pairs={{0,6},{1,25},{2,0},{3,27},{4,2},{5,29},{6,4},{7,31},{8,14},{9,1},{... | collective-permute-start | bytes 6291464 | tf_op jit(solution)/shard_map/ppermute | solution.py:36
  50.0 3.8 %shard_map.87 = (f32[2048,512]{1,0:T(8,128)S(1)}, f32[2048,512]{1,0:T(8,128)S(1)}) custom-call(s32[96]{0:T(128)S(1)} %dynamic-slice_bitcast_fusion.refs_0_.refs_1_, s32[2]{0:T(128)S(1)} %pad_add_fusion.refs_0_.refs_1_, bf16[4096,512]{1,0:T(8,128)(2,1)S(1)} %copy-done.1, bf16[4096,512]{1,0:T(8,128)(2,1)S(1)} %shard_map.79.refs_2_.refs_3_.refs_6_, ...), custom_call_target="tpu_custom_call" | custom-call | flops 1000 | bytes 1000 | tf_op jit(solution)/shard_map/pallas_call | solution.py:133
  53.9 3.9 %collective-permute-start.13 = (f32[32,512]{1,0:T(8,128)S(1)}, f32[32,512]{1,0:T(8,128)S(1)}, u32[]{:S(2)}, u32[]{:S(2)}) collective-permute-start(f32[32,512]{1,0:T(8,128)S(1)} %get-tuple-element.66.refs_9_), channel_id=1, source_target_pairs={{0,64},{32,96},{64,0},{96,32},{1,65},{33,97},{65,1},{97,33},{2,66}... | collective-permute-start | bytes 196616 | tf_op jit(solution)/shard_map/ppermute | solution.py:44
  57.8 3.9 %shard_map.89 = (f32[2048,512]{1,0:T(8,128)S(1)}, f32[2048,512]{1,0:T(8,128)S(1)}) custom-call(s32[96]{0:T(128)S(1)} %dynamic-slice_bitcast_fusion.refs_0_.refs_1_, s32[2]{0:T(128)S(1)} %pad_add_fusion.refs_0_.refs_1_, bf16[4096,512]{1,0:T(8,128)(2,1)S(1)} %copy-done.1, ...), custom_call_target="tpu_custom_call", output_to_operand_aliasing={{0}: (7, {}), {1}: (8, {})} | custom-call | flops 1000 | bytes 1000 | tf_op jit(solution)/shard_map/pallas_call | solution.py:133
  62.3 3.1 %shard_map.91 = (f32[2048,512]{1,0:T(8,128)S(1)}, f32[2048,512]{1,0:T(8,128)S(1)}) custom-call(s32[96]{0:T(128)S(1)} %dynamic-slice_bitcast_fusion.refs_0_.refs_1_, s32[2]{0:T(128)S(1)} %pad_add_fusion.refs_0_.refs_1_, bf16[4096,512]{1,0:T(8,128)(2,1)S(1)} %copy-done.1, ...), custom_call_target="tpu_custom_call", output_to_operand_aliasing={{0}: (6, {}), {1}: (7, {})} | custom-call | flops 1000 | bytes 1000 | tf_op jit(solution)/shard_map/pallas_call | solution.py:133
  66.9 3.4 %collective-permute-start.17 = (f32[32,512]{1,0:T(8,128)S(1)}, f32[32,512]{1,0:T(8,128)S(1)}, u32[]{:S(2)}, u32[]{:S(2)}) collective-permute-start(f32[32,512]{1,0:T(8,128)S(1)} %shard_map.92.refs_8_.refs_0_), channel_id=1, source_target_pairs={{0,16},{1,5},{2,18},{3,7},{4,20},{5,1},{6,22},{7,3},{8,24},{9,13},... | collective-permute-start | bytes 196616 | tf_op jit(solution)/shard_map/ppermute | solution.py:56
  70.3 3.1 %shard_map.93 = (f32[2048,512]{1,0:T(8,128)S(1)}, f32[2048,512]{1,0:T(8,128)S(1)}) custom-call(s32[96]{0:T(128)S(1)} %dynamic-slice_bitcast_fusion.refs_0_.refs_1_, s32[2]{0:T(128)S(1)} %pad_add_fusion.refs_0_.refs_1_, bf16[4096,512]{1,0:T(8,128)(2,1)S(1)} %copy-done.1, ...), custom_call_target="tpu_custom_call", output_to_operand_aliasing={{0}: (6, {}), {1}: (7, {})} | custom-call | flops 1000 | bytes 1000 | tf_op jit(solution)/shard_map/pallas_call | solution.py:133
  76.0 3.9 %collective-permute-done.19.refs_1_ = f32[32,512]{1,0:T(8,128)S(1)} collective-permute-done((f32[32,512]{1,0:T(8,128)S(1)}, f32[32,512]{1,0:T(8,128)S(1)}, u32[]{:S(2)}, u32[]{:S(2)}) %collective-permute-start.19) | collective-permute-done | bytes 65568 | tf_op jit(solution)/shard_map/ppermute | solution.py:56
  79.9 3.4 %collective-permute-start.20 = (f32[32,512]{1,0:T(8,128)S(1)}, f32[32,512]{1,0:T(8,128)S(1)}, u32[]{:S(2)}, u32[]{:S(2)}) collective-permute-start(f32[32,512]{1,0:T(8,128)S(1)} %shard_map.95.refs_0_), channel_id=1, source_target_pairs={{0,16},{1,5},{2,18},{3,7},{4,20},{5,1},{6,22},{7,3},{8,24},{9,13},... | collective-permute-start | bytes 196616 | tf_op jit(solution)/shard_map/ppermute | solution.py:56
  83.3 2.7 %collective-permute-done.20.refs_1_ = f32[32,512]{1,0:T(8,128)S(1)} collective-permute-done((f32[32,512]{1,0:T(8,128)S(1)}, f32[32,512]{1,0:T(8,128)S(1)}, u32[]{:S(2)}, u32[]{:S(2)}) %collective-permute-start.20) | collective-permute-done | bytes 65568 | tf_op jit(solution)/shard_map/ppermute | solution.py:56
  87.6 2.5 %collective-permute-start.22 = (f32[32,512]{1,0:T(8,128)S(1)}, f32[32,512]{1,0:T(8,128)S(1)}, u32[]{:S(2)}, u32[]{:S(2)}) collective-permute-start(f32[32,512]{1,0:T(8,128)S(1)} %shard_map.96.refs_8_), channel_id=1, source_target_pairs={{0,64},{32,96},{64,0},{96,32},{1,65},{33,97},{65,1},{97,33},{2,66}... | collective-permute-start | bytes 196616 | tf_op jit(solution)/shard_map/ppermute | solution.py:44
  90.1 3.1 %shard_map.97 = (f32[2048,512]{1,0:T(8,128)S(1)}, f32[2048,512]{1,0:T(8,128)S(1)}) custom-call(s32[96]{0:T(128)S(1)} %dynamic-slice_bitcast_fusion.refs_0_.refs_1_, s32[2]{0:T(128)S(1)} %pad_add_fusion.refs_0_.refs_1_, bf16[4096,512]{1,0:T(8,128)(2,1)S(1)} %copy-done.1, ...), custom_call_target="tpu_custom_call", output_to_operand_aliasing={{0}: (6, {}), {1}: (7, {})} | custom-call | flops 1000 | bytes 1000 | tf_op jit(solution)/shard_map/pallas_call | solution.py:133
  94.7 3.1 %shard_map.98 = (f32[2048,512]{1,0:T(8,128)S(1)}, f32[2048,512]{1,0:T(8,128)S(1)}) custom-call(s32[96]{0:T(128)S(1)} %dynamic-slice_bitcast_fusion.refs_0_.refs_1_, s32[2]{0:T(128)S(1)} %pad_add_fusion.refs_0_.refs_1_, bf16[4096,512]{1,0:T(8,128)(2,1)S(1)} %copy-done.1, ...), custom_call_target="tpu_custom_call", output_to_operand_aliasing={{0}: (6, {}), {1}: (7, {})} | custom-call | flops 1000 | bytes 1000 | tf_op jit(solution)/shard_map/pallas_call | solution.py:133
  100.3 5.3 %shard_map.99.refs_1_.refs_2_.refs_8_ = f32[32,4096]{1,0:T(8,128)S(1)} custom-call(s32[2]{0:T(128)S(1)} %pad_add_fusion.refs_0_.refs_1_, f32[4,32,512]{2,1,0:T(8,128)S(1)} %constant_dynamic-update-slice_fusion.refs_1_, f32[4,32,512]{2,1,0:T(8,128)S(1)} %collective-permute-done.24.refs_2_, f32[2048,512]{1,0:T(8,128)S(1)} %get-tuple-element.81.refs_3_.refs_2_), custom_call_target="tpu_custom_call" | custom-call | flops 1000 | bytes 1000 | tf_op jit(solution)/shard_map/pallas_call | solution.py:133
  105.6 4.9 %shard_map.100 = (f32[32,512]{1,0:T(8,128)S(1)}, f32[32,512]{1,0:T(8,128)S(1)}, f32[2048,512]{1,0:T(8,128)S(1)}) custom-call(s32[2]{0:T(128)S(1)} %pad_add_fusion.refs_0_.refs_1_, f32[32,4096]{1,0:T(8,128)S(1)} %shard_map.99.refs_1_.refs_2_.refs_8_, f32[2048,512]{1,0:T(8,128)S(1)} %get-tuple-element.81.refs_3_.refs_2_, ...), custom_call_target="tpu_custom_call" | custom-call | flops 1000 | bytes 1000 | tf_op jit(solution)/shard_map/pallas_call | solution.py:133
  114.7 2.9 %shard_map.103.refs_2_ = f32[2048,512]{1,0:T(8,128)S(1)} custom-call(s32[96]{0:T(128)S(1)} %dynamic-slice_bitcast_fusion.refs_0_.refs_1_, f32[2048,512]{1,0:T(8,128)S(1)} %get-tuple-element.83.refs_3_.refs_1_, bf16[4096,512]{1,0:T(8,128)(2,1)S(1)} %shard_map.79.refs_2_.refs_3_.refs_6_, bf16[512,2048]{1,0:T(8,128)(2,1)S(1)} %collective-permute-done.25.refs_7_.refs_3_.refs_6_, ...), custom_call_target="tpu_custom_call" | custom-call | flops 1000 | bytes 1000 | tf_op jit(solution)/shard_map/pallas_call | solution.py:133
  121.1 2.7 %collective-permute-start.31 = (f32[32,512]{1,0:T(8,128)S(1)}, f32[32,512]{1,0:T(8,128)S(1)}, u32[]{:S(2)}, u32[]{:S(2)}) collective-permute-start(f32[32,512]{1,0:T(8,128)S(1)} %shard_map.104.refs_9_), channel_id=1, source_target_pairs={{0,96},{32,0},{64,32},{96,64},{1,97},{33,1},{65,33},{97,65},{2,98}... | collective-permute-start | bytes 196616 | tf_op jit(solution)/shard_map/ppermute | solution.py:48
  126.1 6.4 %shard_map.105 = (f32[4096,512]{1,0:T(8,128)}, f32[32,512]{1,0:T(8,128)}, f32[32,4096]{1,0:T(8,128)}) custom-call(s32[2]{0:T(128)S(1)} %pad_add_fusion.refs_0_.refs_1_, s32[96]{0:T(128)S(1)} %dynamic-slice_bitcast_fusion.refs_0_.refs_1_, f32[2048,512]{1,0:T(8,128)S(1)} %get-tuple-element.81.refs_3_.refs_2_, f32[2048,512]{1,0:T(8,128)S(1)} %get-tuple-element.84.refs_3_, ...), custom_call_target="tpu_custom_call" | custom-call | flops 1000 | bytes 1000 | tf_op jit(solution)/shard_map/pallas_call | solution.py:133
  (85 shorter events, 46.9 us)
Async XLA Ops:
  4.6 9.2 %collective-permute-start.1 = (bf16[4096,512]{1,0:T(8,128)(2,1)}, bf16[4096,512]{1,0:T(8,128)(2,1)}, u32[]{:S(2)}, u32[]{:S(2)}) collective-permute-start(bf16[4096,512]{1,0:T(8,128)(2,1)} %refs_5_.5), channel_id=1, source_target_pairs={{0,1},{1,0},{2,3},{3,2},{4,5},{5,4},{6,7},{7,6},{8,9},{9,8},{10,11... | collective-permute-start | bytes 12582920 | tf_op jit(solution)/shard_map/ppermute | solution.py:40
  4.8 19.3 %collective-permute-start.2 = (bf16[256,2048]{1,0:T(8,128)(2,1)S(1)}, bf16[256,2048]{1,0:T(8,128)(2,1)S(1)}, u32[]{:S(2)}, u32[]{:S(2)}) collective-permute-start(bf16[256,2048]{1,0:T(8,128)(2,1)S(1)} %shard_map.77.refs_3_.refs_0_), channel_id=1, source_target_pairs={{0,24},{1,7},{2,26},{3,1},{4,28},{5,3},{6,30},{7,5},{8,0},{9,15},{... | collective-permute-start | bytes 3145736 | tf_op jit(solution)/shard_map/ppermute | solution.py:36
  7.7 18.5 %collective-permute-start.3 = (bf16[256,2048]{1,0:T(8,128)(2,1)S(1)}, bf16[256,2048]{1,0:T(8,128)(2,1)S(1)}, u32[]{:S(2)}, u32[]{:S(2)}) collective-permute-start(bf16[256,2048]{1,0:T(8,128)(2,1)S(1)} %shard_map.77.refs_3_.refs_0_), channel_id=1, source_target_pairs={{0,8},{1,3},{2,10},{3,5},{4,12},{5,7},{6,14},{7,1},{8,16},{9,11},{... | collective-permute-start | bytes 3145736 | tf_op jit(solution)/shard_map/ppermute | solution.py:36
  16.4 9.8 %collective-permute-start.5 = (f32[32,1024]{1,0:T(8,128)S(1)}, f32[32,1024]{1,0:T(8,128)S(1)}, u32[]{:S(2)}, u32[]{:S(2)}) collective-permute-start(f32[32,1024]{1,0:T(8,128)S(1)} %get-tuple-element.56), channel_id=1, source_target_pairs={{0,4},{1,17},{2,6},{3,19},{4,0},{5,21},{6,2},{7,23},{8,12},{9,25},... | collective-permute-start | bytes 393224 | tf_op jit(solution)/shard_map/ppermute | solution.py:56
  19.3 6.9 %collective-permute-start.6 = (f32[32,1024]{1,0:T(8,128)S(1)}, f32[32,1024]{1,0:T(8,128)S(1)}, u32[]{:S(2)}, u32[]{:S(2)}) collective-permute-start(f32[32,1024]{1,0:T(8,128)S(1)} %get-tuple-element.57), channel_id=1, source_target_pairs={{0,2},{1,9},{2,0},{3,11},{4,6},{5,13},{6,4},{7,15},{8,10},{9,1},{1... | collective-permute-start | bytes 393224 | tf_op jit(solution)/shard_map/ppermute | solution.py:56
  20.3 6.2 %collective-permute-start.7 = (f32[32,1024]{1,0:T(8,128)S(1)}, f32[32,1024]{1,0:T(8,128)S(1)}, u32[]{:S(2)}, u32[]{:S(2)}) collective-permute-start(f32[32,1024]{1,0:T(8,128)S(1)} %get-tuple-element.58), channel_id=1, source_target_pairs={{0,6},{1,25},{2,4},{3,27},{4,2},{5,29},{6,0},{7,31},{8,14},{9,17},... | collective-permute-start | bytes 393224 | tf_op jit(solution)/shard_map/ppermute | solution.py:56
  26.5 13.7 %collective-permute-start.8 = (bf16[128,2048]{1,0:T(8,128)(2,1)S(1)}, bf16[128,2048]{1,0:T(8,128)(2,1)S(1)}, u32[]{:S(2)}, u32[]{:S(2)}) collective-permute-start(bf16[128,2048]{1,0:T(8,128)(2,1)S(1)} %get-tuple-element.59.refs_2_), channel_id=1, source_target_pairs={{0,8},{1,3},{2,10},{3,5},{4,12},{5,7},{6,14},{7,1},{8,16},{9,11},{... | collective-permute-start | bytes 1572872 | tf_op jit(solution)/shard_map/ppermute | solution.py:36
  28.1 14.3 %collective-permute-start.9 = (bf16[128,2048]{1,0:T(8,128)(2,1)S(1)}, bf16[128,2048]{1,0:T(8,128)(2,1)S(1)}, u32[]{:S(2)}, u32[]{:S(2)}) collective-permute-start(bf16[128,2048]{1,0:T(8,128)(2,1)S(1)} %get-tuple-element.60), channel_id=1, source_target_pairs={{0,24},{1,7},{2,26},{3,1},{4,28},{5,3},{6,30},{7,5},{8,0},{9,15},{... | collective-permute-start | bytes 1572872 | tf_op jit(solution)/shard_map/ppermute | solution.py:36
  30.0 32.3 %collective-permute-start.16 = (bf16[512,2048]{1,0:T(8,128)(2,1)S(1)}, bf16[512,2048]{1,0:T(8,128)(2,1)S(1)}, u32[]{:S(2)}, u32[]{:S(2)}) collective-permute-start(bf16[512,2048]{1,0:T(8,128)(2,1)S(1)} %shard_map.83.refs_3_.refs_7_.refs_4_), channel_id=1, source_target_pairs={{0,6},{1,25},{2,0},{3,27},{4,2},{5,29},{6,4},{7,31},{8,14},{9,1},{... | collective-permute-start | bytes 6291464 | tf_op jit(solution)/shard_map/ppermute | solution.py:36
  32.8 29.5 %collective-permute-start.15 = (bf16[512,2048]{1,0:T(8,128)(2,1)S(1)}, bf16[512,2048]{1,0:T(8,128)(2,1)S(1)}, u32[]{:S(2)}, u32[]{:S(2)}) collective-permute-start(bf16[512,2048]{1,0:T(8,128)(2,1)S(1)} %shard_map.83.refs_3_.refs_7_.refs_4_), channel_id=1, source_target_pairs={{0,2},{1,9},{2,4},{3,11},{4,6},{5,13},{6,0},{7,15},{8,10},{9,17},{... | collective-permute-start | bytes 6291464 | tf_op jit(solution)/shard_map/ppermute | solution.py:36
  42.5 43.5 %collective-permute-start.21 = (bf16[512,2048]{1,0:T(8,128)(2,1)S(1)}, bf16[512,2048]{1,0:T(8,128)(2,1)S(1)}, u32[]{:S(2)}, u32[]{:S(2)}) collective-permute-start(bf16[512,2048]{1,0:T(8,128)(2,1)S(1)} %shard_map.85.refs_8_.refs_5_), channel_id=1, source_target_pairs={{0,6},{1,25},{2,0},{3,27},{4,2},{5,29},{6,4},{7,31},{8,14},{9,1},{... | collective-permute-start | bytes 6291464 | tf_op jit(solution)/shard_map/ppermute | solution.py:36
  45.2 44.9 %collective-permute-start.10 = (bf16[512,2048]{1,0:T(8,128)(2,1)S(1)}, bf16[512,2048]{1,0:T(8,128)(2,1)S(1)}, u32[]{:S(2)}, u32[]{:S(2)}) collective-permute-start(bf16[512,2048]{1,0:T(8,128)(2,1)S(1)} %shard_map.85.refs_8_.refs_5_), channel_id=1, source_target_pairs={{0,2},{1,9},{2,4},{3,11},{4,6},{5,13},{6,0},{7,15},{8,10},{9,17},{... | collective-permute-start | bytes 6291464 | tf_op jit(solution)/shard_map/ppermute | solution.py:36
  48.1 5.8 %collective-permute-start.12 = (f32[2,32,512]{2,1,0:T(8,128)S(1)}, f32[2,32,512]{2,1,0:T(8,128)S(1)}, u32[]{:S(2)}, u32[]{:S(2)}) collective-permute-start(f32[2,32,512]{2,1,0:T(8,128)S(1)} %get-tuple-element.63.refs_7_), channel_id=1, source_target_pairs={{0,32},{32,0},{64,96},{96,64},{1,33},{33,1},{65,97},{97,65},{2,34}... | collective-permute-start | bytes 393224 | tf_op jit(solution)/shard_map/ppermute | solution.py:44
  53.9 7.9 %collective-permute-start.13 = (f32[32,512]{1,0:T(8,128)S(1)}, f32[32,512]{1,0:T(8,128)S(1)}, u32[]{:S(2)}, u32[]{:S(2)}) collective-permute-start(f32[32,512]{1,0:T(8,128)S(1)} %get-tuple-element.66.refs_9_), channel_id=1, source_target_pairs={{0,64},{32,96},{64,0},{96,32},{1,65},{33,97},{65,1},{97,33},{2,66}... | collective-permute-start | bytes 196616 | tf_op jit(solution)/shard_map/ppermute | solution.py:44
  61.8 5.1 %collective-permute-start.14 = (f32[32,512]{1,0:T(8,128)S(1)}, f32[32,512]{1,0:T(8,128)S(1)}, u32[]{:S(2)}, u32[]{:S(2)}) collective-permute-start(f32[32,512]{1,0:T(8,128)S(1)} %shard_map.90.refs_8_.refs_0_), channel_id=1, source_target_pairs={{0,8},{1,3},{2,10},{3,1},{4,12},{5,7},{6,14},{7,5},{8,0},{9,11},{1... | collective-permute-start | bytes 196616 | tf_op jit(solution)/shard_map/ppermute | solution.py:56
  66.9 6.6 %collective-permute-start.17 = (f32[32,512]{1,0:T(8,128)S(1)}, f32[32,512]{1,0:T(8,128)S(1)}, u32[]{:S(2)}, u32[]{:S(2)}) collective-permute-start(f32[32,512]{1,0:T(8,128)S(1)} %shard_map.92.refs_8_.refs_0_), channel_id=1, source_target_pairs={{0,16},{1,5},{2,18},{3,7},{4,20},{5,1},{6,22},{7,3},{8,24},{9,13},... | collective-permute-start | bytes 196616 | tf_op jit(solution)/shard_map/ppermute | solution.py:56
  79.9 6.1 %collective-permute-start.20 = (f32[32,512]{1,0:T(8,128)S(1)}, f32[32,512]{1,0:T(8,128)S(1)}, u32[]{:S(2)}, u32[]{:S(2)}) collective-permute-start(f32[32,512]{1,0:T(8,128)S(1)} %shard_map.95.refs_0_), channel_id=1, source_target_pairs={{0,16},{1,5},{2,18},{3,7},{4,20},{5,1},{6,22},{7,3},{8,24},{9,13},... | collective-permute-start | bytes 196616 | tf_op jit(solution)/shard_map/ppermute | solution.py:56
  83.3 27.2 %collective-permute-start.25 = (bf16[512,2048]{1,0:T(8,128)(2,1)S(1)}, bf16[512,2048]{1,0:T(8,128)(2,1)S(1)}, u32[]{:S(2)}, u32[]{:S(2)}) collective-permute-start(bf16[512,2048]{1,0:T(8,128)(2,1)S(1)} %collective-permute-done.15.refs_4_), channel_id=1, source_target_pairs={{0,2},{1,9},{2,4},{3,11},{4,6},{5,13},{6,0},{7,15},{8,10},{9,17},{... | collective-permute-start | bytes 6291464 | tf_op jit(solution)/shard_map/ppermute | solution.py:36
  86.0 26.5 %collective-permute-start.26 = (bf16[512,2048]{1,0:T(8,128)(2,1)S(1)}, bf16[512,2048]{1,0:T(8,128)(2,1)S(1)}, u32[]{:S(2)}, u32[]{:S(2)}) collective-permute-start(bf16[512,2048]{1,0:T(8,128)(2,1)S(1)} %collective-permute-done.21.refs_5_), channel_id=1, source_target_pairs={{0,6},{1,25},{2,0},{3,27},{4,2},{5,29},{6,4},{7,31},{8,14},{9,1},{... | collective-permute-start | bytes 6291464 | tf_op jit(solution)/shard_map/ppermute | solution.py:36
  87.6 5.8 %collective-permute-start.22 = (f32[32,512]{1,0:T(8,128)S(1)}, f32[32,512]{1,0:T(8,128)S(1)}, u32[]{:S(2)}, u32[]{:S(2)}) collective-permute-start(f32[32,512]{1,0:T(8,128)S(1)} %shard_map.96.refs_8_), channel_id=1, source_target_pairs={{0,64},{32,96},{64,0},{96,32},{1,65},{33,97},{65,1},{97,33},{2,66}... | collective-permute-start | bytes 196616 | tf_op jit(solution)/shard_map/ppermute | solution.py:44
  93.4 5.0 %collective-permute-start.23 = (f32[2,32,512]{2,1,0:T(8,128)S(1)}, f32[2,32,512]{2,1,0:T(8,128)S(1)}, u32[]{:S(2)}, u32[]{:S(2)}) collective-permute-start(f32[2,32,512]{2,1,0:T(8,128)S(1)} %pad_maximum_fusion.refs_8_), channel_id=1, source_target_pairs={{0,32},{32,0},{64,96},{96,64},{1,33},{33,1},{65,97},{97,65},{2,34}... | collective-permute-start | bytes 393224 | tf_op jit(solution)/shard_map/ppermute | solution.py:44
  117.6 8.4 %collective-permute-start.28 = (f32[2048,512]{1,0:T(8,128)S(1)}, f32[2048,512]{1,0:T(8,128)S(1)}, u32[]{:S(2)}, u32[]{:S(2)}) collective-permute-start(f32[2048,512]{1,0:T(8,128)S(1)} %shard_map.103.refs_2_), channel_id=1, source_target_pairs={{0,1},{1,0},{2,3},{3,2},{4,5},{5,4},{6,7},{7,6},{8,9},{9,8},{10,11... | collective-permute-start | bytes 12582920 | tf_op jit(solution)/shard_map/ppermute | solution.py:40
  118.1 5.8 %collective-permute-start.29 = (f32[32,512]{1,0:T(8,128)S(1)}, f32[32,512]{1,0:T(8,128)S(1)}, u32[]{:S(2)}, u32[]{:S(2)}) collective-permute-start(f32[32,512]{1,0:T(8,128)S(1)} %shard_map.104.refs_9_), channel_id=1, source_target_pairs={{0,64},{32,96},{64,0},{96,32},{1,65},{33,97},{65,1},{97,33},{2,66}... | collective-permute-start | bytes 196616 | tf_op jit(solution)/shard_map/ppermute | solution.py:48
  120.6 5.5 %collective-permute-start.30 = (f32[32,512]{1,0:T(8,128)S(1)}, f32[32,512]{1,0:T(8,128)S(1)}, u32[]{:S(2)}, u32[]{:S(2)}) collective-permute-start(f32[32,512]{1,0:T(8,128)S(1)} %shard_map.104.refs_9_), channel_id=1, source_target_pairs={{0,32},{32,64},{64,96},{96,0},{1,33},{33,65},{65,97},{97,1},{2,34}... | collective-permute-start | bytes 196616 | tf_op jit(solution)/shard_map/ppermute | solution.py:48
  (13 other events, 44.8 us)

commit v6 on v5

--- a/solution.py
+++ b/solution.py
@@ -533,7 +533,7 @@
     l0, r0 = hop(g0, False, 1), hop(g0, False, -1)
     e_got = swap(later(e_other, g0))
     e_own = errors(pos, q, e, 0, (g0,))
-    (g1,) = pack(stack_kernel, (b, c, d), (4 * T,), (e_own,))
+    (g1,) = pack(stack_kernel, (b, c, d), (4 * T,), (e_own, e_got))
     l1, r1 = hop(g1, False, 1), hop(g1, False, -1)
 
     keep, send = sketch_part(pos, h, (e_own, e_got), (g0, g1), ())

time: 134 us -> 134 us (level)
  waiting for transfers between devices: 25.6 us -> 23.8 us
  starting transfers between devices: 43 us -> 44.7 us
    ppermute x10, starting transfers between devices: 13.2 us -> 15.4 us  [hop(): return lax.ppermute(array, 'tensor', pairs)]
    ppermute x8, waiting for transfers between devices: 6.2 us -> 4.67 us  [swap(): return lax.ppermute(array, 'tensor', [(i, i ^ 1) for i in range(2 * N * N)])]
    ppermute x7, waiting for transfers between devices: 8.35 us -> 6.97 us  [twin(): return lax.ppermute(array, 'tensor', pairs)]
  transfers between devices with their start and end apart: 32 -> 32, of which waited for: 16 -> 15; matrix products, arithmetic and copies ran while one was open for 1% -> 1% of each run, Pallas kernels for 37% -> 37%
where the time goes in v6:
time: 134 us; the launch traced here: 133 us
  Pallas kernels  57.9 us (43%)
  starting transfers between devices  44.7 us (33%)
  waiting for transfers between devices  23.8 us (18%)
  local copies, waits for them, and re-layouts  4.98 us (4%)
    pallas_call x30, Pallas kernels, run(): pl.pallas_call(wrapped, out_shape=out_shape, compiler_params=options, **kw)  57.9 us
    ppermute x10, starting transfers between devices, hop(): return lax.ppermute(array, 'tensor', pairs)  15.4 us
    ppermute x7, starting transfers between devices, twin(): return lax.ppermute(array, 'tensor', pairs)  13.9 us
    ppermute x4, starting transfers between devices, hop_z(): return lax.ppermute(array, 'dp', [(i, i ^ bit) for i in range(N)])  8.36 us
    ppermute x10, waiting for transfers between devices, hop(): return lax.ppermute(array, 'tensor', pairs)  8.01 us
    ppermute x7, waiting for transfers between devices, twin(): return lax.ppermute(array, 'tensor', pairs)  6.97 us
    ppermute x3, starting transfers between devices, around_z(): return lax.ppermute(array, 'dp', [(i, (i + d) % N) for i in range(N)])  5.14 us
    ppermute x8, waiting for transfers between devices, swap(): return lax.ppermute(array, 'tensor', [(i, i ^ 1) for i in range(2 * N * N)])  4.67 us
  transfers between devices with their start and end apart: 32, of which 15 were waited for; matrix products, arithmetic and copies ran while one was open for 1% of the time, Pallas kernels for 37%

profile of v6, /device:TPU:0, one launch (start us, length us, event | category | flops | bytes accessed | tf_op | source)
XLA Modules:
  0.0 132.6 jit_solution(2435903269941635922)
XLA Ops:
  4.8 2.8 %collective-permute-start.2 = (bf16[256,2048]{1,0:T(8,128)(2,1)S(1)}, bf16[256,2048]{1,0:T(8,128)(2,1)S(1)}, u32[]{:S(2)}, u32[]{:S(2)}) collective-permute-start(bf16[256,2048]{1,0:T(8,128)(2,1)S(1)} %shard_map.77.refs_3_.refs_0_), channel_id=1, source_target_pairs={{0,24},{1,7},{2,26},{3,1},{4,28},{5,3},{6,30},{7,5},{8,0},{9,15},{... | collective-permute-start | bytes 3145736 | tf_op jit(solution)/shard_map/ppermute | solution.py:36
  16.4 2.9 %collective-permute-start.5 = (f32[32,1024]{1,0:T(8,128)S(1)}, f32[32,1024]{1,0:T(8,128)S(1)}, u32[]{:S(2)}, u32[]{:S(2)}) collective-permute-start(f32[32,1024]{1,0:T(8,128)S(1)} %get-tuple-element.56), channel_id=1, source_target_pairs={{0,4},{1,17},{2,6},{3,19},{4,0},{5,21},{6,2},{7,23},{8,12},{9,25},... | collective-permute-start | bytes 393224 | tf_op jit(solution)/shard_map/ppermute | solution.py:56
  20.5 3.6 %shard_map.81.refs_2_ = f32[4,32,512]{2,1,0:T(8,128)S(1)} custom-call(s32[2]{0:T(128)S(1)} %pad_add_fusion.refs_0_.refs_1_, f32[32,512]{1,0:T(8,128)S(1)} %bitcast.12, f32[4096,512]{1,0:T(8,128)} %bitcast.15, f32[32,1024]{1,0:T(8,128)S(1)} %get-tuple-element.55.refs_3_.refs_1_), custom_call_target="tpu_custom_call" | custom-call | flops 1000 | bytes 1000 | tf_op jit(solution)/shard_map/pallas_call | solution.py:133
  30.0 2.9 %collective-permute-start.16 = (bf16[512,2048]{1,0:T(8,128)(2,1)S(1)}, bf16[512,2048]{1,0:T(8,128)(2,1)S(1)}, u32[]{:S(2)}, u32[]{:S(2)}) collective-permute-start(bf16[512,2048]{1,0:T(8,128)(2,1)S(1)} %shard_map.83.refs_3_.refs_7_.refs_4_), channel_id=1, source_target_pairs={{0,6},{1,25},{2,0},{3,27},{4,2},{5,29},{6,4},{7,31},{8,14},{9,1},{... | collective-permute-start | bytes 6291464 | tf_op jit(solution)/shard_map/ppermute | solution.py:36
  32.8 3.6 %shard_map.84.refs_3_.refs_5_ = f32[4,32,512]{2,1,0:T(8,128)S(1)} custom-call(s32[2]{0:T(128)S(1)} %pad_add_fusion.refs_0_.refs_1_, f32[32,512]{1,0:T(8,128)S(1)} %bitcast.13, f32[4096,512]{1,0:T(8,128)} %bitcast.16, bf16[512,2048]{1,0:T(8,128)(2,1)S(1)} %shard_map.83.refs_3_.refs_7_.refs_4_), custom_call_target="tpu_custom_call" | custom-call | flops 1000 | bytes 1000 | tf_op jit(solution)/shard_map/pallas_call | solution.py:133
  36.4 3.8 %collective-permute-done.8.refs_1_ = bf16[128,2048]{1,0:T(8,128)(2,1)S(1)} collective-permute-done((bf16[128,2048]{1,0:T(8,128)(2,1)S(1)}, bf16[128,2048]{1,0:T(8,128)(2,1)S(1)}, u32[]{:S(2)}, u32[]{:S(2)}) %collective-permute-start.8) | collective-permute-done | bytes 524320 | tf_op jit(solution)/shard_map/ppermute | solution.py:36
  42.5 2.7 %collective-permute-start.21 = (bf16[512,2048]{1,0:T(8,128)(2,1)S(1)}, bf16[512,2048]{1,0:T(8,128)(2,1)S(1)}, u32[]{:S(2)}, u32[]{:S(2)}) collective-permute-start(bf16[512,2048]{1,0:T(8,128)(2,1)S(1)} %shard_map.85.refs_8_.refs_5_), channel_id=1, source_target_pairs={{0,6},{1,25},{2,0},{3,27},{4,2},{5,29},{6,4},{7,31},{8,14},{9,1},{... | collective-permute-start | bytes 6291464 | tf_op jit(solution)/shard_map/ppermute | solution.py:36
  48.5 3.8 %shard_map.87 = (f32[2048,512]{1,0:T(8,128)S(1)}, f32[2048,512]{1,0:T(8,128)S(1)}) custom-call(s32[96]{0:T(128)S(1)} %dynamic-slice_bitcast_fusion.refs_0_.refs_1_, s32[2]{0:T(128)S(1)} %pad_add_fusion.refs_0_.refs_1_, bf16[4096,512]{1,0:T(8,128)(2,1)S(1)} %copy-done.1, bf16[4096,512]{1,0:T(8,128)(2,1)S(1)} %shard_map.79.refs_2_.refs_3_.refs_6_, ...), custom_call_target="tpu_custom_call" | custom-call | flops 1000 | bytes 1000 | tf_op jit(solution)/shard_map/pallas_call | solution.py:133
  52.3 3.8 %collective-permute-start.13 = (f32[32,512]{1,0:T(8,128)S(1)}, f32[32,512]{1,0:T(8,128)S(1)}, u32[]{:S(2)}, u32[]{:S(2)}) collective-permute-start(f32[32,512]{1,0:T(8,128)S(1)} %get-tuple-element.66.refs_9_), channel_id=1, source_target_pairs={{0,64},{32,96},{64,0},{96,32},{1,65},{33,97},{65,1},{97,33},{2,66}... | collective-permute-start | bytes 196616 | tf_op jit(solution)/shard_map/ppermute | solution.py:44
  56.2 3.9 %shard_map.89 = (f32[2048,512]{1,0:T(8,128)S(1)}, f32[2048,512]{1,0:T(8,128)S(1)}) custom-call(s32[96]{0:T(128)S(1)} %dynamic-slice_bitcast_fusion.refs_0_.refs_1_, s32[2]{0:T(128)S(1)} %pad_add_fusion.refs_0_.refs_1_, bf16[4096,512]{1,0:T(8,128)(2,1)S(1)} %copy-done.1, ...), custom_call_target="tpu_custom_call", output_to_operand_aliasing={{0}: (7, {}), {1}: (8, {})} | custom-call | flops 1000 | bytes 1000 | tf_op jit(solution)/shard_map/pallas_call | solution.py:133
  61.7 3.1 %shard_map.91 = (f32[2048,512]{1,0:T(8,128)S(1)}, f32[2048,512]{1,0:T(8,128)S(1)}) custom-call(s32[96]{0:T(128)S(1)} %dynamic-slice_bitcast_fusion.refs_0_.refs_1_, s32[2]{0:T(128)S(1)} %pad_add_fusion.refs_0_.refs_1_, bf16[4096,512]{1,0:T(8,128)(2,1)S(1)} %copy-done.1, ...), custom_call_target="tpu_custom_call", output_to_operand_aliasing={{0}: (6, {}), {1}: (7, {})} | custom-call | flops 1000 | bytes 1000 | tf_op jit(solution)/shard_map/pallas_call | solution.py:133
  65.3 3.4 %collective-permute-start.17 = (f32[32,512]{1,0:T(8,128)S(1)}, f32[32,512]{1,0:T(8,128)S(1)}, u32[]{:S(2)}, u32[]{:S(2)}) collective-permute-start(f32[32,512]{1,0:T(8,128)S(1)} %shard_map.92.refs_8_.refs_0_), channel_id=1, source_target_pairs={{0,16},{1,5},{2,18},{3,7},{4,20},{5,1},{6,22},{7,3},{8,24},{9,13},... | collective-permute-start | bytes 196616 | tf_op jit(solution)/shard_map/ppermute | solution.py:56
  68.7 3.1 %shard_map.93 = (f32[2048,512]{1,0:T(8,128)S(1)}, f32[2048,512]{1,0:T(8,128)S(1)}) custom-call(s32[96]{0:T(128)S(1)} %dynamic-slice_bitcast_fusion.refs_0_.refs_1_, s32[2]{0:T(128)S(1)} %pad_add_fusion.refs_0_.refs_1_, bf16[4096,512]{1,0:T(8,128)(2,1)S(1)} %copy-done.1, ...), custom_call_target="tpu_custom_call", output_to_operand_aliasing={{0}: (6, {}), {1}: (7, {})} | custom-call | flops 1000 | bytes 1000 | tf_op jit(solution)/shard_map/pallas_call | solution.py:133
  74.7 3.6 %collective-permute-done.19.refs_1_ = f32[32,512]{1,0:T(8,128)S(1)} collective-permute-done((f32[32,512]{1,0:T(8,128)S(1)}, f32[32,512]{1,0:T(8,128)S(1)}, u32[]{:S(2)}, u32[]{:S(2)}) %collective-permute-start.19) | collective-permute-done | bytes 65568 | tf_op jit(solution)/shard_map/ppermute | solution.py:56
  78.3 3.4 %collective-permute-start.20 = (f32[32,512]{1,0:T(8,128)S(1)}, f32[32,512]{1,0:T(8,128)S(1)}, u32[]{:S(2)}, u32[]{:S(2)}) collective-permute-start(f32[32,512]{1,0:T(8,128)S(1)} %shard_map.95.refs_0_), channel_id=1, source_target_pairs={{0,16},{1,5},{2,18},{3,7},{4,20},{5,1},{6,22},{7,3},{8,24},{9,13},... | collective-permute-start | bytes 196616 | tf_op jit(solution)/shard_map/ppermute | solution.py:56
  82.3 2.7 %collective-permute-done.20.refs_1_ = f32[32,512]{1,0:T(8,128)S(1)} collective-permute-done((f32[32,512]{1,0:T(8,128)S(1)}, f32[32,512]{1,0:T(8,128)S(1)}, u32[]{:S(2)}, u32[]{:S(2)}) %collective-permute-start.20) | collective-permute-done | bytes 65568 | tf_op jit(solution)/shard_map/ppermute | solution.py:56
  84.9 3.2 %collective-permute-start.26 = (bf16[512,2048]{1,0:T(8,128)(2,1)S(1)}, bf16[512,2048]{1,0:T(8,128)(2,1)S(1)}, u32[]{:S(2)}, u32[]{:S(2)}) collective-permute-start(bf16[512,2048]{1,0:T(8,128)(2,1)S(1)} %collective-permute-done.21.refs_5_), channel_id=1, source_target_pairs={{0,6},{1,25},{2,0},{3,27},{4,2},{5,29},{6,4},{7,31},{8,14},{9,1},{... | collective-permute-start | bytes 6291464 | tf_op jit(solution)/shard_map/ppermute | solution.py:36
  90.0 3.1 %shard_map.97 = (f32[2048,512]{1,0:T(8,128)S(1)}, f32[2048,512]{1,0:T(8,128)S(1)}) custom-call(s32[96]{0:T(128)S(1)} %dynamic-slice_bitcast_fusion.refs_0_.refs_1_, s32[2]{0:T(128)S(1)} %pad_add_fusion.refs_0_.refs_1_, bf16[4096,512]{1,0:T(8,128)(2,1)S(1)} %copy-done.1, ...), custom_call_target="tpu_custom_call", output_to_operand_aliasing={{0}: (6, {}), {1}: (7, {})} | custom-call | flops 1000 | bytes 1000 | tf_op jit(solution)/shard_map/pallas_call | solution.py:133
  94.6 3.1 %shard_map.98 = (f32[2048,512]{1,0:T(8,128)S(1)}, f32[2048,512]{1,0:T(8,128)S(1)}) custom-call(s32[96]{0:T(128)S(1)} %dynamic-slice_bitcast_fusion.refs_0_.refs_1_, s32[2]{0:T(128)S(1)} %pad_add_fusion.refs_0_.refs_1_, bf16[4096,512]{1,0:T(8,128)(2,1)S(1)} %copy-done.1, ...), custom_call_target="tpu_custom_call", output_to_operand_aliasing={{0}: (6, {}), {1}: (7, {})} | custom-call | flops 1000 | bytes 1000 | tf_op jit(solution)/shard_map/pallas_call | solution.py:133
  100.8 5.3 %shard_map.99.refs_1_.refs_2_.refs_8_ = f32[32,4096]{1,0:T(8,128)S(1)} custom-call(s32[2]{0:T(128)S(1)} %pad_add_fusion.refs_0_.refs_1_, f32[4,32,512]{2,1,0:T(8,128)S(1)} %constant_dynamic-update-slice_fusion.refs_1_, f32[4,32,512]{2,1,0:T(8,128)S(1)} %collective-permute-done.24.refs_2_, f32[2048,512]{1,0:T(8,128)S(1)} %get-tuple-element.81.refs_3_.refs_2_), custom_call_target="tpu_custom_call" | custom-call | flops 1000 | bytes 1000 | tf_op jit(solution)/shard_map/pallas_call | solution.py:133
  106.2 4.9 %shard_map.100 = (f32[32,512]{1,0:T(8,128)S(1)}, f32[32,512]{1,0:T(8,128)S(1)}, f32[2048,512]{1,0:T(8,128)S(1)}) custom-call(s32[2]{0:T(128)S(1)} %pad_add_fusion.refs_0_.refs_1_, f32[32,4096]{1,0:T(8,128)S(1)} %shard_map.99.refs_1_.refs_2_.refs_8_, f32[2048,512]{1,0:T(8,128)S(1)} %get-tuple-element.81.refs_3_.refs_2_, ...), custom_call_target="tpu_custom_call" | custom-call | flops 1000 | bytes 1000 | tf_op jit(solution)/shard_map/pallas_call | solution.py:133
  115.2 2.9 %shard_map.103.refs_2_ = f32[2048,512]{1,0:T(8,128)S(1)} custom-call(s32[96]{0:T(128)S(1)} %dynamic-slice_bitcast_fusion.refs_0_.refs_1_, f32[2048,512]{1,0:T(8,128)S(1)} %get-tuple-element.83.refs_3_.refs_1_, bf16[4096,512]{1,0:T(8,128)(2,1)S(1)} %shard_map.79.refs_2_.refs_3_.refs_6_, bf16[512,2048]{1,0:T(8,128)(2,1)S(1)} %collective-permute-done.25.refs_7_.refs_3_.refs_6_, ...), custom_call_target="tpu_custom_call" | custom-call | flops 1000 | bytes 1000 | tf_op jit(solution)/shard_map/pallas_call | solution.py:133
  121.1 2.7 %collective-permute-start.31 = (f32[32,512]{1,0:T(8,128)S(1)}, f32[32,512]{1,0:T(8,128)S(1)}, u32[]{:S(2)}, u32[]{:S(2)}) collective-permute-start(f32[32,512]{1,0:T(8,128)S(1)} %shard_map.104.refs_9_), channel_id=1, source_target_pairs={{0,96},{32,0},{64,32},{96,64},{1,97},{33,1},{65,33},{97,65},{2,98}... | collective-permute-start | bytes 196616 | tf_op jit(solution)/shard_map/ppermute | solution.py:48
  126.0 6.4 %shard_map.105 = (f32[4096,512]{1,0:T(8,128)}, f32[32,512]{1,0:T(8,128)}, f32[32,4096]{1,0:T(8,128)}) custom-call(s32[2]{0:T(128)S(1)} %pad_add_fusion.refs_0_.refs_1_, s32[96]{0:T(128)S(1)} %dynamic-slice_bitcast_fusion.refs_0_.refs_1_, f32[2048,512]{1,0:T(8,128)S(1)} %get-tuple-element.81.refs_3_.refs_2_, f32[2048,512]{1,0:T(8,128)S(1)} %get-tuple-element.84.refs_3_, ...), custom_call_target="tpu_custom_call" | custom-call | flops 1000 | bytes 1000 | tf_op jit(solution)/shard_map/pallas_call | solution.py:133
  (85 shorter events, 46.6 us)
Async XLA Ops:
  4.6 9.2 %collective-permute-start.1 = (bf16[4096,512]{1,0:T(8,128)(2,1)}, bf16[4096,512]{1,0:T(8,128)(2,1)}, u32[]{:S(2)}, u32[]{:S(2)}) collective-permute-start(bf16[4096,512]{1,0:T(8,128)(2,1)} %refs_5_.5), channel_id=1, source_target_pairs={{0,1},{1,0},{2,3},{3,2},{4,5},{5,4},{6,7},{7,6},{8,9},{9,8},{10,11... | collective-permute-start | bytes 12582920 | tf_op jit(solution)/shard_map/ppermute | solution.py:40
  4.8 19.3 %collective-permute-start.2 = (bf16[256,2048]{1,0:T(8,128)(2,1)S(1)}, bf16[256,2048]{1,0:T(8,128)(2,1)S(1)}, u32[]{:S(2)}, u32[]{:S(2)}) collective-permute-start(bf16[256,2048]{1,0:T(8,128)(2,1)S(1)} %shard_map.77.refs_3_.refs_0_), channel_id=1, source_target_pairs={{0,24},{1,7},{2,26},{3,1},{4,28},{5,3},{6,30},{7,5},{8,0},{9,15},{... | collective-permute-start | bytes 3145736 | tf_op jit(solution)/shard_map/ppermute | solution.py:36
  7.7 18.5 %collective-permute-start.3 = (bf16[256,2048]{1,0:T(8,128)(2,1)S(1)}, bf16[256,2048]{1,0:T(8,128)(2,1)S(1)}, u32[]{:S(2)}, u32[]{:S(2)}) collective-permute-start(bf16[256,2048]{1,0:T(8,128)(2,1)S(1)} %shard_map.77.refs_3_.refs_0_), channel_id=1, source_target_pairs={{0,8},{1,3},{2,10},{3,5},{4,12},{5,7},{6,14},{7,1},{8,16},{9,11},{... | collective-permute-start | bytes 3145736 | tf_op jit(solution)/shard_map/ppermute | solution.py:36
  16.4 9.8 %collective-permute-start.5 = (f32[32,1024]{1,0:T(8,128)S(1)}, f32[32,1024]{1,0:T(8,128)S(1)}, u32[]{:S(2)}, u32[]{:S(2)}) collective-permute-start(f32[32,1024]{1,0:T(8,128)S(1)} %get-tuple-element.56), channel_id=1, source_target_pairs={{0,4},{1,17},{2,6},{3,19},{4,0},{5,21},{6,2},{7,23},{8,12},{9,25},... | collective-permute-start | bytes 393224 | tf_op jit(solution)/shard_map/ppermute | solution.py:56
  19.3 6.9 %collective-permute-start.6 = (f32[32,1024]{1,0:T(8,128)S(1)}, f32[32,1024]{1,0:T(8,128)S(1)}, u32[]{:S(2)}, u32[]{:S(2)}) collective-permute-start(f32[32,1024]{1,0:T(8,128)S(1)} %get-tuple-element.57), channel_id=1, source_target_pairs={{0,2},{1,9},{2,0},{3,11},{4,6},{5,13},{6,4},{7,15},{8,10},{9,1},{1... | collective-permute-start | bytes 393224 | tf_op jit(solution)/shard_map/ppermute | solution.py:56
  20.3 6.2 %collective-permute-start.7 = (f32[32,1024]{1,0:T(8,128)S(1)}, f32[32,1024]{1,0:T(8,128)S(1)}, u32[]{:S(2)}, u32[]{:S(2)}) collective-permute-start(f32[32,1024]{1,0:T(8,128)S(1)} %get-tuple-element.58), channel_id=1, source_target_pairs={{0,6},{1,25},{2,4},{3,27},{4,2},{5,29},{6,0},{7,31},{8,14},{9,17},... | collective-permute-start | bytes 393224 | tf_op jit(solution)/shard_map/ppermute | solution.py:56
  26.5 13.7 %collective-permute-start.8 = (bf16[128,2048]{1,0:T(8,128)(2,1)S(1)}, bf16[128,2048]{1,0:T(8,128)(2,1)S(1)}, u32[]{:S(2)}, u32[]{:S(2)}) collective-permute-start(bf16[128,2048]{1,0:T(8,128)(2,1)S(1)} %get-tuple-element.59.refs_2_), channel_id=1, source_target_pairs={{0,8},{1,3},{2,10},{3,5},{4,12},{5,7},{6,14},{7,1},{8,16},{9,11},{... | collective-permute-start | bytes 1572872 | tf_op jit(solution)/shard_map/ppermute | solution.py:36
  28.1 14.3 %collective-permute-start.9 = (bf16[128,2048]{1,0:T(8,128)(2,1)S(1)}, bf16[128,2048]{1,0:T(8,128)(2,1)S(1)}, u32[]{:S(2)}, u32[]{:S(2)}) collective-permute-start(bf16[128,2048]{1,0:T(8,128)(2,1)S(1)} %get-tuple-element.60), channel_id=1, source_target_pairs={{0,24},{1,7},{2,26},{3,1},{4,28},{5,3},{6,30},{7,5},{8,0},{9,15},{... | collective-permute-start | bytes 1572872 | tf_op jit(solution)/shard_map/ppermute | solution.py:36
  30.0 31.8 %collective-permute-start.16 = (bf16[512,2048]{1,0:T(8,128)(2,1)S(1)}, bf16[512,2048]{1,0:T(8,128)(2,1)S(1)}, u32[]{:S(2)}, u32[]{:S(2)}) collective-permute-start(bf16[512,2048]{1,0:T(8,128)(2,1)S(1)} %shard_map.83.refs_3_.refs_7_.refs_4_), channel_id=1, source_target_pairs={{0,6},{1,25},{2,0},{3,27},{4,2},{5,29},{6,4},{7,31},{8,14},{9,1},{... | collective-permute-start | bytes 6291464 | tf_op jit(solution)/shard_map/ppermute | solution.py:36
  32.8 28.9 %collective-permute-start.15 = (bf16[512,2048]{1,0:T(8,128)(2,1)S(1)}, bf16[512,2048]{1,0:T(8,128)(2,1)S(1)}, u32[]{:S(2)}, u32[]{:S(2)}) collective-permute-start(bf16[512,2048]{1,0:T(8,128)(2,1)S(1)} %shard_map.83.refs_3_.refs_7_.refs_4_), channel_id=1, source_target_pairs={{0,2},{1,9},{2,4},{3,11},{4,6},{5,13},{6,0},{7,15},{8,10},{9,17},{... | collective-permute-start | bytes 6291464 | tf_op jit(solution)/shard_map/ppermute | solution.py:36
  42.5 42.4 %collective-permute-start.21 = (bf16[512,2048]{1,0:T(8,128)(2,1)S(1)}, bf16[512,2048]{1,0:T(8,128)(2,1)S(1)}, u32[]{:S(2)}, u32[]{:S(2)}) collective-permute-start(bf16[512,2048]{1,0:T(8,128)(2,1)S(1)} %shard_map.85.refs_8_.refs_5_), channel_id=1, source_target_pairs={{0,6},{1,25},{2,0},{3,27},{4,2},{5,29},{6,4},{7,31},{8,14},{9,1},{... | collective-permute-start | bytes 6291464 | tf_op jit(solution)/shard_map/ppermute | solution.py:36
  45.2 44.9 %collective-permute-start.11 = (bf16[512,2048]{1,0:T(8,128)(2,1)S(1)}, bf16[512,2048]{1,0:T(8,128)(2,1)S(1)}, u32[]{:S(2)}, u32[]{:S(2)}) collective-permute-start(bf16[512,2048]{1,0:T(8,128)(2,1)S(1)} %shard_map.85.refs_8_.refs_5_), channel_id=1, source_target_pairs={{0,2},{1,9},{2,4},{3,11},{4,6},{5,13},{6,0},{7,15},{8,10},{9,17},{... | collective-permute-start | bytes 6291464 | tf_op jit(solution)/shard_map/ppermute | solution.py:36
  46.5 5.8 %collective-permute-start.12 = (f32[2,32,512]{2,1,0:T(8,128)S(1)}, f32[2,32,512]{2,1,0:T(8,128)S(1)}, u32[]{:S(2)}, u32[]{:S(2)}) collective-permute-start(f32[2,32,512]{2,1,0:T(8,128)S(1)} %get-tuple-element.63.refs_7_), channel_id=1, source_target_pairs={{0,32},{32,0},{64,96},{96,64},{1,33},{33,1},{65,97},{97,65},{2,34}... | collective-permute-start | bytes 393224 | tf_op jit(solution)/shard_map/ppermute | solution.py:44
  52.3 7.8 %collective-permute-start.13 = (f32[32,512]{1,0:T(8,128)S(1)}, f32[32,512]{1,0:T(8,128)S(1)}, u32[]{:S(2)}, u32[]{:S(2)}) collective-permute-start(f32[32,512]{1,0:T(8,128)S(1)} %get-tuple-element.66.refs_9_), channel_id=1, source_target_pairs={{0,64},{32,96},{64,0},{96,32},{1,65},{33,97},{65,1},{97,33},{2,66}... | collective-permute-start | bytes 196616 | tf_op jit(solution)/shard_map/ppermute | solution.py:44
  60.2 5.1 %collective-permute-start.14 = (f32[32,512]{1,0:T(8,128)S(1)}, f32[32,512]{1,0:T(8,128)S(1)}, u32[]{:S(2)}, u32[]{:S(2)}) collective-permute-start(f32[32,512]{1,0:T(8,128)S(1)} %shard_map.90.refs_8_.refs_0_), channel_id=1, source_target_pairs={{0,8},{1,3},{2,10},{3,1},{4,12},{5,7},{6,14},{7,5},{8,0},{9,11},{1... | collective-permute-start | bytes 196616 | tf_op jit(solution)/shard_map/ppermute | solution.py:56
  65.3 6.6 %collective-permute-start.17 = (f32[32,512]{1,0:T(8,128)S(1)}, f32[32,512]{1,0:T(8,128)S(1)}, u32[]{:S(2)}, u32[]{:S(2)}) collective-permute-start(f32[32,512]{1,0:T(8,128)S(1)} %shard_map.92.refs_8_.refs_0_), channel_id=1, source_target_pairs={{0,16},{1,5},{2,18},{3,7},{4,20},{5,1},{6,22},{7,3},{8,24},{9,13},... | collective-permute-start | bytes 196616 | tf_op jit(solution)/shard_map/ppermute | solution.py:56
  78.3 6.6 %collective-permute-start.20 = (f32[32,512]{1,0:T(8,128)S(1)}, f32[32,512]{1,0:T(8,128)S(1)}, u32[]{:S(2)}, u32[]{:S(2)}) collective-permute-start(f32[32,512]{1,0:T(8,128)S(1)} %shard_map.95.refs_0_), channel_id=1, source_target_pairs={{0,16},{1,5},{2,18},{3,7},{4,20},{5,1},{6,22},{7,3},{8,24},{9,13},... | collective-permute-start | bytes 196616 | tf_op jit(solution)/shard_map/ppermute | solution.py:56
  81.7 29.4 %collective-permute-start.25 = (bf16[512,2048]{1,0:T(8,128)(2,1)S(1)}, bf16[512,2048]{1,0:T(8,128)(2,1)S(1)}, u32[]{:S(2)}, u32[]{:S(2)}) collective-permute-start(bf16[512,2048]{1,0:T(8,128)(2,1)S(1)} %collective-permute-done.15.refs_4_), channel_id=1, source_target_pairs={{0,2},{1,9},{2,4},{3,11},{4,6},{5,13},{6,0},{7,15},{8,10},{9,17},{... | collective-permute-start | bytes 6291464 | tf_op jit(solution)/shard_map/ppermute | solution.py:36
  84.9 28.1 %collective-permute-start.26 = (bf16[512,2048]{1,0:T(8,128)(2,1)S(1)}, bf16[512,2048]{1,0:T(8,128)(2,1)S(1)}, u32[]{:S(2)}, u32[]{:S(2)}) collective-permute-start(bf16[512,2048]{1,0:T(8,128)(2,1)S(1)} %collective-permute-done.21.refs_5_), channel_id=1, source_target_pairs={{0,6},{1,25},{2,0},{3,27},{4,2},{5,29},{6,4},{7,31},{8,14},{9,1},{... | collective-permute-start | bytes 6291464 | tf_op jit(solution)/shard_map/ppermute | solution.py:36
  88.1 5.8 %collective-permute-start.22 = (f32[32,512]{1,0:T(8,128)S(1)}, f32[32,512]{1,0:T(8,128)S(1)}, u32[]{:S(2)}, u32[]{:S(2)}) collective-permute-start(f32[32,512]{1,0:T(8,128)S(1)} %shard_map.96.refs_8_), channel_id=1, source_target_pairs={{0,64},{32,96},{64,0},{96,32},{1,65},{33,97},{65,1},{97,33},{2,66}... | collective-permute-start | bytes 196616 | tf_op jit(solution)/shard_map/ppermute | solution.py:44
  93.9 5.0 %collective-permute-start.23 = (f32[2,32,512]{2,1,0:T(8,128)S(1)}, f32[2,32,512]{2,1,0:T(8,128)S(1)}, u32[]{:S(2)}, u32[]{:S(2)}) collective-permute-start(f32[2,32,512]{2,1,0:T(8,128)S(1)} %pad_maximum_fusion.refs_8_), channel_id=1, source_target_pairs={{0,32},{32,0},{64,96},{96,64},{1,33},{33,1},{65,97},{97,65},{2,34}... | collective-permute-start | bytes 393224 | tf_op jit(solution)/shard_map/ppermute | solution.py:44
  118.2 7.8 %collective-permute-start.28 = (f32[2048,512]{1,0:T(8,128)S(1)}, f32[2048,512]{1,0:T(8,128)S(1)}, u32[]{:S(2)}, u32[]{:S(2)}) collective-permute-start(f32[2048,512]{1,0:T(8,128)S(1)} %shard_map.103.refs_2_), channel_id=1, source_target_pairs={{0,1},{1,0},{2,3},{3,2},{4,5},{5,4},{6,7},{7,6},{8,9},{9,8},{10,11... | collective-permute-start | bytes 12582920 | tf_op jit(solution)/shard_map/ppermute | solution.py:40
  118.6 6.4 %collective-permute-start.29 = (f32[32,512]{1,0:T(8,128)S(1)}, f32[32,512]{1,0:T(8,128)S(1)}, u32[]{:S(2)}, u32[]{:S(2)}) collective-permute-start(f32[32,512]{1,0:T(8,128)S(1)} %shard_map.104.refs_9_), channel_id=1, source_target_pairs={{0,64},{32,96},{64,0},{96,32},{1,65},{33,97},{65,1},{97,33},{2,66}... | collective-permute-start | bytes 196616 | tf_op jit(solution)/shard_map/ppermute | solution.py:48
  120.5 5.5 %collective-permute-start.30 = (f32[32,512]{1,0:T(8,128)S(1)}, f32[32,512]{1,0:T(8,128)S(1)}, u32[]{:S(2)}, u32[]{:S(2)}) collective-permute-start(f32[32,512]{1,0:T(8,128)S(1)} %shard_map.104.refs_9_), channel_id=1, source_target_pairs={{0,32},{32,64},{64,96},{96,0},{1,33},{33,65},{65,97},{97,1},{2,34}... | collective-permute-start | bytes 196616 | tf_op jit(solution)/shard_map/ppermute | solution.py:48
  (13 other events, 45.4 us)
